TPU v7x, 512 devices: a whole 4x8x8 slice. The times are simulated.
512 devices in a mesh: blk: 128 (over y_lo, z, x), rep: 4 (over y_hi, core).
Axes of the slice: x: 4, y: 8 (y_hi: 2, y_lo: 4; y = y_hi * 4 + y_lo), z: 8, core: 2. Of those that a mesh axis runs over, the one named last changes fastest.
Arguments:
- frames: float32 [16384, 3, 1024], P(('blk', 'rep')), may hold values from -25 to 25
Outputs:
- deviation: float32 [16384, 384], P(('blk', 'rep'))
All inputs are finite; a program needn't handle non-finite values.
Results may differ from a plain program's by a relative error of at most 0.0003.
Values sent between devices are 32-bit elements; how exact they have to be, the bound alone decides.
No kernel may reach another device: no remote copies, remote signals or barrier semaphores. Data moves between devices by JAX's collectives and lax.ppermute only.
A program may use at most 64 MiB of HBM per device.

v0:
```python
import jax
import jax.numpy as jnp
from jax import lax
from jax.sharding import PartitionSpec as P

REACH = 1
ITERS = 8


def passed_along(value, axis, steps):
    count = lax.axis_size(axis)
    pairs = [(source, (source + steps) % count) for source in range(count)]
    return lax.ppermute(value, axis, pairs)


def centre(frames):
    return frames - jnp.mean(frames, axis=2, keepdims=True)


def square_norms(centred):
    return jnp.sum(centred * centred, axis=(1, 2))


def polar_trace(covariance, scaling):
    iterate = covariance * scaling
    for sweep in range(ITERS):
        gram_matrix = (
            iterate[0][:, None] * iterate[0][None, :]
            + iterate[1][:, None] * iterate[1][None, :]
            + iterate[2][:, None] * iterate[2][None, :]
        )
        product = (
            iterate[:, 0][:, None] * gram_matrix[0][None, :]
            + iterate[:, 1][:, None] * gram_matrix[1][None, :]
            + iterate[:, 2][:, None] * gram_matrix[2][None, :]
        )
        iterate = 0.5 * (3.0 * iterate - product)
    return jnp.sum(iterate * covariance, axis=(0, 1))


def pair_deviation(resident, resident_norm, visitor):
    atom_count = resident.shape[2]
    row_count = resident.shape[0]
    partner_count = visitor.shape[0]
    visitor_norm = square_norms(visitor)
    products = lax.dot_general(
        resident.reshape(row_count * 3, atom_count),
        visitor.reshape(partner_count * 3, atom_count),
        (((1,), (1,)), ((), ())),
        precision=lax.Precision.HIGHEST,
        preferred_element_type=jnp.float32,
    )
    covariance = products.reshape(row_count, 3, partner_count, 3).transpose(1, 3, 0, 2)
    inverse_root = 1.0 / jnp.sqrt(resident_norm + 1e-06)
    partner_root = 1.0 / jnp.sqrt(visitor_norm + 1e-06)
    scaling = inverse_root[:, None] * partner_root[None, :]
    aligned = polar_trace(covariance, scaling)
    return (resident_norm[:, None] + visitor_norm[None, :] - 2.0 * aligned) / atom_count


def on_device(frames):
    resident = centre(frames)
    own_norm = square_norms(resident)
    reach = REACH
    computed = list(range(-reach, reach + 1))
    gathered = lax.all_gather(resident, "rep", axis=0, tiled=True)
    groups = {}
    for offset in computed:
        if offset == 0:
            visitor = gathered
        else:
            visitor = passed_along(gathered, "blk", -offset)
        groups[offset] = pair_deviation(resident, own_norm, visitor)
    return jnp.concatenate([groups[offset] for offset in range(-reach, reach + 1)], axis=1)


def solution(mesh):
    placed = (P(("blk", "rep"), None, None),)
    return jax.shard_map(
        on_device, mesh=mesh, in_specs=placed, out_specs=P(("blk", "rep"), None), check_vma=False
    )
```

profile of v0, /device:TPU:1, one launch (start us, length us, event | category | flops | bytes accessed | tf_op | source)
XLA Modules:
  0.0 121.4 jit_solution(2163408485099330215)
XLA Ops:
  6.5 0.0 all-gather.2.cloned.1.call-start
  6.5 1.1 reduce_sum.72
  7.6 2.0 %multiply_reduce_fusion.3 = (f32[32]{0:T(128)S(1)}, f32[32,3,1024]{2,0,1:T(8,128)}) fusion(f32[32,3,1024]{2,0,1:T(8,128)} %param.1, f32[32,3]{0,1:T(4,128)S(1)} %broadcast_multiply_fusion.15), kind=kLoop, calls=%fused_computation.15 | loop fusion | flops 294880 | bytes 786944 | tf_op jit(solution)/shard_map/reduce_sum | solution.py:21
  9.6 0.0 all-gather.2.cloned.1.call-update
  9.6 46.1 %all-gather.2.cloned.1.call-done = f32[128,3,1024]{2,0,1:T(8,128)} async-done(((f32[32,3,1024]{2,0,1:T(8,128)}), f32[128,3,1024]{2,0,1:T(8,128)}) %all-gather.2.cloned.1.call-update) | async-done | bytes 1572880 | tf_op jit(solution)/shard_map/all_gather | solution.py:66
  55.7 5.5 %collective-permute-start.1 = (f32[128,3,1024]{2,0,1:T(8,128)}, f32[128,3,1024]{2,0,1:T(8,128)S(1)}, u32[]{:S(2)}, u32[]{:S(2)}) collective-permute-start(f32[128,3,1024]{2,0,1:T(8,128)} %all-gather.2.cloned.1.call-done), channel_id=1, source_target_pairs={{0,508},{4,0},{8,4},{12,8},{16,12},{20,16},{24,20},{28,24},{32,28}... | collective-permute-start | bytes 4718600 | tf_op jit(solution)/shard_map/ppermute | solution.py:13
  61.2 1.9 %collective-permute-start = (f32[128,3,1024]{2,0,1:T(8,128)}, f32[128,3,1024]{2,0,1:T(8,128)S(1)}, u32[]{:S(2)}, u32[]{:S(2)}) collective-permute-start(f32[128,3,1024]{2,0,1:T(8,128)} %all-gather.2.cloned.1.call-done), channel_id=1, source_target_pairs={{0,4},{4,8},{8,12},{12,16},{16,20},{20,24},{24,28},{28,32},{32,36}... | collective-permute-start | bytes 4718600 | tf_op jit(solution)/shard_map/ppermute | solution.py:13
  63.2 1.6 %multiply_reduce_fusion.1 = f32[128]{0:T(128)S(1)} fusion(f32[128,3,1024]{2,0,1:T(8,128)} %all-gather.2.cloned.1.call-done), kind=kLoop, calls=%fused_computation.7 | loop fusion | flops 786304 | bytes 1573376 | tf_op jit(solution)/shard_map/reduce_sum | solution.py:21
  64.8 0.0 copy-start
  64.8 0.0 copy-start.1
  64.8 30.2 %collective-permute-done.1 = f32[128,3,1024]{2,0,1:T(8,128)S(1)} collective-permute-done((f32[128,3,1024]{2,0,1:T(8,128)}, f32[128,3,1024]{2,0,1:T(8,128)S(1)}, u32[]{:S(2)}, u32[]{:S(2)}) %collective-permute-start.1) | collective-permute-done | bytes 1572896 | tf_op jit(solution)/shard_map/ppermute | solution.py:13
  95.0 0.2 multiply_reduce_fusion
  95.2 9.5 %collective-permute-done = f32[128,3,1024]{2,0,1:T(8,128)S(1)} collective-permute-done((f32[128,3,1024]{2,0,1:T(8,128)}, f32[128,3,1024]{2,0,1:T(8,128)S(1)}, u32[]{:S(2)}, u32[]{:S(2)}) %collective-permute-start) | collective-permute-done | bytes 1572896 | tf_op jit(solution)/shard_map/ppermute | solution.py:13
  104.8 0.2 multiply_reduce_fusion.2
  105.0 0.1 broadcast_multiply_fusion.14
  105.0 0.0 copy-done
  105.0 0.0 copy-done.1
  105.0 1.5 %broadcast_multiply_fusion.1 = (f32[3,3,32,128]{3,2,1,0:T(8,128)S(1)}, f32[3,3,32,128]{3,2,1,0:T(8,128)S(1)}) fusion(f32[32,128]{1,0:T(8,128)S(1)} %get-tuple-element.245, f32[128,3,1024]{2,0,1:T(8,128)S(1)} %copy-done.1, f32[32,3,1024]{2,0,1:T(8,128)S(1)} %copy-done), kind=kOutput, calls=%fused_computation.78 | convolution fusion | flops 453021696 | bytes 2277376 | tf_op jit(solution)/shard_map/dot_general | solution.py:46
  106.7 0.1 fusion.22
  106.8 0.1 broadcast_multiply_fusion.7
  107.0 0.1 fusion.23
  107.2 0.1 broadcast_multiply_fusion.6
  107.4 0.1 fusion.24
  107.5 0.1 broadcast_multiply_fusion.5
  107.7 0.1 fusion.25
  107.8 1.5 %broadcast_multiply_fusion.11 = (f32[3,3,32,128]{3,2,1,0:T(8,128)S(1)}, f32[3,3,32,128]{3,2,1,0:T(8,128)S(1)}) fusion(f32[32,128]{1,0:T(8,128)S(1)} %get-tuple-element.244, f32[128,3,1024]{2,0,1:T(8,128)S(1)} %collective-permute-done, f32[32,3,1024]{2,0,1:T(8,128)S(1)} %copy-done), kind=kOutput, calls=%fused_computation.88 | convolution fusion | flops 453021696 | bytes 2277376 | tf_op jit(solution)/shard_map/dot_general | solution.py:46
  109.4 0.1 fusion.18
  109.6 0.1 broadcast_multiply_fusion.10
  109.8 0.1 fusion.19
  109.9 0.1 broadcast_multiply_fusion.9
  110.1 0.1 fusion.20
  110.3 0.1 broadcast_multiply_fusion.8
  110.5 0.1 fusion.21
  110.6 1.5 %broadcast_multiply_fusion = (f32[3,3,32,128]{3,2,1,0:T(8,128)S(1)}, f32[3,3,32,128]{3,2,1,0:T(8,128)S(1)}) fusion(f32[32,128]{1,0:T(8,128)S(1)} %get-tuple-element.246, f32[128,3,1024]{2,0,1:T(8,128)S(1)} %collective-permute-done.1, f32[32,3,1024]{2,0,1:T(8,128)S(1)} %copy-done), kind=kOutput, calls=%fused_computation.77 | convolution fusion | flops 453021696 | bytes 2277376 | tf_op jit(solution)/shard_map/dot_general | solution.py:46
  112.2 0.1 fusion.26
  112.4 0.1 broadcast_multiply_fusion.4
  112.6 0.1 fusion.27
  112.7 0.1 broadcast_multiply_fusion.3
  112.9 0.1 fusion.28
  113.0 0.1 broadcast_multiply_fusion.2
  113.2 0.1 fusion.29
  113.5 0.1 multiply_reduce_fusion.5
  113.6 0.1 multiply_reduce_fusion.6
  113.7 0.1 multiply_reduce_fusion.4
  113.8 0.1 subtract_multiply_fusion.2
  113.9 0.6 pad_maximum_fusion
  (101 shorter events, 1.5 us)
Async XLA Ops:
  6.5 49.2 %all-gather.2.cloned.1.call-start = ((), (), s32[]{:S(2)}) async-start(), calls=%async_computation | async-start | bytes 1966080 | tf_op jit(solution)/shard_map/all_gather | solution.py:66
  55.7 39.3 %collective-permute-start.1 = (f32[128,3,1024]{2,0,1:T(8,128)}, f32[128,3,1024]{2,0,1:T(8,128)S(1)}, u32[]{:S(2)}, u32[]{:S(2)}) collective-permute-start(f32[128,3,1024]{2,0,1:T(8,128)} %all-gather.2.cloned.1.call-done), channel_id=1, source_target_pairs={{0,508},{4,0},{8,4},{12,8},{16,12},{20,16},{24,20},{28,24},{32,28}... | collective-permute-start | bytes 4718600 | tf_op jit(solution)/shard_map/ppermute | solution.py:13
  61.2 43.5 %collective-permute-start = (f32[128,3,1024]{2,0,1:T(8,128)}, f32[128,3,1024]{2,0,1:T(8,128)S(1)}, u32[]{:S(2)}, u32[]{:S(2)}) collective-permute-start(f32[128,3,1024]{2,0,1:T(8,128)} %all-gather.2.cloned.1.call-done), channel_id=1, source_target_pairs={{0,4},{4,8},{8,12},{12,16},{16,20},{20,24},{24,28},{28,32},{32,36}... | collective-permute-start | bytes 4718600 | tf_op jit(solution)/shard_map/ppermute | solution.py:13
  64.8 40.2 %copy-start = (f32[32,3,1024]{2,0,1:T(8,128)S(1)}, f32[32,3,1024]{2,0,1:T(8,128)}, u32[]{:S(2)}) copy-start(f32[32,3,1024]{2,0,1:T(8,128)} %get-tuple-element.24) | copy-start | bytes 1179652
  64.8 40.2 %copy-start.1 = (f32[128,3,1024]{2,0,1:T(8,128)S(1)}, f32[128,3,1024]{2,0,1:T(8,128)}, u32[]{:S(2)}) copy-start(f32[128,3,1024]{2,0,1:T(8,128)} %all-gather.2.cloned.1.call-done) | copy-start | bytes 4718596
Sparse Core Ops, SparseCore 0:
  9.8 45.9 all-gather.1
where the time goes:
time: 122 us; the launch traced here: 121 us
  waiting for transfers between devices  85.8 us (70%)
  between operations  14.4 us (12%)
  other arithmetic  8.24 us (7%)
  starting transfers between devices  7.43 us (6%)
  matrix products  4.63 us (4%)
    all_gather x1, waiting for transfers between devices, on_device(): gathered = lax.all_gather(resident, 'rep', axis=0, tiled=True)  46.1 us
    ppermute x2, waiting for transfers between devices, passed_along(): return lax.ppermute(value, axis, pairs)  39.7 us
    ppermute x2, starting transfers between devices, passed_along(): return lax.ppermute(value, axis, pairs)  7.43 us
    dot_general x3, matrix products, pair_deviation(): lax.dot_general(resident.reshape(row_count * 3, atom_count), visitor.resh...  4.63 us
    reduce_sum x4, other arithmetic, square_norms(): return jnp.sum(centred * centred, axis=(1, 2))  3.98 us
  transfers between devices with their start and end apart: 3, of which 3 were waited for; matrix products, arithmetic and copies ran while one was open for 2% of the time, Pallas kernels for 0%

commit v1 on v0

v1 whole, which is shorter than its diff:
```python
import functools

import jax
import jax.numpy as jnp
from jax import lax
from jax.experimental import pallas as pl
from jax.experimental.pallas import tpu as pltpu
from jax.sharding import PartitionSpec as P

ITERS = 8
ATOMS = 1024
AXES = ("blk", "rep")
CHIPS = 256


def device_of(chip, core):
    half, block = divmod(chip % CHIPS, CHIPS // 2)
    return block * 4 + half * 2 + core


def moved(value, chips, cores):
    pairs = [
        (device_of(chip, core), device_of(chip + chips, (core + cores) % 2))
        for chip in range(CHIPS)
        for core in range(2)
    ]
    return lax.ppermute(value, AXES, pairs)


def centred_of(raw):
    return raw - jnp.sum(raw, axis=1, keepdims=True) * (1.0 / ATOMS)


def split(value):
    high = value.astype(jnp.bfloat16)
    low = (value - high.astype(jnp.float32)).astype(jnp.bfloat16)
    return high, low


def prepare_kernel(core_ref, z0, z1, a0, a1, b0, b1, high_ref, low_ref, norm_ref, column_ref):
    core = core_ref[0]
    column_ref[...] = jnp.zeros_like(column_ref)
    for place, pair in enumerate(((z0, z1), (a0, a1), (b0, b1))):
        for other, ref in enumerate(pair):
            at = core if other == 0 else 1 - core
            start = pl.multiple_of(64 * place + 32 * at, 32)
            norm = jnp.zeros((32, 1), jnp.float32)
            for b in range(3):
                centred = centred_of(ref[32 * b : 32 * b + 32, :])
                norm = norm + jnp.sum(centred * centred, axis=1, keepdims=True)
                high, low = split(centred)
                high_ref[b, pl.ds(start, 32), :] = high
                low_ref[b, pl.ds(start, 32), :] = low
            column_ref[pl.ds(start, 32), :] = jnp.broadcast_to(norm, (32, 128))
    for b in range(3):
        high_ref[b, 192:256, :] = jnp.zeros((64, ATOMS), jnp.bfloat16)
        low_ref[b, 192:256, :] = jnp.zeros((64, ATOMS), jnp.bfloat16)
    norm_ref[...] = jnp.transpose(column_ref[...])[0:8, :]


def polar_trace(cov, scale):
    x = [[cov[a][b] * scale for b in range(3)] for a in range(3)]
    for _ in range(ITERS):
        m = {}
        for p in range(3):
            for q in range(p, 3):
                g = x[0][p] * x[0][q] + x[1][p] * x[1][q] + x[2][p] * x[2][q]
                m[p, q] = m[q, p] = 1.5 - 0.5 * g if p == q else -0.5 * g
        x = [[x[a][0] * m[0, b] + x[a][1] * m[1, b] + x[a][2] * m[2, b] for b in range(3)] for a in range(3)]
    return sum(x[a][b] * cov[a][b] for a in range(3) for b in range(3))


def rows_kernel(rows_ref, high_ref, low_ref, norm_ref, out_ref, left_ref, cov_ref):
    norm = jnp.zeros((32, 1), jnp.float32)
    for a in range(3):
        centred = centred_of(rows_ref[32 * a : 32 * a + 32, :])
        norm = norm + jnp.sum(centred * centred, axis=1, keepdims=True)
        high, low = split(centred)
        left_ref[32 * a : 32 * a + 32, :] = high
        left_ref[96 + 32 * a : 128 + 32 * a, :] = low
    dims = (((1,), (1,)), ((), ()))
    for b in range(3):
        one = lax.dot_general(left_ref[...], high_ref[b], dims, preferred_element_type=jnp.float32)
        two = lax.dot_general(left_ref[...], low_ref[b], dims, preferred_element_type=jnp.float32)
        cov_ref[b] = one[:96] + (one[96:] + two[:96] + two[96:])
    row_root = 1.0 / jnp.sqrt(norm + 1e-6)
    tiles = []
    for t in range(2):
        lanes = slice(128 * t, 128 * t + 128)
        columns = norm_ref[0:1, lanes]
        scale = row_root * (1.0 / jnp.sqrt(columns + 1e-6))
        cov = [[cov_ref[b, 32 * a : 32 * a + 32, lanes] for b in range(3)] for a in range(3)]
        aligned = polar_trace(cov, scale)
        tiles.append((norm + columns - 2.0 * aligned) * (1.0 / ATOMS))
    prev, own, nxt = tiles[0][:, :64], tiles[0][:, 64:], tiles[1][:, :64]
    out_ref[...] = jnp.concatenate([prev, prev, own, own, nxt, nxt], axis=1)


def prepare(core, *frames):
    spec = pl.BlockSpec(memory_space=pltpu.VMEM)
    return pl.pallas_call(
        prepare_kernel,
        out_shape=(
            jax.ShapeDtypeStruct((3, 256, ATOMS), jnp.bfloat16),
            jax.ShapeDtypeStruct((3, 256, ATOMS), jnp.bfloat16),
            jax.ShapeDtypeStruct((8, 256), jnp.float32),
        ),
        in_specs=[pl.BlockSpec(memory_space=pltpu.SMEM)] + [spec] * 6,
        out_specs=(spec, spec, spec),
        scratch_shapes=[pltpu.VMEM((256, 128), jnp.float32)],
        compiler_params=pltpu.CompilerParams(vmem_limit_bytes=32 << 20),
        name="prepare",
    )(core, *frames)


def deviations(rows, high, low, norm, name):
    spec = pl.BlockSpec(memory_space=pltpu.VMEM)
    return pl.pallas_call(
        rows_kernel,
        out_shape=jax.ShapeDtypeStruct((32, 384), jnp.float32),
        in_specs=[spec] * 4,
        out_specs=spec,
        scratch_shapes=[pltpu.VMEM((192, ATOMS), jnp.bfloat16), pltpu.VMEM((3, 96, 256), jnp.float32)],
        compiler_params=pltpu.CompilerParams(vmem_limit_bytes=32 << 20),
        name=name,
    )(rows, high, low, norm)


def on_device(frames):
    rep = lax.axis_index("rep")
    half, core = rep // 2, rep % 2
    chip = half * (CHIPS // 2) + lax.axis_index("blk")
    raw = frames.transpose(1, 0, 2).reshape(96, ATOMS)
    far = moved(raw, CHIPS // 2, 0)
    nxt = moved(raw, -1, 0)
    prv = moved(raw, 1, 0)
    raw_other = moved(raw, 0, 1)
    nxt_other = moved(nxt, 0, 1)
    prv_other = moved(prv, 0, 1)
    high, low, norm = prepare(
        core.reshape(1).astype(jnp.int32), prv, prv_other, raw, raw_other, nxt, nxt_other
    )
    for_partner = deviations(far, high, low, norm, "rows_of_partner")
    returned = moved(for_partner, CHIPS // 2, 0)
    own = deviations(raw, high, low, norm, "rows_of_own")
    lane = lax.broadcasted_iota(jnp.int32, (1, 384), 1)
    column_chip = (chip + CHIPS - 1 + lane // 128) % CHIPS
    here = column_chip // (CHIPS // 2) == lane // 64 % 2
    return jnp.where(here, own, returned)


def solution(mesh):
    return jax.shard_map(
        on_device,
        mesh=mesh,
        in_specs=(P(AXES, None, None),),
        out_specs=P(AXES, None),
        check_vma=False,
    )
```

time: 122 us -> 67 us (0.55)
  waiting for transfers between devices: 85.8 us -> 24.1 us
  starting transfers between devices: 7.43 us -> 35.9 us
  between operations: 14.4 us -> 0.12 us
  other arithmetic: 8.24 us -> 0.65 us
  Pallas kernels: 0 us -> 4.95 us
  matrix products: 4.63 us -> 0 us
    all_gather x1 -> x0, waiting for transfers between devices: 46.1 us -> none  [on_device(): gathered = lax.all_gather(resident, 'rep', axis=0, tiled=True)]
    ppermute x2 -> x7, starting transfers between devices: 7.43 us -> 35.9 us  [moved(): return lax.ppermute(value, AXES, pairs)]
    ppermute x2 -> x7, waiting for transfers between devices: 39.7 us -> 24.1 us  [moved(): return lax.ppermute(value, AXES, pairs)]
    reduce_sum x8 -> x0, other arithmetic: 5.4 us -> none  [the longest x4 3.98 us: square_norms(): return jnp.sum(centred * centred, axis=(1, 2))]
    pallas_call x0 -> x3, Pallas kernels: none -> 4.95 us  [the longest x2 4.04 us: deviations(): pl.pallas_call(rows_kernel, out_shape=jax.ShapeDtypeStruct((32, 384), jnp...]
    dot_general x3 -> x0, matrix products: 4.63 us -> none  [pair_deviation(): lax.dot_general(resident.reshape(row_count * 3, atom_count), visitor.resh...]
    mul x22 -> x0, other arithmetic: 1.54 us -> none  [the longest x21 1.47 us: polar_trace(): iterate = 0.5 * (3.0 * iterate - product)]
  transfers between devices with their start and end apart: 3 -> 7, of which waited for: 3 -> 3; matrix products, arithmetic and copies ran while one was open for 2% -> 0% of each run, Pallas kernels for 0% -> 4%
where the time goes in v1:
time: 67 us; the launch traced here: 66.7 us
  starting transfers between devices  35.9 us (54%)
  waiting for transfers between devices  24.1 us (36%)
  Pallas kernels  4.95 us (7%)
  local copies, waits for them, and re-layouts  0.99 us (1%)
    ppermute x7, starting transfers between devices, moved(): return lax.ppermute(value, AXES, pairs)  35.9 us
    ppermute x7, waiting for transfers between devices, moved(): return lax.ppermute(value, AXES, pairs)  24.1 us
    pallas_call x2, Pallas kernels, deviations(): pl.pallas_call(rows_kernel, out_shape=jax.ShapeDtypeStruct((32, 384), jnp...  4.04 us
  transfers between devices with their start and end apart: 7, of which 3 were waited for; matrix products, arithmetic and copies ran while one was open for 0% of the time, Pallas kernels for 4%

profile of v1, /device:TPU:1, one launch (start us, length us, event | category | flops | bytes accessed | tf_op | source)
XLA Modules:
  0.0 66.7 jit_solution(4301035154067979117)
XLA Ops:
  0.0 3.9 %collective-permute-start = (f32[96,1024]{1,0:T(8,128)}, f32[96,1024]{1,0:T(8,128)S(1)}, u32[]{:S(2)}, u32[]{:S(2)}) collective-permute-start(f32[96,1024]{1,0:T(8,128)} %bitcast.4), channel_id=1, source_target_pairs={{0,4},{1,5},{4,8},{5,9},{8,12},{9,13},{12,16},{13,17},{16,20},{17,... | collective-permute-start | bytes 1179656 | tf_op jit(solution)/shard_map/ppermute | solution.py:27
  3.9 14.6 %collective-permute-start.3 = (f32[96,1024]{1,0:T(8,128)}, f32[96,1024]{1,0:T(8,128)S(1)}, u32[]{:S(2)}, u32[]{:S(2)}) collective-permute-start(f32[96,1024]{1,0:T(8,128)} %bitcast.5), channel_id=1, source_target_pairs={{0,510},{1,511},{4,0},{5,1},{8,4},{9,5},{12,8},{13,9},{16,12},{17,... | collective-permute-start | bytes 1179656 | tf_op jit(solution)/shard_map/ppermute | solution.py:27
  18.5 2.9 %collective-permute-start.2 = (f32[96,1024]{1,0:T(8,128)}, f32[96,1024]{1,0:T(8,128)S(1)}, u32[]{:S(2)}, u32[]{:S(2)}) collective-permute-start(f32[96,1024]{1,0:T(8,128)} %bitcast.6), channel_id=1, source_target_pairs={{0,1},{1,0},{4,5},{5,4},{8,9},{9,8},{12,13},{13,12},{16,17},{17,16... | collective-permute-start | bytes 1179656 | tf_op jit(solution)/shard_map/ppermute | solution.py:27
  21.4 4.2 %collective-permute-done.z0 = f32[96,1024]{1,0:T(8,128)S(1)} collective-permute-done((f32[96,1024]{1,0:T(8,128)}, f32[96,1024]{1,0:T(8,128)S(1)}, u32[]{:S(2)}, u32[]{:S(2)}) %collective-permute-start) | collective-permute-done | bytes 393248 | tf_op jit(solution)/shard_map/ppermute | solution.py:27
  25.6 3.1 %collective-permute-start.1 = (f32[96,1024]{1,0:T(8,128)S(1)}, f32[96,1024]{1,0:T(8,128)S(1)}, u32[]{:S(2)}, u32[]{:S(2)}) collective-permute-start(f32[96,1024]{1,0:T(8,128)S(1)} %collective-permute-done.z0), channel_id=1, source_target_pairs={{0,1},{1,0},{4,5},{5,4},{8,9},{9,8},{12,13},{13,12},{16,17},{17,16... | collective-permute-start | bytes 1179656 | tf_op jit(solution)/shard_map/ppermute | solution.py:27
  28.8 0.0 collective-permute-done.3.b0
  28.8 1.9 %collective-permute-start.4 = (f32[96,1024]{1,0:T(8,128)S(1)}, f32[96,1024]{1,0:T(8,128)S(1)}, u32[]{:S(2)}, u32[]{:S(2)}) collective-permute-start(f32[96,1024]{1,0:T(8,128)S(1)} %collective-permute-done.3.b0), channel_id=1, source_target_pairs={{0,1},{1,0},{4,5},{5,4},{8,9},{9,8},{12,13},{13,12},{16,17},{17,16... | collective-permute-start | bytes 1179656 | tf_op jit(solution)/shard_map/ppermute | solution.py:27
  30.7 4.4 %collective-permute-start.5 = (f32[96,1024]{1,0:T(8,128)}, f32[96,1024]{1,0:T(8,128)S(1)}, u32[]{:S(2)}, u32[]{:S(2)}) collective-permute-start(f32[96,1024]{1,0:T(8,128)} %bitcast.7), channel_id=1, source_target_pairs={{0,2},{1,3},{4,6},{5,7},{8,10},{9,11},{12,14},{13,15},{16,18},{17,... | collective-permute-start | bytes 1179656 | tf_op jit(solution)/shard_map/ppermute | solution.py:27
  35.2 0.0 collective-permute-done.2.a1
  35.2 0.0 collective-permute-done.1.z1
  35.2 0.0 collective-permute-done.4.b1
  35.2 0.0 copy-start
  35.2 1.0 %copy-done = f32[32,3,1024]{2,0,1:T(8,128)S(1)} copy-done((f32[32,3,1024]{2,0,1:T(8,128)S(1)}, f32[32,3,1024]{2,0,1:T(8,128)}, u32[]{:S(2)}) %copy-start) | copy-done | bytes 393240
  36.2 0.9 %prepare.1 = (bf16[3,256,1024]{2,1,0:T(8,128)(2,1)S(1)}, bf16[3,256,1024]{2,1,0:T(8,128)(2,1)S(1)}, f32[8,256]{1,0:T(8,128)S(1)}) custom-call(s32[1]{0:T(128)} %bitcast.2.core_ref, f32[96,1024]{1,0:T(8,128)S(1)} %collective-permute-done.z0, f32[96,1024]{1,0:T(8,128)S(1)} %collective-permute-done.1.z1, f32[96,1024]{1,0:T(8,128)S(1)} %bitcast.8, ...), custom_call_target="tpu_custom_call" | custom-call | tf_op jit(solution)/shard_map/prepare/pallas_call | solution.py:101
  37.1 18.2 %collective-permute-done.5.rows_ref = f32[96,1024]{1,0:T(8,128)S(1)} collective-permute-done((f32[96,1024]{1,0:T(8,128)}, f32[96,1024]{1,0:T(8,128)S(1)}, u32[]{:S(2)}, u32[]{:S(2)}) %collective-permute-start.5) | collective-permute-done | bytes 393248 | tf_op jit(solution)/shard_map/ppermute | solution.py:27
  55.3 2.0 %rows_of_partner.1 = f32[32,384]{1,0:T(8,128)S(1)} custom-call(f32[96,1024]{1,0:T(8,128)S(1)} %collective-permute-done.5.rows_ref, bf16[3,256,1024]{2,1,0:T(8,128)(2,1)S(1)} %get-tuple-element.8.high_ref, bf16[3,256,1024]{2,1,0:T(8,128)(2,1)S(1)} %get-tuple-element.9.low_ref, f32[8,256]{1,0:T(8,128)S(1)} %get-tuple-element.10.norm_ref), custom_call_target="tpu_custom_call" | custom-call | tf_op jit(solution)/shard_map/rows_of_partner/pallas_call | solution.py:118
  57.3 5.1 %collective-permute-start.6 = (f32[32,384]{1,0:T(8,128)S(1)}, f32[32,384]{1,0:T(8,128)S(1)}, u32[]{:S(2)}, u32[]{:S(2)}) collective-permute-start(f32[32,384]{1,0:T(8,128)S(1)} %rows_of_partner.1), channel_id=1, source_target_pairs={{0,2},{1,3},{4,6},{5,7},{8,10},{9,11},{12,14},{13,15},{16,18},{17,... | collective-permute-start | bytes 147464 | tf_op jit(solution)/shard_map/ppermute | solution.py:27
  62.5 2.0 %rows_of_own.1 = f32[32,384]{1,0:T(8,128)S(1)} custom-call(f32[96,1024]{1,0:T(8,128)S(1)} %bitcast.9, bf16[3,256,1024]{2,1,0:T(8,128)(2,1)S(1)} %get-tuple-element.8.high_ref, bf16[3,256,1024]{2,1,0:T(8,128)(2,1)S(1)} %get-tuple-element.9.low_ref, f32[8,256]{1,0:T(8,128)S(1)} %get-tuple-element.10.norm_ref), custom_call_target="tpu_custom_call" | custom-call | tf_op jit(solution)/shard_map/rows_of_own/pallas_call | solution.py:118
  64.5 1.6 %collective-permute-done.6 = f32[32,384]{1,0:T(8,128)S(1)} collective-permute-done((f32[32,384]{1,0:T(8,128)S(1)}, f32[32,384]{1,0:T(8,128)S(1)}, u32[]{:S(2)}, u32[]{:S(2)}) %collective-permute-start.6) | collective-permute-done | bytes 49184 | tf_op jit(solution)/shard_map/ppermute | solution.py:27
  66.1 0.6 broadcast_select_fusion
  (1 shorter events, 0.0 us)
Async XLA Ops:
  0.0 25.6 %collective-permute-start = (f32[96,1024]{1,0:T(8,128)}, f32[96,1024]{1,0:T(8,128)S(1)}, u32[]{:S(2)}, u32[]{:S(2)}) collective-permute-start(f32[96,1024]{1,0:T(8,128)} %bitcast.4), channel_id=1, source_target_pairs={{0,4},{1,5},{4,8},{5,9},{8,12},{9,13},{12,16},{13,17},{16,20},{17,... | collective-permute-start | bytes 1179656 | tf_op jit(solution)/shard_map/ppermute | solution.py:27
  3.9 24.8 %collective-permute-start.3 = (f32[96,1024]{1,0:T(8,128)}, f32[96,1024]{1,0:T(8,128)S(1)}, u32[]{:S(2)}, u32[]{:S(2)}) collective-permute-start(f32[96,1024]{1,0:T(8,128)} %bitcast.5), channel_id=1, source_target_pairs={{0,510},{1,511},{4,0},{5,1},{8,4},{9,5},{12,8},{13,9},{16,12},{17,... | collective-permute-start | bytes 1179656 | tf_op jit(solution)/shard_map/ppermute | solution.py:27
  18.5 16.6 %collective-permute-start.2 = (f32[96,1024]{1,0:T(8,128)}, f32[96,1024]{1,0:T(8,128)S(1)}, u32[]{:S(2)}, u32[]{:S(2)}) collective-permute-start(f32[96,1024]{1,0:T(8,128)} %bitcast.6), channel_id=1, source_target_pairs={{0,1},{1,0},{4,5},{5,4},{8,9},{9,8},{12,13},{13,12},{16,17},{17,16... | collective-permute-start | bytes 1179656 | tf_op jit(solution)/shard_map/ppermute | solution.py:27
  25.6 9.5 %collective-permute-start.1 = (f32[96,1024]{1,0:T(8,128)S(1)}, f32[96,1024]{1,0:T(8,128)S(1)}, u32[]{:S(2)}, u32[]{:S(2)}) collective-permute-start(f32[96,1024]{1,0:T(8,128)S(1)} %collective-permute-done.z0), channel_id=1, source_target_pairs={{0,1},{1,0},{4,5},{5,4},{8,9},{9,8},{12,13},{13,12},{16,17},{17,16... | collective-permute-start | bytes 1179656 | tf_op jit(solution)/shard_map/ppermute | solution.py:27
  28.8 6.4 %collective-permute-start.4 = (f32[96,1024]{1,0:T(8,128)S(1)}, f32[96,1024]{1,0:T(8,128)S(1)}, u32[]{:S(2)}, u32[]{:S(2)}) collective-permute-start(f32[96,1024]{1,0:T(8,128)S(1)} %collective-permute-done.3.b0), channel_id=1, source_target_pairs={{0,1},{1,0},{4,5},{5,4},{8,9},{9,8},{12,13},{13,12},{16,17},{17,16... | collective-permute-start | bytes 1179656 | tf_op jit(solution)/shard_map/ppermute | solution.py:27
  30.7 24.6 %collective-permute-start.5 = (f32[96,1024]{1,0:T(8,128)}, f32[96,1024]{1,0:T(8,128)S(1)}, u32[]{:S(2)}, u32[]{:S(2)}) collective-permute-start(f32[96,1024]{1,0:T(8,128)} %bitcast.7), channel_id=1, source_target_pairs={{0,2},{1,3},{4,6},{5,7},{8,10},{9,11},{12,14},{13,15},{16,18},{17,... | collective-permute-start | bytes 1179656 | tf_op jit(solution)/shard_map/ppermute | solution.py:27
  35.2 1.0 %copy-start = (f32[32,3,1024]{2,0,1:T(8,128)S(1)}, f32[32,3,1024]{2,0,1:T(8,128)}, u32[]{:S(2)}) copy-start(f32[32,3,1024]{2,0,1:T(8,128)} %param.1) | copy-start | bytes 1179652
  57.3 8.7 %collective-permute-start.6 = (f32[32,384]{1,0:T(8,128)S(1)}, f32[32,384]{1,0:T(8,128)S(1)}, u32[]{:S(2)}, u32[]{:S(2)}) collective-permute-start(f32[32,384]{1,0:T(8,128)S(1)} %rows_of_partner.1), channel_id=1, source_target_pairs={{0,2},{1,3},{4,6},{5,7},{8,10},{9,11},{12,14},{13,15},{16,18},{17,... | collective-permute-start | bytes 147464 | tf_op jit(solution)/shard_map/ppermute | solution.py:27

commit v2 on v1

v2 whole, which is shorter than its diff:
```python
import functools

import jax
import jax.numpy as jnp
from jax import lax
from jax.experimental import pallas as pl
from jax.experimental.pallas import tpu as pltpu
from jax.sharding import PartitionSpec as P

ITERS = 8
ATOMS = 1024
AXES = ("blk", "rep")
CHIPS = 256
PLANE = 32


def device_of(chip, core):
    half, block = divmod(chip % CHIPS, CHIPS // 2)
    return block * 4 + half * 2 + core


def moved(value, chips, cores, senders=range(CHIPS)):
    pairs = [
        (device_of(chip, core), device_of(chip + chips, (core + cores) % 2))
        for chip in senders
        for core in range(2)
    ]
    return lax.ppermute(value, AXES, pairs)


def centred_of(raw):
    return raw - jnp.sum(raw, axis=1, keepdims=True) * (1.0 / ATOMS)


def split(value):
    high = value.astype(jnp.bfloat16)
    low = (value - high.astype(jnp.float32)).astype(jnp.bfloat16)
    return high, low


def prepare_kernel(core_ref, *refs):
    frames, (high_ref, low_ref, norm_ref, column_ref) = refs[:6], refs[6:]
    core = core_ref[0]
    column_ref[...] = jnp.zeros_like(column_ref)
    for n, ref in enumerate(frames):
        at = core if n % 2 == 0 else 1 - core
        start = pl.multiple_of(64 * (n // 2) + 32 * at, 32)
        norm = jnp.zeros((32, 1), jnp.float32)
        for b in range(3):
            centred = centred_of(ref[32 * b : 32 * b + 32, :])
            norm = norm + jnp.sum(centred * centred, axis=1, keepdims=True)
            high, low = split(centred)
            high_ref[b, pl.ds(start, 32), :] = high
            low_ref[b, pl.ds(start, 32), :] = low
        column_ref[pl.ds(start, 32), :] = jnp.broadcast_to(norm, (32, 128))
    for b in range(3):
        high_ref[b, 192:256, :] = jnp.zeros((64, ATOMS), jnp.bfloat16)
        low_ref[b, 192:256, :] = jnp.zeros((64, ATOMS), jnp.bfloat16)
    norm_ref[...] = jnp.transpose(column_ref[...])[0:8, :]


def polar_trace(cov, scale):
    x = [[cov[a][b] * scale for b in range(3)] for a in range(3)]
    for _ in range(ITERS):
        m = {}
        for p in range(3):
            for q in range(p, 3):
                g = x[0][p] * x[0][q] + x[1][p] * x[1][q] + x[2][p] * x[2][q]
                m[p, q] = m[q, p] = 1.5 - 0.5 * g if p == q else -0.5 * g
        x = [[x[a][0] * m[0, b] + x[a][1] * m[1, b] + x[a][2] * m[2, b] for b in range(3)] for a in range(3)]
    return sum(x[a][b] * cov[a][b] for a in range(3) for b in range(3))


def fill_rows(rows_ref, high_ref, low_ref, norm_ref, out_ref, left_ref, cov_ref):
    norm = jnp.zeros((32, 1), jnp.float32)
    for a in range(3):
        centred = centred_of(rows_ref[32 * a : 32 * a + 32, :])
        norm = norm + jnp.sum(centred * centred, axis=1, keepdims=True)
        high, low = split(centred)
        left_ref[32 * a : 32 * a + 32, :] = high
        left_ref[96 + 32 * a : 128 + 32 * a, :] = low
    dims = (((1,), (1,)), ((), ()))
    for b in range(3):
        one = lax.dot_general(left_ref[...], high_ref[b], dims, preferred_element_type=jnp.float32)
        two = lax.dot_general(left_ref[...], low_ref[b], dims, preferred_element_type=jnp.float32)
        cov_ref[b] = one[:96] + (one[96:] + two[:96] + two[96:])
    row_root = 1.0 / jnp.sqrt(norm + 1e-6)
    tiles = []
    for t in range(2):
        lanes = slice(128 * t, 128 * t + 128)
        columns = norm_ref[0:1, lanes]
        scale = row_root * (1.0 / jnp.sqrt(columns + 1e-6))
        cov = [[cov_ref[b, 32 * a : 32 * a + 32, lanes] for b in range(3)] for a in range(3)]
        aligned = polar_trace(cov, scale)
        tiles.append((norm + columns - 2.0 * aligned) * (1.0 / ATOMS))
    if out_ref.shape[1] == 128:
        out_ref[...] = tiles[0]
    else:
        prev, own, nxt = tiles[0][:, :64], tiles[0][:, 64:], tiles[1][:, :64]
        out_ref[...] = jnp.concatenate([prev, prev, own, own, nxt, nxt], axis=1)


def own_kernel(rows_ref, high_ref, low_ref, norm_ref, partner_ref, out_ref, message_ref, left_ref, cov_ref):
    fill_rows(rows_ref, high_ref, low_ref, norm_ref, out_ref, left_ref, cov_ref)
    message_ref[...] = jnp.concatenate([out_ref[:, :64], partner_ref[:, :64]], axis=1)


def partner_kernel(chip_ref, rows_ref, high_ref, low_ref, norm_ref, *refs, before):
    out_ref, left_ref, cov_ref = refs[-3:]
    here = (chip_ref[0] % PLANE == PLANE - 1) == before

    @pl.when(here)
    def _():
        fill_rows(rows_ref, high_ref, low_ref, norm_ref, out_ref, left_ref, cov_ref)

    @pl.when(jnp.logical_not(here))
    def _():
        out_ref[...] = jnp.zeros_like(out_ref)


def next_kernel(chip_ref, core_ref, tiles_ref, mine_ref, other_ref, out_ref):
    chip, core = chip_ref[0], core_ref[0]
    out_ref[...] = tiles_ref[...]

    @pl.when(chip % PLANE == PLANE - 1)
    def _():
        mine, other = mine_ref[...], other_ref[...]
        zero = core == 0
        pair = jnp.concatenate([jnp.where(zero, mine, other), jnp.where(zero, other, mine)], axis=0)
        pair = jnp.concatenate([pair, pair], axis=0)
        turned = jnp.transpose(pair)[:, :64]
        same = jnp.where(zero, turned[0:32], turned[32:64])
        cross = jnp.where(zero, turned[64:96], turned[96:128])
        first = (chip + 1) % CHIPS // (CHIPS // 2) == 0
        out_ref[:, 256:384] = jnp.concatenate(
            [jnp.where(first, same, cross), jnp.where(first, cross, same)], axis=1
        )


def final_kernel(chip_ref, tiles_ref, far_ref, out_ref):
    chip = chip_ref[0]
    out_ref[...] = tiles_ref[...]

    @pl.when(chip % PLANE == PLANE - 1)
    def _():
        prev, own = far_ref[:, :64], far_ref[:, 64:]
        far = jnp.concatenate([prev, prev, own, own], axis=1)
        out_ref[:, :256] = jnp.where(is_here(chip)[:, :256], tiles_ref[:, :256], far)


def is_here(chip):
    lane = lax.broadcasted_iota(jnp.int32, (32, 384), 1)
    return (chip + (CHIPS - 1) + lane // 128) % CHIPS // (CHIPS // 2) == lane // 64 % 2


def tiles_kernel(chip_ref, own_ref, far_ref, out_ref):
    out_ref[...] = jnp.where(is_here(chip_ref[0]), own_ref[...], far_ref[...])


def small_call(kernel, scalars, arrays, name):
    return pl.pallas_call(
        kernel,
        out_shape=TILES,
        in_specs=[pl.BlockSpec(memory_space=pltpu.SMEM)] * len(scalars) + [SPEC] * len(arrays),
        out_specs=SPEC,
        compiler_params=pltpu.CompilerParams(vmem_limit_bytes=2 << 20),
        name=name,
    )(*scalars, *arrays)


def prepare(core, *frames):
    spec = pl.BlockSpec(memory_space=pltpu.VMEM)
    wide = jax.ShapeDtypeStruct((3, 256, ATOMS), jnp.bfloat16)
    return pl.pallas_call(
        prepare_kernel,
        out_shape=(wide, wide, jax.ShapeDtypeStruct((8, 256), jnp.float32)),
        in_specs=[pl.BlockSpec(memory_space=pltpu.SMEM)] + [spec] * 6,
        out_specs=(spec, spec, spec),
        scratch_shapes=[pltpu.VMEM((256, 128), jnp.float32)],
        compiler_params=pltpu.CompilerParams(vmem_limit_bytes=24 << 20),
        name="prepare",
    )(core, *frames)


SPEC = pl.BlockSpec(memory_space=pltpu.VMEM)
SCRATCH = [pltpu.VMEM((192, ATOMS), jnp.bfloat16), pltpu.VMEM((3, 96, 256), jnp.float32)]
TILES = jax.ShapeDtypeStruct((32, 384), jnp.float32)
MESSAGE = jax.ShapeDtypeStruct((32, 128), jnp.float32)


def own_rows(rows, high, low, norm, partner):
    return pl.pallas_call(
        own_kernel,
        out_shape=(TILES, MESSAGE),
        in_specs=[SPEC] * 5,
        out_specs=(SPEC, SPEC),
        scratch_shapes=SCRATCH,
        compiler_params=pltpu.CompilerParams(vmem_limit_bytes=24 << 20),
        name="rows_of_own",
    )(rows, high, low, norm, partner)


def partner_rows(chip, before, *arrays):
    return pl.pallas_call(
        functools.partial(partner_kernel, before=before),
        out_shape=MESSAGE if before else TILES,
        in_specs=[pl.BlockSpec(memory_space=pltpu.SMEM)] + [SPEC] * len(arrays),
        out_specs=SPEC,
        scratch_shapes=SCRATCH,
        compiler_params=pltpu.CompilerParams(vmem_limit_bytes=24 << 20),
        name="rows_of_partner",
    )(chip, *arrays)


def on_device(frames):
    rep = lax.axis_index("rep")
    core = rep % 2
    chip = rep // 2 * (CHIPS // 2) + lax.axis_index("blk")
    always = chip < CHIPS
    chips = range(CHIPS)
    afters = [c for c in chips if c % PLANE == 0]
    befores = [c for c in chips if c % PLANE == PLANE - 1]
    not_after = [c for c in chips if c not in afters]
    not_before = [c for c in chips if c not in befores]
    half = CHIPS // 2
    raw = frames.transpose(1, 0, 2).reshape(96, ATOMS)

    prv = moved(raw, 1, 0)
    nxt = moved(raw, -1, 0, not_after)
    far = moved(raw, half, 0, not_before)
    far_before = moved(raw, half, 0, befores)

    def swap_near(prv, nxt):
        return moved(prv, 0, 1), moved(nxt, 0, 1, not_before)

    raw_other, then = lax.cond(always, lambda raw: (moved(raw, 0, 1), chip), lambda raw: (raw, chip), raw)
    prv_other, nxt_other = lax.cond(then < CHIPS, swap_near, lambda prv, nxt: (prv, nxt), prv, nxt)
    place = tuple(value.reshape(1).astype(jnp.int32) for value in (chip, core))
    columns = prepare(place[1], prv, prv_other, raw, raw_other, nxt, nxt_other)
    for_partner = partner_rows(place[0], False, far, *columns)
    returned = moved(for_partner, half, 0, not_before)
    own, message = own_rows(raw, *columns, for_partner)
    mine = moved(message, -1, 0, afters)
    other = moved(message, -1, 1, afters)
    for_partner_before = partner_rows(place[0], True, far_before, *columns, message)
    returned_before = moved(for_partner_before, half, 0, befores)
    tiles = small_call(tiles_kernel, place[:1], (own, returned), "tiles")
    tiles = small_call(next_kernel, place, (tiles, mine, other), "next_columns")
    return small_call(final_kernel, place[:1], (tiles, returned_before), "final")


def solution(mesh):
    return jax.shard_map(
        on_device,
        mesh=mesh,
        in_specs=(P(AXES, None, None),),
        out_specs=P(AXES, None),
        check_vma=False,
    )
```

time: 67 us -> 48.9 us (0.73)
  the two profiles are of different devices: /device:TPU:1 before, /device:TPU:256 now
where the time goes in v2:
time: 48.9 us; the launch traced here: 48.5 us
  starting transfers between devices  37.9 us (78%)
  Pallas kernels  6.87 us (14%)
  waiting for transfers between devices  3.5 us (7%)
    ppermute x11, starting transfers between devices, moved(): return lax.ppermute(value, AXES, pairs)  37.9 us
    ppermute x11, waiting for transfers between devices, moved(): return lax.ppermute(value, AXES, pairs)  3.5 us
    pallas_call x1, Pallas kernels, prepare(): pl.pallas_call(prepare_kernel, out_shape=(wide, wide, jax.ShapeDtypeStruc...  2.13 us
    pallas_call x2, Pallas kernels, partner_rows(): pl.pallas_call(functools.partial(partner_kernel, before=before), out_shap...  2.04 us
    pallas_call x1, Pallas kernels, own_rows(): pl.pallas_call(own_kernel, out_shape=(TILES, MESSAGE), in_specs=[SPEC] *...  2.02 us
  transfers between devices with their start and end apart: 11, of which 2 were waited for; matrix products, arithmetic and copies ran while one was open for 0% of the time, Pallas kernels for 13%

profile of v2, /device:TPU:256, one launch (start us, length us, event | category | flops | bytes accessed | tf_op | source)
XLA Modules:
  0.0 48.5 jit_solution(292962948401914411)
XLA Ops:
  0.0 3.4 %collective-permute-start.3 = (f32[96,1024]{1,0:T(8,128)}, f32[96,1024]{1,0:T(8,128)S(1)}, u32[]{:S(2)}, u32[]{:S(2)}) collective-permute-start(f32[96,1024]{1,0:T(8,128)} %bitcast.5), channel_id=1, source_target_pairs={{0,4},{1,5},{4,8},{5,9},{8,12},{9,13},{12,16},{13,17},{16,20},{17,... | collective-permute-start | bytes 1179656 | tf_op jit(solution)/shard_map/ppermute | solution.py:28
  3.4 5.8 %collective-permute-start.4 = (f32[96,1024]{1,0:T(8,128)}, f32[96,1024]{1,0:T(8,128)S(1)}, u32[]{:S(2)}, u32[]{:S(2)}) collective-permute-start(f32[96,1024]{1,0:T(8,128)} %bitcast.6), channel_id=1, source_target_pairs={{4,0},{5,1},{8,4},{9,5},{12,8},{13,9},{16,12},{17,13},{20,16},{21,... | collective-permute-start | bytes 1179656 | tf_op jit(solution)/shard_map/ppermute | solution.py:28
  9.2 7.7 %collective-permute-start.5 = (f32[96,1024]{1,0:T(8,128)}, f32[96,1024]{1,0:T(8,128)S(1)}, u32[]{:S(2)}, u32[]{:S(2)}) collective-permute-start(f32[96,1024]{1,0:T(8,128)} %bitcast.7), channel_id=1, source_target_pairs={{0,2},{1,3},{4,6},{5,7},{8,10},{9,11},{12,14},{13,15},{16,18},{17,... | collective-permute-start | bytes 1179656 | tf_op jit(solution)/shard_map/ppermute | solution.py:28
  16.9 0.7 %collective-permute-start.9 = (f32[96,1024]{1,0:T(8,128)}, f32[96,1024]{1,0:T(8,128)S(1)}, u32[]{:S(2)}, u32[]{:S(2)}) collective-permute-start(f32[96,1024]{1,0:T(8,128)} %bitcast.8), channel_id=1, source_target_pairs={{124,126},{125,127},{252,254},{253,255},{380,382},{381,383},{508,5... | collective-permute-start | bytes 1179656 | tf_op jit(solution)/shard_map/ppermute | solution.py:28
  17.6 4.0 %conditional.3 = (f32[96,1024]{1,0:T(8,128)}) conditional(s32[]{:T(128)} %convert_element_type.4, f32[96,1024]{1,0:T(8,128)} %bitcast.9, f32[96,1024]{1,0:T(8,128)} %bitcast.10), branch_computations={%region_2.3_spmd, %region_3.4_spmd} | conditional | bytes 1572912 | solution.py:236
  17.6 1.9 %collective-permute-start.2 = (f32[96,1024]{1,0:T(8,128)}, f32[96,1024]{1,0:T(8,128)}, u32[]{:S(2)}, u32[]{:S(2)}) collective-permute-start(f32[96,1024]{1,0:T(8,128)} %param.3), channel_id=1, source_target_pairs={{0,1},{1,0},{4,5},{5,4},{8,9},{9,8},{12,13},{13,12},{16,17},{17,16... | collective-permute-start | bytes 1179656 | tf_op jit(solution)/shard_map/cond/branch_1_fun/ppermute | solution.py:28
  19.6 2.0 %collective-permute-done.2 = f32[96,1024]{1,0:T(8,128)} collective-permute-done((f32[96,1024]{1,0:T(8,128)}, f32[96,1024]{1,0:T(8,128)}, u32[]{:S(2)}, u32[]{:S(2)}) %collective-permute-start.2) | collective-permute-done | bytes 393248 | tf_op jit(solution)/shard_map/cond/branch_1_fun/ppermute | solution.py:28
  21.6 0.0 copy-start
  21.6 0.0 collective-permute-done.3.refs_0_
  21.6 0.0 collective-permute-done.4.refs_4_
  21.6 6.0 %conditional.2 = (f32[96,1024]{1,0:T(8,128)}, f32[96,1024]{1,0:T(8,128)}) conditional(s32[]{:T(128)} %convert_element_type.4, (f32[96,1024]{1,0:T(8,128)S(1)}, f32[96,1024]{1,0:T(8,128)S(1)}) %tuple.18, (f32[96,1024]{1,0:T(8,128)S(1)}, f32[96,1024]{1,0:T(8,128)S(1)}) %tuple.18), branch_computations={%region_0.1_spmd, %region_1.2_spmd} | conditional | bytes 3145824 | solution.py:237
  21.6 2.2 %collective-permute-start = (f32[96,1024]{1,0:T(8,128)S(1)}, f32[96,1024]{1,0:T(8,128)}, u32[]{:S(2)}, u32[]{:S(2)}) collective-permute-start(f32[96,1024]{1,0:T(8,128)S(1)} %get-tuple-element.18), channel_id=1, source_target_pairs={{0,1},{1,0},{4,5},{5,4},{8,9},{9,8},{12,13},{13,12},{16,17},{17,16... | collective-permute-start | bytes 1179656 | tf_op jit(solution)/shard_map/cond/branch_1_fun/ppermute | solution.py:28
  23.8 2.3 %collective-permute-start.1 = (f32[96,1024]{1,0:T(8,128)S(1)}, f32[96,1024]{1,0:T(8,128)}, u32[]{:S(2)}, u32[]{:S(2)}) collective-permute-start(f32[96,1024]{1,0:T(8,128)S(1)} %get-tuple-element.19), channel_id=1, source_target_pairs={{0,1},{1,0},{4,5},{5,4},{8,9},{9,8},{12,13},{13,12},{16,17},{17,16... | collective-permute-start | bytes 1179656 | tf_op jit(solution)/shard_map/cond/branch_1_fun/ppermute | solution.py:28
  26.1 0.0 collective-permute-done
  26.1 1.4 %collective-permute-done.1 = f32[96,1024]{1,0:T(8,128)} collective-permute-done((f32[96,1024]{1,0:T(8,128)S(1)}, f32[96,1024]{1,0:T(8,128)}, u32[]{:S(2)}, u32[]{:S(2)}) %collective-permute-start.1) | collective-permute-done | bytes 393248 | tf_op jit(solution)/shard_map/cond/branch_1_fun/ppermute | solution.py:28
  27.6 0.0 copy-done
  27.6 2.1 %prepare.1 = (bf16[3,256,1024]{2,1,0:T(8,128)(2,1)S(1)}, bf16[3,256,1024]{2,1,0:T(8,128)(2,1)S(1)}, f32[8,256]{1,0:T(8,128)S(1)}) custom-call(s32[1]{0:T(128)} %bitcast.1.core_ref, f32[96,1024]{1,0:T(8,128)S(1)} %collective-permute-done.3.refs_0_, f32[96,1024]{1,0:T(8,128)} %get-tuple-element.27.refs_1_, f32[96,1024]{1,0:T(8,128)S(1)} %bitcast.11, ...), custom_call_target="tpu_custom_call" | custom-call | tf_op jit(solution)/shard_map/prepare/pallas_call | solution.py:174
  29.7 0.0 collective-permute-done.5.rows_ref
  29.7 2.0 %rows_of_partner.2.partner_ref = f32[32,384]{1,0:T(8,128)S(1)} custom-call(s32[1]{0:T(128)} %bitcast.chip_ref, f32[96,1024]{1,0:T(8,128)S(1)} %collective-permute-done.5.rows_ref, bf16[3,256,1024]{2,1,0:T(8,128)(2,1)S(1)} %get-tuple-element.29.high_ref, bf16[3,256,1024]{2,1,0:T(8,128)(2,1)S(1)} %get-tuple-element.30.low_ref, ...), custom_call_target="tpu_custom_call" | custom-call | tf_op jit(solution)/shard_map/rows_of_partner/pallas_call | solution.py:204
  31.7 12.0 %collective-permute-start.6 = (f32[32,384]{1,0:T(8,128)S(1)}, f32[32,384]{1,0:T(8,128)S(1)}, u32[]{:S(2)}, u32[]{:S(2)}) collective-permute-start(f32[32,384]{1,0:T(8,128)S(1)} %rows_of_partner.2.partner_ref), channel_id=1, source_target_pairs={{0,2},{1,3},{4,6},{5,7},{8,10},{9,11},{12,14},{13,15},{16,18},{17,... | collective-permute-start | bytes 147464 | tf_op jit(solution)/shard_map/ppermute | solution.py:28
  43.7 2.0 %rows_of_own.1 = (f32[32,384]{1,0:T(8,128)S(1)}, f32[32,128]{1,0:T(8,128)S(1)}) custom-call(f32[96,1024]{1,0:T(8,128)S(1)} %bitcast.12, bf16[3,256,1024]{2,1,0:T(8,128)(2,1)S(1)} %get-tuple-element.29.high_ref, bf16[3,256,1024]{2,1,0:T(8,128)(2,1)S(1)} %get-tuple-element.30.low_ref, f32[8,256]{1,0:T(8,128)S(1)} %get-tuple-element.31.norm_ref, ...), custom_call_target="tpu_custom_call" | custom-call | tf_op jit(solution)/shard_map/rows_of_own/pallas_call | solution.py:192
  45.8 0.7 %collective-permute-start.7 = (f32[32,128]{1,0:T(8,128)S(1)}, f32[32,128]{1,0:T(8,128)S(1)}, u32[]{:S(2)}, u32[]{:S(2)}) collective-permute-start(f32[32,128]{1,0:T(8,128)S(1)} %get-tuple-element.33.refs_0_), channel_id=1, source_target_pairs={{0,510},{1,511},{128,124},{129,125},{256,252},{257,253},{384,380},... | collective-permute-start | bytes 49160 | tf_op jit(solution)/shard_map/ppermute | solution.py:28
  46.4 0.7 %collective-permute-start.8 = (f32[32,128]{1,0:T(8,128)S(1)}, f32[32,128]{1,0:T(8,128)S(1)}, u32[]{:S(2)}, u32[]{:S(2)}) collective-permute-start(f32[32,128]{1,0:T(8,128)S(1)} %get-tuple-element.33.refs_0_), channel_id=1, source_target_pairs={{0,511},{1,510},{128,125},{129,124},{256,253},{257,252},{384,381},... | collective-permute-start | bytes 49160 | tf_op jit(solution)/shard_map/ppermute | solution.py:28
  47.1 0.0 collective-permute-done.9.rows_ref
  47.1 0.7 %collective-permute-start.10 = (f32[32,128]{1,0:T(8,128)S(1)}, f32[32,128]{1,0:T(8,128)S(1)}, u32[]{:S(2)}, u32[]{:S(2)}) collective-permute-start(f32[32,128]{1,0:T(8,128)S(1)} %rows_of_partner.3), channel_id=1, source_target_pairs={{124,126},{125,127},{252,254},{253,255},{380,382},{381,383},{508,5... | collective-permute-start | bytes 49160 | tf_op jit(solution)/shard_map/ppermute | solution.py:28
  47.8 0.0 collective-permute-done.6.far_ref
  47.8 0.0 collective-permute-done.7.mine_ref
  47.9 0.0 collective-permute-done.8.other_ref
  47.9 0.0 collective-permute-done.10.far_ref
  47.9 0.6 %final.1 = f32[32,384]{1,0:T(8,128)} custom-call(s32[1]{0:T(128)} %bitcast.chip_ref, f32[32,384]{1,0:T(8,128)S(1)} %next_columns.1.tiles_ref, f32[32,128]{1,0:T(8,128)S(1)} %collective-permute-done.10.far_ref), custom_call_target="tpu_custom_call" | custom-call | tf_op jit(solution)/shard_map/final/pallas_call | solution.py:161
  (3 shorter events, 0.1 us)
Async XLA Ops:
  0.0 21.6 %collective-permute-start.3 = (f32[96,1024]{1,0:T(8,128)}, f32[96,1024]{1,0:T(8,128)S(1)}, u32[]{:S(2)}, u32[]{:S(2)}) collective-permute-start(f32[96,1024]{1,0:T(8,128)} %bitcast.5), channel_id=1, source_target_pairs={{0,4},{1,5},{4,8},{5,9},{8,12},{9,13},{12,16},{13,17},{16,20},{17,... | collective-permute-start | bytes 1179656 | tf_op jit(solution)/shard_map/ppermute | solution.py:28
  3.4 18.2 %collective-permute-start.4 = (f32[96,1024]{1,0:T(8,128)}, f32[96,1024]{1,0:T(8,128)S(1)}, u32[]{:S(2)}, u32[]{:S(2)}) collective-permute-start(f32[96,1024]{1,0:T(8,128)} %bitcast.6), channel_id=1, source_target_pairs={{4,0},{5,1},{8,4},{9,5},{12,8},{13,9},{16,12},{17,13},{20,16},{21,... | collective-permute-start | bytes 1179656 | tf_op jit(solution)/shard_map/ppermute | solution.py:28
  9.2 20.5 %collective-permute-start.5 = (f32[96,1024]{1,0:T(8,128)}, f32[96,1024]{1,0:T(8,128)S(1)}, u32[]{:S(2)}, u32[]{:S(2)}) collective-permute-start(f32[96,1024]{1,0:T(8,128)} %bitcast.7), channel_id=1, source_target_pairs={{0,2},{1,3},{4,6},{5,7},{8,10},{9,11},{12,14},{13,15},{16,18},{17,... | collective-permute-start | bytes 1179656 | tf_op jit(solution)/shard_map/ppermute | solution.py:28
  16.9 30.2 %collective-permute-start.9 = (f32[96,1024]{1,0:T(8,128)}, f32[96,1024]{1,0:T(8,128)S(1)}, u32[]{:S(2)}, u32[]{:S(2)}) collective-permute-start(f32[96,1024]{1,0:T(8,128)} %bitcast.8), channel_id=1, source_target_pairs={{124,126},{125,127},{252,254},{253,255},{380,382},{381,383},{508,5... | collective-permute-start | bytes 1179656 | tf_op jit(solution)/shard_map/ppermute | solution.py:28
  17.6 4.0 %collective-permute-start.2 = (f32[96,1024]{1,0:T(8,128)}, f32[96,1024]{1,0:T(8,128)}, u32[]{:S(2)}, u32[]{:S(2)}) collective-permute-start(f32[96,1024]{1,0:T(8,128)} %param.3), channel_id=1, source_target_pairs={{0,1},{1,0},{4,5},{5,4},{8,9},{9,8},{12,13},{13,12},{16,17},{17,16... | collective-permute-start | bytes 1179656 | tf_op jit(solution)/shard_map/cond/branch_1_fun/ppermute | solution.py:28
  21.6 6.0 %copy-start = (f32[32,3,1024]{2,0,1:T(8,128)S(1)}, f32[32,3,1024]{2,0,1:T(8,128)}, u32[]{:S(2)}) copy-start(f32[32,3,1024]{2,0,1:T(8,128)} %param.5) | copy-start | bytes 1179652
  21.6 4.5 %collective-permute-start = (f32[96,1024]{1,0:T(8,128)S(1)}, f32[96,1024]{1,0:T(8,128)}, u32[]{:S(2)}, u32[]{:S(2)}) collective-permute-start(f32[96,1024]{1,0:T(8,128)S(1)} %get-tuple-element.18), channel_id=1, source_target_pairs={{0,1},{1,0},{4,5},{5,4},{8,9},{9,8},{12,13},{13,12},{16,17},{17,16... | collective-permute-start | bytes 1179656 | tf_op jit(solution)/shard_map/cond/branch_1_fun/ppermute | solution.py:28
  23.8 3.8 %collective-permute-start.1 = (f32[96,1024]{1,0:T(8,128)S(1)}, f32[96,1024]{1,0:T(8,128)}, u32[]{:S(2)}, u32[]{:S(2)}) collective-permute-start(f32[96,1024]{1,0:T(8,128)S(1)} %get-tuple-element.19), channel_id=1, source_target_pairs={{0,1},{1,0},{4,5},{5,4},{8,9},{9,8},{12,13},{13,12},{16,17},{17,16... | collective-permute-start | bytes 1179656 | tf_op jit(solution)/shard_map/cond/branch_1_fun/ppermute | solution.py:28
  31.7 16.1 %collective-permute-start.6 = (f32[32,384]{1,0:T(8,128)S(1)}, f32[32,384]{1,0:T(8,128)S(1)}, u32[]{:S(2)}, u32[]{:S(2)}) collective-permute-start(f32[32,384]{1,0:T(8,128)S(1)} %rows_of_partner.2.partner_ref), channel_id=1, source_target_pairs={{0,2},{1,3},{4,6},{5,7},{8,10},{9,11},{12,14},{13,15},{16,18},{17,... | collective-permute-start | bytes 147464 | tf_op jit(solution)/shard_map/ppermute | solution.py:28
  45.8 2.1 %collective-permute-start.7 = (f32[32,128]{1,0:T(8,128)S(1)}, f32[32,128]{1,0:T(8,128)S(1)}, u32[]{:S(2)}, u32[]{:S(2)}) collective-permute-start(f32[32,128]{1,0:T(8,128)S(1)} %get-tuple-element.33.refs_0_), channel_id=1, source_target_pairs={{0,510},{1,511},{128,124},{129,125},{256,252},{257,253},{384,380},... | collective-permute-start | bytes 49160 | tf_op jit(solution)/shard_map/ppermute | solution.py:28
  46.4 1.4 %collective-permute-start.8 = (f32[32,128]{1,0:T(8,128)S(1)}, f32[32,128]{1,0:T(8,128)S(1)}, u32[]{:S(2)}, u32[]{:S(2)}) collective-permute-start(f32[32,128]{1,0:T(8,128)S(1)} %get-tuple-element.33.refs_0_), channel_id=1, source_target_pairs={{0,511},{1,510},{128,125},{129,124},{256,253},{257,252},{384,381},... | collective-permute-start | bytes 49160 | tf_op jit(solution)/shard_map/ppermute | solution.py:28
  47.1 0.8 %collective-permute-start.10 = (f32[32,128]{1,0:T(8,128)S(1)}, f32[32,128]{1,0:T(8,128)S(1)}, u32[]{:S(2)}, u32[]{:S(2)}) collective-permute-start(f32[32,128]{1,0:T(8,128)S(1)} %rows_of_partner.3), channel_id=1, source_target_pairs={{124,126},{125,127},{252,254},{253,255},{380,382},{381,383},{508,5... | collective-permute-start | bytes 49160 | tf_op jit(solution)/shard_map/ppermute | solution.py:28

commit v3 on v2

--- a/solution.py
+++ b/solution.py
@@ -94,15 +94,46 @@
         aligned = polar_trace(cov, scale)
         tiles.append((norm + columns - 2.0 * aligned) * (1.0 / ATOMS))
     if out_ref.shape[1] == 128:
-        out_ref[...] = tiles[0]
+        out_ref[0:32, :] = tiles[0]
+        if out_ref.shape[0] == 48:
+            out_ref[32:48, :] = jnp.concatenate([tiles[1][:16, :64], tiles[1][16:, :64]], axis=1)
     else:
-        prev, own, nxt = tiles[0][:, :64], tiles[0][:, 64:], tiles[1][:, :64]
-        out_ref[...] = jnp.concatenate([prev, prev, own, own, nxt, nxt], axis=1)
-
-
-def own_kernel(rows_ref, high_ref, low_ref, norm_ref, partner_ref, out_ref, message_ref, left_ref, cov_ref):
-    fill_rows(rows_ref, high_ref, low_ref, norm_ref, out_ref, left_ref, cov_ref)
-    message_ref[...] = jnp.concatenate([out_ref[:, :64], partner_ref[:, :64]], axis=1)
+        out_ref[...] = doubled(tiles[0], tiles[1][:, :64])
+
+
+def doubled(first, nxt):
+    prev, own = first[:, :64], first[:, 64:]
+    return jnp.concatenate([prev, prev, own, own, nxt, nxt], axis=1)
+
+
+def is_late(chip):
+    return jnp.logical_and(chip % PLANE == 0, jnp.logical_or(chip == 0, chip // PLANE >= 3))
+
+
+def early_kernel(chip_ref, rows_ref, high_ref, low_ref, norm_ref, out_ref, left_ref, cov_ref):
+    late = is_late(chip_ref[0])
+
+    @pl.when(jnp.logical_not(late))
+    def _():
+        fill_rows(rows_ref, high_ref, low_ref, norm_ref, out_ref, left_ref, cov_ref)
+
+    @pl.when(late)
+    def _():
+        out_ref[...] = jnp.zeros_like(out_ref)
+
+
+def own_kernel(chip_ref, rows_ref, high_ref, low_ref, norm_ref, early_ref, partner_ref, out_ref, message_ref, left_ref, cov_ref):
+    late = is_late(chip_ref[0])
+
+    @pl.when(late)
+    def _():
+        fill_rows(rows_ref, high_ref, low_ref, norm_ref, out_ref, left_ref, cov_ref)
+
+    @pl.when(jnp.logical_not(late))
+    def _():
+        out_ref[...] = early_ref[...]
+
+    message_ref[...] = jnp.concatenate([out_ref[:, :64], partner_ref[0:32, :64]], axis=1)
 
 
 def partner_kernel(chip_ref, rows_ref, high_ref, low_ref, norm_ref, *refs, before):
@@ -154,7 +185,8 @@
 
 
 def tiles_kernel(chip_ref, own_ref, far_ref, out_ref):
-    out_ref[...] = jnp.where(is_here(chip_ref[0]), own_ref[...], far_ref[...])
+    nxt = jnp.concatenate([far_ref[32:48, :64], far_ref[32:48, 64:]], axis=0)
+    out_ref[...] = jnp.where(is_here(chip_ref[0]), own_ref[...], doubled(far_ref[0:32, :], nxt))
 
 
 def small_call(kernel, scalars, arrays, name):
@@ -186,24 +218,25 @@
 SCRATCH = [pltpu.VMEM((192, ATOMS), jnp.bfloat16), pltpu.VMEM((3, 96, 256), jnp.float32)]
 TILES = jax.ShapeDtypeStruct((32, 384), jnp.float32)
 MESSAGE = jax.ShapeDtypeStruct((32, 128), jnp.float32)
-
-
-def own_rows(rows, high, low, norm, partner):
-    return pl.pallas_call(
-        own_kernel,
-        out_shape=(TILES, MESSAGE),
-        in_specs=[SPEC] * 5,
-        out_specs=(SPEC, SPEC),
+PACKED = jax.ShapeDtypeStruct((48, 128), jnp.float32)
+
+
+def own_rows(chip, rows, high, low, norm, *more):
+    return pl.pallas_call(
+        own_kernel if more else early_kernel,
+        out_shape=(TILES, MESSAGE) if more else TILES,
+        in_specs=[pl.BlockSpec(memory_space=pltpu.SMEM)] + [SPEC] * (4 + len(more)),
+        out_specs=(SPEC, SPEC) if more else SPEC,
         scratch_shapes=SCRATCH,
         compiler_params=pltpu.CompilerParams(vmem_limit_bytes=24 << 20),
-        name="rows_of_own",
-    )(rows, high, low, norm, partner)
+        name="rows_of_own" if more else "early_rows_of_own",
+    )(chip, rows, high, low, norm, *more)
 
 
 def partner_rows(chip, before, *arrays):
     return pl.pallas_call(
         functools.partial(partner_kernel, before=before),
-        out_shape=MESSAGE if before else TILES,
+        out_shape=MESSAGE if before else PACKED,
         in_specs=[pl.BlockSpec(memory_space=pltpu.SMEM)] + [SPEC] * len(arrays),
         out_specs=SPEC,
         scratch_shapes=SCRATCH,
@@ -237,9 +270,10 @@
     prv_other, nxt_other = lax.cond(then < CHIPS, swap_near, lambda prv, nxt: (prv, nxt), prv, nxt)
     place = tuple(value.reshape(1).astype(jnp.int32) for value in (chip, core))
     columns = prepare(place[1], prv, prv_other, raw, raw_other, nxt, nxt_other)
-    for_partner = partner_rows(place[0], False, far, *columns)
+    early = own_rows(place[0], raw, *columns)
+    for_partner = partner_rows(place[0], False, far, *columns, early)
     returned = moved(for_partner, half, 0, not_before)
-    own, message = own_rows(raw, *columns, for_partner)
+    own, message = own_rows(place[0], raw, *columns, early, for_partner)
     mine = moved(message, -1, 0, afters)
     other = moved(message, -1, 1, afters)
     for_partner_before = partner_rows(place[0], True, far_before, *columns, message)

time: 48.9 us -> 47.7 us (0.975)
  the two profiles are of different devices: /device:TPU:256 before, /device:TPU:1 now
where the time goes in v3:
time: 47.7 us; the launch traced here: 47.4 us
  starting transfers between devices  29.2 us (61%)
  waiting for transfers between devices  10.9 us (23%)
  Pallas kernels  7.05 us (15%)
    ppermute x11, starting transfers between devices, moved(): return lax.ppermute(value, AXES, pairs)  29.2 us
    ppermute x11, waiting for transfers between devices, moved(): return lax.ppermute(value, AXES, pairs)  10.9 us
    pallas_call x1, Pallas kernels, prepare(): pl.pallas_call(prepare_kernel, out_shape=(wide, wide, jax.ShapeDtypeStruc...  2.13 us
    pallas_call x2, Pallas kernels, own_rows(): pl.pallas_call(own_kernel if more else early_kernel, out_shape=(TILES, ME...  2.1 us
    pallas_call x2, Pallas kernels, partner_rows(): pl.pallas_call(functools.partial(partner_kernel, before=before), out_shap...  2.03 us
  transfers between devices with their start and end apart: 11, of which 3 were waited for; matrix products, arithmetic and copies ran while one was open for 0% of the time, Pallas kernels for 14%

profile of v3, /device:TPU:1, one launch (start us, length us, event | category | flops | bytes accessed | tf_op | source)
XLA Modules:
  0.0 47.4 jit_solution(17037884912143675930)
XLA Ops:
  0.0 3.9 %collective-permute-start.3 = (f32[96,1024]{1,0:T(8,128)}, f32[96,1024]{1,0:T(8,128)S(1)}, u32[]{:S(2)}, u32[]{:S(2)}) collective-permute-start(f32[96,1024]{1,0:T(8,128)} %bitcast.5), channel_id=1, source_target_pairs={{0,4},{1,5},{4,8},{5,9},{8,12},{9,13},{12,16},{13,17},{16,20},{17,... | collective-permute-start | bytes 1179656 | tf_op jit(solution)/shard_map/ppermute | solution.py:28
  3.9 1.3 %collective-permute-start.4 = (f32[96,1024]{1,0:T(8,128)}, f32[96,1024]{1,0:T(8,128)S(1)}, u32[]{:S(2)}, u32[]{:S(2)}) collective-permute-start(f32[96,1024]{1,0:T(8,128)} %bitcast.6), channel_id=1, source_target_pairs={{4,0},{5,1},{8,4},{9,5},{12,8},{13,9},{16,12},{17,13},{20,16},{21,... | collective-permute-start | bytes 1179656 | tf_op jit(solution)/shard_map/ppermute | solution.py:28
  5.2 7.5 %collective-permute-start.5 = (f32[96,1024]{1,0:T(8,128)}, f32[96,1024]{1,0:T(8,128)S(1)}, u32[]{:S(2)}, u32[]{:S(2)}) collective-permute-start(f32[96,1024]{1,0:T(8,128)} %bitcast.7), channel_id=1, source_target_pairs={{0,2},{1,3},{4,6},{5,7},{8,10},{9,11},{12,14},{13,15},{16,18},{17,... | collective-permute-start | bytes 1179656 | tf_op jit(solution)/shard_map/ppermute | solution.py:28
  12.7 0.7 %collective-permute-start.9 = (f32[96,1024]{1,0:T(8,128)}, f32[96,1024]{1,0:T(8,128)S(1)}, u32[]{:S(2)}, u32[]{:S(2)}) collective-permute-start(f32[96,1024]{1,0:T(8,128)} %bitcast.8), channel_id=1, source_target_pairs={{124,126},{125,127},{252,254},{253,255},{380,382},{381,383},{508,5... | collective-permute-start | bytes 1179656 | tf_op jit(solution)/shard_map/ppermute | solution.py:28
  13.4 4.8 %conditional.3 = (f32[96,1024]{1,0:T(8,128)}) conditional(s32[]{:T(128)} %convert_element_type.4, f32[96,1024]{1,0:T(8,128)} %bitcast.9, f32[96,1024]{1,0:T(8,128)} %bitcast.10), branch_computations={%region_2.3_spmd, %region_3.4_spmd} | conditional | bytes 1572912 | solution.py:269
  13.4 3.1 %collective-permute-start.2 = (f32[96,1024]{1,0:T(8,128)}, f32[96,1024]{1,0:T(8,128)}, u32[]{:S(2)}, u32[]{:S(2)}) collective-permute-start(f32[96,1024]{1,0:T(8,128)} %param.3), channel_id=1, source_target_pairs={{0,1},{1,0},{4,5},{5,4},{8,9},{9,8},{12,13},{13,12},{16,17},{17,16... | collective-permute-start | bytes 1179656 | tf_op jit(solution)/shard_map/cond/branch_1_fun/ppermute | solution.py:28
  16.6 1.7 %collective-permute-done.2 = f32[96,1024]{1,0:T(8,128)} collective-permute-done((f32[96,1024]{1,0:T(8,128)}, f32[96,1024]{1,0:T(8,128)}, u32[]{:S(2)}, u32[]{:S(2)}) %collective-permute-start.2) | collective-permute-done | bytes 393248 | tf_op jit(solution)/shard_map/cond/branch_1_fun/ppermute | solution.py:28
  18.3 0.0 copy-start
  18.3 7.4 %collective-permute-done.3.refs_0_ = f32[96,1024]{1,0:T(8,128)S(1)} collective-permute-done((f32[96,1024]{1,0:T(8,128)}, f32[96,1024]{1,0:T(8,128)S(1)}, u32[]{:S(2)}, u32[]{:S(2)}) %collective-permute-start.3) | collective-permute-done | bytes 393248 | tf_op jit(solution)/shard_map/ppermute | solution.py:28
  25.6 0.0 collective-permute-done.4.refs_4_
  25.6 6.9 %conditional.2 = (f32[96,1024]{1,0:T(8,128)}, f32[96,1024]{1,0:T(8,128)}) conditional(s32[]{:T(128)} %convert_element_type.4, (f32[96,1024]{1,0:T(8,128)S(1)}, f32[96,1024]{1,0:T(8,128)S(1)}) %tuple.18, (f32[96,1024]{1,0:T(8,128)S(1)}, f32[96,1024]{1,0:T(8,128)S(1)}) %tuple.18), branch_computations={%region_0.1_spmd, %region_1.2_spmd} | conditional | bytes 3145824 | solution.py:270
  25.6 3.1 %collective-permute-start = (f32[96,1024]{1,0:T(8,128)S(1)}, f32[96,1024]{1,0:T(8,128)}, u32[]{:S(2)}, u32[]{:S(2)}) collective-permute-start(f32[96,1024]{1,0:T(8,128)S(1)} %get-tuple-element.18), channel_id=1, source_target_pairs={{0,1},{1,0},{4,5},{5,4},{8,9},{9,8},{12,13},{13,12},{16,17},{17,16... | collective-permute-start | bytes 1179656 | tf_op jit(solution)/shard_map/cond/branch_1_fun/ppermute | solution.py:28
  28.8 1.9 %collective-permute-start.1 = (f32[96,1024]{1,0:T(8,128)S(1)}, f32[96,1024]{1,0:T(8,128)}, u32[]{:S(2)}, u32[]{:S(2)}) collective-permute-start(f32[96,1024]{1,0:T(8,128)S(1)} %get-tuple-element.19), channel_id=1, source_target_pairs={{0,1},{1,0},{4,5},{5,4},{8,9},{9,8},{12,13},{13,12},{16,17},{17,16... | collective-permute-start | bytes 1179656 | tf_op jit(solution)/shard_map/cond/branch_1_fun/ppermute | solution.py:28
  30.7 0.0 collective-permute-done
  30.7 1.8 %collective-permute-done.1 = f32[96,1024]{1,0:T(8,128)} collective-permute-done((f32[96,1024]{1,0:T(8,128)S(1)}, f32[96,1024]{1,0:T(8,128)}, u32[]{:S(2)}, u32[]{:S(2)}) %collective-permute-start.1) | collective-permute-done | bytes 393248 | tf_op jit(solution)/shard_map/cond/branch_1_fun/ppermute | solution.py:28
  32.5 0.0 copy-done
  32.5 2.1 %prepare.1 = (bf16[3,256,1024]{2,1,0:T(8,128)(2,1)S(1)}, bf16[3,256,1024]{2,1,0:T(8,128)(2,1)S(1)}, f32[8,256]{1,0:T(8,128)S(1)}) custom-call(s32[1]{0:T(128)} %bitcast.1.core_ref, f32[96,1024]{1,0:T(8,128)S(1)} %collective-permute-done.3.refs_0_, f32[96,1024]{1,0:T(8,128)} %get-tuple-element.27.refs_1_, f32[96,1024]{1,0:T(8,128)S(1)} %bitcast.11, ...), custom_call_target="tpu_custom_call" | custom-call | tf_op jit(solution)/shard_map/prepare/pallas_call | solution.py:206
  34.7 0.0 collective-permute-done.5.rows_ref
  34.7 2.0 %rows_of_partner.2.partner_ref = f32[48,128]{1,0:T(8,128)S(1)} custom-call(s32[1]{0:T(128)} %bitcast.chip_ref, f32[96,1024]{1,0:T(8,128)S(1)} %collective-permute-done.5.rows_ref, bf16[3,256,1024]{2,1,0:T(8,128)(2,1)S(1)} %get-tuple-element.29.high_ref, bf16[3,256,1024]{2,1,0:T(8,128)(2,1)S(1)} %get-tuple-element.30.low_ref, ...), custom_call_target="tpu_custom_call" | custom-call | tf_op jit(solution)/shard_map/rows_of_partner/pallas_call | solution.py:237
  36.7 4.4 %collective-permute-start.6 = (f32[48,128]{1,0:T(8,128)S(1)}, f32[48,128]{1,0:T(8,128)S(1)}, u32[]{:S(2)}, u32[]{:S(2)}) collective-permute-start(f32[48,128]{1,0:T(8,128)S(1)} %rows_of_partner.2.partner_ref), channel_id=1, source_target_pairs={{0,2},{1,3},{4,6},{5,7},{8,10},{9,11},{12,14},{13,15},{16,18},{17,... | collective-permute-start | bytes 73736 | tf_op jit(solution)/shard_map/ppermute | solution.py:28
  41.1 2.1 %rows_of_own.1 = (f32[32,384]{1,0:T(8,128)S(1)}, f32[32,128]{1,0:T(8,128)S(1)}) custom-call(s32[1]{0:T(128)} %bitcast.chip_ref, f32[96,1024]{1,0:T(8,128)S(1)} %bitcast.13, bf16[3,256,1024]{2,1,0:T(8,128)(2,1)S(1)} %get-tuple-element.29.high_ref, bf16[3,256,1024]{2,1,0:T(8,128)(2,1)S(1)} %get-tuple-element.30.low_ref, ...), custom_call_target="tpu_custom_call" | custom-call | tf_op jit(solution)/shard_map/rows_of_own/pallas_call | solution.py:225
  43.2 1.3 %collective-permute-start.7 = (f32[32,128]{1,0:T(8,128)S(1)}, f32[32,128]{1,0:T(8,128)S(1)}, u32[]{:S(2)}, u32[]{:S(2)}) collective-permute-start(f32[32,128]{1,0:T(8,128)S(1)} %get-tuple-element.33.refs_0_), channel_id=1, source_target_pairs={{0,510},{1,511},{128,124},{129,125},{256,252},{257,253},{384,380},... | collective-permute-start | bytes 49160 | tf_op jit(solution)/shard_map/ppermute | solution.py:28
  44.5 1.3 %collective-permute-start.8 = (f32[32,128]{1,0:T(8,128)S(1)}, f32[32,128]{1,0:T(8,128)S(1)}, u32[]{:S(2)}, u32[]{:S(2)}) collective-permute-start(f32[32,128]{1,0:T(8,128)S(1)} %get-tuple-element.33.refs_0_), channel_id=1, source_target_pairs={{0,511},{1,510},{128,125},{129,124},{256,253},{257,252},{384,381},... | collective-permute-start | bytes 49160 | tf_op jit(solution)/shard_map/ppermute | solution.py:28
  45.8 0.0 collective-permute-done.9.rows_ref
  45.9 0.7 %collective-permute-start.10 = (f32[32,128]{1,0:T(8,128)S(1)}, f32[32,128]{1,0:T(8,128)S(1)}, u32[]{:S(2)}, u32[]{:S(2)}) collective-permute-start(f32[32,128]{1,0:T(8,128)S(1)} %rows_of_partner.3), channel_id=1, source_target_pairs={{124,126},{125,127},{252,254},{253,255},{380,382},{381,383},{508,5... | collective-permute-start | bytes 49160 | tf_op jit(solution)/shard_map/ppermute | solution.py:28
  46.5 0.0 collective-permute-done.6.far_ref
  46.5 0.1 tiles.1.tiles_ref
  46.7 0.0 collective-permute-done.7.mine_ref
  46.7 0.0 collective-permute-done.8.other_ref
  46.7 0.0 collective-permute-done.10.far_ref
  46.7 0.6 %final.1 = f32[32,384]{1,0:T(8,128)} custom-call(s32[1]{0:T(128)} %bitcast.chip_ref, f32[32,384]{1,0:T(8,128)S(1)} %next_columns.1.tiles_ref, f32[32,128]{1,0:T(8,128)S(1)} %collective-permute-done.10.far_ref), custom_call_target="tpu_custom_call" | custom-call | tf_op jit(solution)/shard_map/final/pallas_call | solution.py:193
  (3 shorter events, 0.0 us)
Async XLA Ops:
  0.0 25.6 %collective-permute-start.3 = (f32[96,1024]{1,0:T(8,128)}, f32[96,1024]{1,0:T(8,128)S(1)}, u32[]{:S(2)}, u32[]{:S(2)}) collective-permute-start(f32[96,1024]{1,0:T(8,128)} %bitcast.5), channel_id=1, source_target_pairs={{0,4},{1,5},{4,8},{5,9},{8,12},{9,13},{12,16},{13,17},{16,20},{17,... | collective-permute-start | bytes 1179656 | tf_op jit(solution)/shard_map/ppermute | solution.py:28
  3.9 21.7 %collective-permute-start.4 = (f32[96,1024]{1,0:T(8,128)}, f32[96,1024]{1,0:T(8,128)S(1)}, u32[]{:S(2)}, u32[]{:S(2)}) collective-permute-start(f32[96,1024]{1,0:T(8,128)} %bitcast.6), channel_id=1, source_target_pairs={{4,0},{5,1},{8,4},{9,5},{12,8},{13,9},{16,12},{17,13},{20,16},{21,... | collective-permute-start | bytes 1179656 | tf_op jit(solution)/shard_map/ppermute | solution.py:28
  5.2 29.4 %collective-permute-start.5 = (f32[96,1024]{1,0:T(8,128)}, f32[96,1024]{1,0:T(8,128)S(1)}, u32[]{:S(2)}, u32[]{:S(2)}) collective-permute-start(f32[96,1024]{1,0:T(8,128)} %bitcast.7), channel_id=1, source_target_pairs={{0,2},{1,3},{4,6},{5,7},{8,10},{9,11},{12,14},{13,15},{16,18},{17,... | collective-permute-start | bytes 1179656 | tf_op jit(solution)/shard_map/ppermute | solution.py:28
  12.7 33.1 %collective-permute-start.9 = (f32[96,1024]{1,0:T(8,128)}, f32[96,1024]{1,0:T(8,128)S(1)}, u32[]{:S(2)}, u32[]{:S(2)}) collective-permute-start(f32[96,1024]{1,0:T(8,128)} %bitcast.8), channel_id=1, source_target_pairs={{124,126},{125,127},{252,254},{253,255},{380,382},{381,383},{508,5... | collective-permute-start | bytes 1179656 | tf_op jit(solution)/shard_map/ppermute | solution.py:28
  13.4 4.8 %collective-permute-start.2 = (f32[96,1024]{1,0:T(8,128)}, f32[96,1024]{1,0:T(8,128)}, u32[]{:S(2)}, u32[]{:S(2)}) collective-permute-start(f32[96,1024]{1,0:T(8,128)} %param.3), channel_id=1, source_target_pairs={{0,1},{1,0},{4,5},{5,4},{8,9},{9,8},{12,13},{13,12},{16,17},{17,16... | collective-permute-start | bytes 1179656 | tf_op jit(solution)/shard_map/cond/branch_1_fun/ppermute | solution.py:28
  18.3 14.3 %copy-start = (f32[32,3,1024]{2,0,1:T(8,128)S(1)}, f32[32,3,1024]{2,0,1:T(8,128)}, u32[]{:S(2)}) copy-start(f32[32,3,1024]{2,0,1:T(8,128)} %param.5) | copy-start | bytes 1179652
  25.6 5.1 %collective-permute-start = (f32[96,1024]{1,0:T(8,128)S(1)}, f32[96,1024]{1,0:T(8,128)}, u32[]{:S(2)}, u32[]{:S(2)}) collective-permute-start(f32[96,1024]{1,0:T(8,128)S(1)} %get-tuple-element.18), channel_id=1, source_target_pairs={{0,1},{1,0},{4,5},{5,4},{8,9},{9,8},{12,13},{13,12},{16,17},{17,16... | collective-permute-start | bytes 1179656 | tf_op jit(solution)/shard_map/cond/branch_1_fun/ppermute | solution.py:28
  28.8 3.7 %collective-permute-start.1 = (f32[96,1024]{1,0:T(8,128)S(1)}, f32[96,1024]{1,0:T(8,128)}, u32[]{:S(2)}, u32[]{:S(2)}) collective-permute-start(f32[96,1024]{1,0:T(8,128)S(1)} %get-tuple-element.19), channel_id=1, source_target_pairs={{0,1},{1,0},{4,5},{5,4},{8,9},{9,8},{12,13},{13,12},{16,17},{17,16... | collective-permute-start | bytes 1179656 | tf_op jit(solution)/shard_map/cond/branch_1_fun/ppermute | solution.py:28
  36.7 9.8 %collective-permute-start.6 = (f32[48,128]{1,0:T(8,128)S(1)}, f32[48,128]{1,0:T(8,128)S(1)}, u32[]{:S(2)}, u32[]{:S(2)}) collective-permute-start(f32[48,128]{1,0:T(8,128)S(1)} %rows_of_partner.2.partner_ref), channel_id=1, source_target_pairs={{0,2},{1,3},{4,6},{5,7},{8,10},{9,11},{12,14},{13,15},{16,18},{17,... | collective-permute-start | bytes 73736 | tf_op jit(solution)/shard_map/ppermute | solution.py:28
  43.2 3.5 %collective-permute-start.7 = (f32[32,128]{1,0:T(8,128)S(1)}, f32[32,128]{1,0:T(8,128)S(1)}, u32[]{:S(2)}, u32[]{:S(2)}) collective-permute-start(f32[32,128]{1,0:T(8,128)S(1)} %get-tuple-element.33.refs_0_), channel_id=1, source_target_pairs={{0,510},{1,511},{128,124},{129,125},{256,252},{257,253},{384,380},... | collective-permute-start | bytes 49160 | tf_op jit(solution)/shard_map/ppermute | solution.py:28
  44.5 2.2 %collective-permute-start.8 = (f32[32,128]{1,0:T(8,128)S(1)}, f32[32,128]{1,0:T(8,128)S(1)}, u32[]{:S(2)}, u32[]{:S(2)}) collective-permute-start(f32[32,128]{1,0:T(8,128)S(1)} %get-tuple-element.33.refs_0_), channel_id=1, source_target_pairs={{0,511},{1,510},{128,125},{129,124},{256,253},{257,252},{384,381},... | collective-permute-start | bytes 49160 | tf_op jit(solution)/shard_map/ppermute | solution.py:28
  45.9 0.9 %collective-permute-start.10 = (f32[32,128]{1,0:T(8,128)S(1)}, f32[32,128]{1,0:T(8,128)S(1)}, u32[]{:S(2)}, u32[]{:S(2)}) collective-permute-start(f32[32,128]{1,0:T(8,128)S(1)} %rows_of_partner.3), channel_id=1, source_target_pairs={{124,126},{125,127},{252,254},{253,255},{380,382},{381,383},{508,5... | collective-permute-start | bytes 49160 | tf_op jit(solution)/shard_map/ppermute | solution.py:28

commit v4 on v3

--- a/solution.py
+++ b/solution.py
@@ -28,6 +28,11 @@
     return lax.ppermute(value, AXES, pairs)
 
 
+def stepped(value, steps):
+    pairs = [(device_of(chip, core), device_of(chip + step, core)) for chip, step in steps for core in range(2)]
+    return lax.ppermute(value, AXES, pairs)
+
+
 def centred_of(raw):
     return raw - jnp.sum(raw, axis=1, keepdims=True) * (1.0 / ATOMS)
 
@@ -38,13 +43,14 @@
     return high, low
 
 
-def prepare_kernel(core_ref, *refs):
+def prepare_kernel(chip_ref, core_ref, *refs):
     frames, (high_ref, low_ref, norm_ref, column_ref) = refs[:6], refs[6:]
-    core = core_ref[0]
+    core, odd = core_ref[0], chip_ref[0] % 2
     column_ref[...] = jnp.zeros_like(column_ref)
     for n, ref in enumerate(frames):
         at = core if n % 2 == 0 else 1 - core
-        start = pl.multiple_of(64 * (n // 2) + 32 * at, 32)
+        group = (2 * odd, 1, 2 - 2 * odd)[n // 2]
+        start = pl.multiple_of(64 * group + 32 * at, 32)
         norm = jnp.zeros((32, 1), jnp.float32)
         for b in range(3):
             centred = centred_of(ref[32 * b : 32 * b + 32, :])
@@ -200,18 +206,18 @@
     )(*scalars, *arrays)
 
 
-def prepare(core, *frames):
+def prepare(chip, core, *frames):
     spec = pl.BlockSpec(memory_space=pltpu.VMEM)
     wide = jax.ShapeDtypeStruct((3, 256, ATOMS), jnp.bfloat16)
     return pl.pallas_call(
         prepare_kernel,
         out_shape=(wide, wide, jax.ShapeDtypeStruct((8, 256), jnp.float32)),
-        in_specs=[pl.BlockSpec(memory_space=pltpu.SMEM)] + [spec] * 6,
+        in_specs=[pl.BlockSpec(memory_space=pltpu.SMEM)] * 2 + [spec] * 6,
         out_specs=(spec, spec, spec),
         scratch_shapes=[pltpu.VMEM((256, 128), jnp.float32)],
         compiler_params=pltpu.CompilerParams(vmem_limit_bytes=24 << 20),
         name="prepare",
-    )(core, *frames)
+    )(chip, core, *frames)
 
 
 SPEC = pl.BlockSpec(memory_space=pltpu.VMEM)
@@ -258,18 +264,20 @@
     half = CHIPS // 2
     raw = frames.transpose(1, 0, 2).reshape(96, ATOMS)
 
-    prv = moved(raw, 1, 0)
-    nxt = moved(raw, -1, 0, not_after)
+    first = [(c, 1 if c % 2 else -1) for c in chips if c % PLANE]
+    second = [(c, -1 if c % 2 else 1) for c in chips]
+    one = stepped(raw, first)
+    two = stepped(raw, second)
     far = moved(raw, half, 0, not_before)
     far_before = moved(raw, half, 0, befores)
 
-    def swap_near(prv, nxt):
-        return moved(prv, 0, 1), moved(nxt, 0, 1, not_before)
+    def swap_near(one, two):
+        return moved(one, 0, 1, not_before), moved(two, 0, 1)
 
     raw_other, then = lax.cond(always, lambda raw: (moved(raw, 0, 1), chip), lambda raw: (raw, chip), raw)
-    prv_other, nxt_other = lax.cond(then < CHIPS, swap_near, lambda prv, nxt: (prv, nxt), prv, nxt)
+    one_other, two_other = lax.cond(then < CHIPS, swap_near, lambda one, two: (one, two), one, two)
     place = tuple(value.reshape(1).astype(jnp.int32) for value in (chip, core))
-    columns = prepare(place[1], prv, prv_other, raw, raw_other, nxt, nxt_other)
+    columns = prepare(*place, one, one_other, raw, raw_other, two, two_other)
     early = own_rows(place[0], raw, *columns)
     for_partner = partner_rows(place[0], False, far, *columns, early)
     returned = moved(for_partner, half, 0, not_before)

time: 47.7 us -> 47.1 us (0.987)
  waiting for transfers between devices: 10.9 us -> 8.13 us
  starting transfers between devices: 29.2 us -> 31.3 us
    ppermute x11 -> x9, waiting for transfers between devices: 10.9 us -> 3.51 us  [moved(): return lax.ppermute(value, AXES, pairs)]
    ppermute x0 -> x2, starting transfers between devices: none -> 7.06 us  [stepped(): return lax.ppermute(value, AXES, pairs)]
    ppermute x11 -> x9, starting transfers between devices: 29.2 us -> 24.3 us  [moved(): return lax.ppermute(value, AXES, pairs)]
    ppermute x0 -> x2, waiting for transfers between devices: none -> 4.63 us  [stepped(): return lax.ppermute(value, AXES, pairs)]
where the time goes in v4:
time: 47.1 us; the launch traced here: 46.8 us
  starting transfers between devices  31.3 us (66%)
  waiting for transfers between devices  8.13 us (17%)
  Pallas kernels  7.09 us (15%)
    ppermute x9, starting transfers between devices, moved(): return lax.ppermute(value, AXES, pairs)  24.3 us
    ppermute x2, starting transfers between devices, stepped(): return lax.ppermute(value, AXES, pairs)  7.06 us
    ppermute x2, waiting for transfers between devices, stepped(): return lax.ppermute(value, AXES, pairs)  4.63 us
    ppermute x9, waiting for transfers between devices, moved(): return lax.ppermute(value, AXES, pairs)  3.51 us
    pallas_call x1, Pallas kernels, prepare(): pl.pallas_call(prepare_kernel, out_shape=(wide, wide, jax.ShapeDtypeStruc...  2.16 us
    pallas_call x2, Pallas kernels, own_rows(): pl.pallas_call(own_kernel if more else early_kernel, out_shape=(TILES, ME...  2.11 us
    pallas_call x2, Pallas kernels, partner_rows(): pl.pallas_call(functools.partial(partner_kernel, before=before), out_shap...  2.03 us
  transfers between devices with their start and end apart: 11, of which 3 were waited for; matrix products, arithmetic and copies ran while one was open for 0% of the time, Pallas kernels for 14%

profile of v4, /device:TPU:1, one launch (start us, length us, event | category | flops | bytes accessed | tf_op | source)
XLA Modules:
  0.0 46.8 jit_solution(7956800157552147669)
XLA Ops:
  0.0 1.3 %collective-permute-start.3 = (f32[96,1024]{1,0:T(8,128)}, f32[96,1024]{1,0:T(8,128)S(1)}, u32[]{:S(2)}, u32[]{:S(2)}) collective-permute-start(f32[96,1024]{1,0:T(8,128)} %bitcast.5), channel_id=1, source_target_pairs={{4,8},{5,9},{8,4},{9,5},{12,16},{13,17},{16,12},{17,13},{20,24},{2... | collective-permute-start | bytes 1179656 | tf_op jit(solution)/shard_map/ppermute | solution.py:33
  1.3 5.8 %collective-permute-start.4 = (f32[96,1024]{1,0:T(8,128)}, f32[96,1024]{1,0:T(8,128)S(1)}, u32[]{:S(2)}, u32[]{:S(2)}) collective-permute-start(f32[96,1024]{1,0:T(8,128)} %bitcast.6), channel_id=1, source_target_pairs={{0,4},{1,5},{4,0},{5,1},{8,12},{9,13},{12,8},{13,9},{16,20},{17,21... | collective-permute-start | bytes 1179656 | tf_op jit(solution)/shard_map/ppermute | solution.py:33
  7.1 7.5 %collective-permute-start.5 = (f32[96,1024]{1,0:T(8,128)}, f32[96,1024]{1,0:T(8,128)S(1)}, u32[]{:S(2)}, u32[]{:S(2)}) collective-permute-start(f32[96,1024]{1,0:T(8,128)} %bitcast.7), channel_id=1, source_target_pairs={{0,2},{1,3},{4,6},{5,7},{8,10},{9,11},{12,14},{13,15},{16,18},{17,... | collective-permute-start | bytes 1179656 | tf_op jit(solution)/shard_map/ppermute | solution.py:28
  14.5 0.7 %collective-permute-start.9 = (f32[96,1024]{1,0:T(8,128)}, f32[96,1024]{1,0:T(8,128)S(1)}, u32[]{:S(2)}, u32[]{:S(2)}) collective-permute-start(f32[96,1024]{1,0:T(8,128)} %bitcast.8), channel_id=1, source_target_pairs={{124,126},{125,127},{252,254},{253,255},{380,382},{381,383},{508,5... | collective-permute-start | bytes 1179656 | tf_op jit(solution)/shard_map/ppermute | solution.py:28
  15.3 5.1 %conditional.3 = (f32[96,1024]{1,0:T(8,128)}) conditional(s32[]{:T(128)} %convert_element_type.4, f32[96,1024]{1,0:T(8,128)} %bitcast.9, f32[96,1024]{1,0:T(8,128)} %bitcast.10), branch_computations={%region_2.3_spmd, %region_3.4_spmd} | conditional | bytes 1572912 | solution.py:277
  15.3 3.4 %collective-permute-start.2 = (f32[96,1024]{1,0:T(8,128)}, f32[96,1024]{1,0:T(8,128)}, u32[]{:S(2)}, u32[]{:S(2)}) collective-permute-start(f32[96,1024]{1,0:T(8,128)} %param.3), channel_id=1, source_target_pairs={{0,1},{1,0},{4,5},{5,4},{8,9},{9,8},{12,13},{13,12},{16,17},{17,16... | collective-permute-start | bytes 1179656 | tf_op jit(solution)/shard_map/cond/branch_1_fun/ppermute | solution.py:28
  18.7 1.7 %collective-permute-done.2 = f32[96,1024]{1,0:T(8,128)} collective-permute-done((f32[96,1024]{1,0:T(8,128)}, f32[96,1024]{1,0:T(8,128)}, u32[]{:S(2)}, u32[]{:S(2)}) %collective-permute-start.2) | collective-permute-done | bytes 393248 | tf_op jit(solution)/shard_map/cond/branch_1_fun/ppermute | solution.py:28
  20.4 0.0 copy-start
  20.4 4.6 %collective-permute-done.3.refs_0_ = f32[96,1024]{1,0:T(8,128)S(1)} collective-permute-done((f32[96,1024]{1,0:T(8,128)}, f32[96,1024]{1,0:T(8,128)S(1)}, u32[]{:S(2)}, u32[]{:S(2)}) %collective-permute-start.3) | collective-permute-done | bytes 393248 | tf_op jit(solution)/shard_map/ppermute | solution.py:33
  25.0 0.0 collective-permute-done.4.refs_4_
  25.0 6.9 %conditional.2 = (f32[96,1024]{1,0:T(8,128)}, f32[96,1024]{1,0:T(8,128)}) conditional(s32[]{:T(128)} %convert_element_type.4, (f32[96,1024]{1,0:T(8,128)S(1)}, f32[96,1024]{1,0:T(8,128)S(1)}) %tuple.18, (f32[96,1024]{1,0:T(8,128)S(1)}, f32[96,1024]{1,0:T(8,128)S(1)}) %tuple.18), branch_computations={%region_0.1_spmd, %region_1.2_spmd} | conditional | bytes 3145824 | solution.py:278
  25.0 3.2 %collective-permute-start = (f32[96,1024]{1,0:T(8,128)S(1)}, f32[96,1024]{1,0:T(8,128)}, u32[]{:S(2)}, u32[]{:S(2)}) collective-permute-start(f32[96,1024]{1,0:T(8,128)S(1)} %get-tuple-element.18), channel_id=1, source_target_pairs={{0,1},{1,0},{4,5},{5,4},{8,9},{9,8},{12,13},{13,12},{16,17},{17,16... | collective-permute-start | bytes 1179656 | tf_op jit(solution)/shard_map/cond/branch_1_fun/ppermute | solution.py:28
  28.2 1.9 %collective-permute-start.1 = (f32[96,1024]{1,0:T(8,128)S(1)}, f32[96,1024]{1,0:T(8,128)}, u32[]{:S(2)}, u32[]{:S(2)}) collective-permute-start(f32[96,1024]{1,0:T(8,128)S(1)} %get-tuple-element.19), channel_id=1, source_target_pairs={{0,1},{1,0},{4,5},{5,4},{8,9},{9,8},{12,13},{13,12},{16,17},{17,16... | collective-permute-start | bytes 1179656 | tf_op jit(solution)/shard_map/cond/branch_1_fun/ppermute | solution.py:28
  30.1 0.0 collective-permute-done
  30.1 1.8 %collective-permute-done.1 = f32[96,1024]{1,0:T(8,128)} collective-permute-done((f32[96,1024]{1,0:T(8,128)S(1)}, f32[96,1024]{1,0:T(8,128)}, u32[]{:S(2)}, u32[]{:S(2)}) %collective-permute-start.1) | collective-permute-done | bytes 393248 | tf_op jit(solution)/shard_map/cond/branch_1_fun/ppermute | solution.py:28
  31.9 0.0 copy-done
  31.9 2.2 %prepare.1 = (bf16[3,256,1024]{2,1,0:T(8,128)(2,1)S(1)}, bf16[3,256,1024]{2,1,0:T(8,128)(2,1)S(1)}, f32[8,256]{1,0:T(8,128)S(1)}) custom-call(s32[1]{0:T(128)} %bitcast.chip_ref, s32[1]{0:T(128)} %bitcast.1.core_ref, f32[96,1024]{1,0:T(8,128)S(1)} %collective-permute-done.3.refs_0_, f32[96,1024]{1,0:T(8,128)} %get-tuple-element.27.refs_1_, ...), custom_call_target="tpu_custom_call" | custom-call | tf_op jit(solution)/shard_map/prepare/pallas_call | solution.py:212
  34.1 0.0 collective-permute-done.5.rows_ref
  34.1 2.0 %rows_of_partner.2.partner_ref = f32[48,128]{1,0:T(8,128)S(1)} custom-call(s32[1]{0:T(128)} %bitcast.chip_ref, f32[96,1024]{1,0:T(8,128)S(1)} %collective-permute-done.5.rows_ref, bf16[3,256,1024]{2,1,0:T(8,128)(2,1)S(1)} %get-tuple-element.29.high_ref, bf16[3,256,1024]{2,1,0:T(8,128)(2,1)S(1)} %get-tuple-element.30.low_ref, ...), custom_call_target="tpu_custom_call" | custom-call | tf_op jit(solution)/shard_map/rows_of_partner/pallas_call | solution.py:243
  36.1 4.4 %collective-permute-start.6 = (f32[48,128]{1,0:T(8,128)S(1)}, f32[48,128]{1,0:T(8,128)S(1)}, u32[]{:S(2)}, u32[]{:S(2)}) collective-permute-start(f32[48,128]{1,0:T(8,128)S(1)} %rows_of_partner.2.partner_ref), channel_id=1, source_target_pairs={{0,2},{1,3},{4,6},{5,7},{8,10},{9,11},{12,14},{13,15},{16,18},{17,... | collective-permute-start | bytes 73736 | tf_op jit(solution)/shard_map/ppermute | solution.py:28
  40.5 2.1 %rows_of_own.1 = (f32[32,384]{1,0:T(8,128)S(1)}, f32[32,128]{1,0:T(8,128)S(1)}) custom-call(s32[1]{0:T(128)} %bitcast.chip_ref, f32[96,1024]{1,0:T(8,128)S(1)} %bitcast.13, bf16[3,256,1024]{2,1,0:T(8,128)(2,1)S(1)} %get-tuple-element.29.high_ref, bf16[3,256,1024]{2,1,0:T(8,128)(2,1)S(1)} %get-tuple-element.30.low_ref, ...), custom_call_target="tpu_custom_call" | custom-call | tf_op jit(solution)/shard_map/rows_of_own/pallas_call | solution.py:231
  42.6 1.3 %collective-permute-start.7 = (f32[32,128]{1,0:T(8,128)S(1)}, f32[32,128]{1,0:T(8,128)S(1)}, u32[]{:S(2)}, u32[]{:S(2)}) collective-permute-start(f32[32,128]{1,0:T(8,128)S(1)} %get-tuple-element.33.refs_0_), channel_id=1, source_target_pairs={{0,510},{1,511},{128,124},{129,125},{256,252},{257,253},{384,380},... | collective-permute-start | bytes 49160 | tf_op jit(solution)/shard_map/ppermute | solution.py:28
  43.9 1.3 %collective-permute-start.8 = (f32[32,128]{1,0:T(8,128)S(1)}, f32[32,128]{1,0:T(8,128)S(1)}, u32[]{:S(2)}, u32[]{:S(2)}) collective-permute-start(f32[32,128]{1,0:T(8,128)S(1)} %get-tuple-element.33.refs_0_), channel_id=1, source_target_pairs={{0,511},{1,510},{128,125},{129,124},{256,253},{257,252},{384,381},... | collective-permute-start | bytes 49160 | tf_op jit(solution)/shard_map/ppermute | solution.py:28
  45.2 0.0 collective-permute-done.9.rows_ref
  45.3 0.7 %collective-permute-start.10 = (f32[32,128]{1,0:T(8,128)S(1)}, f32[32,128]{1,0:T(8,128)S(1)}, u32[]{:S(2)}, u32[]{:S(2)}) collective-permute-start(f32[32,128]{1,0:T(8,128)S(1)} %rows_of_partner.3), channel_id=1, source_target_pairs={{124,126},{125,127},{252,254},{253,255},{380,382},{381,383},{508,5... | collective-permute-start | bytes 49160 | tf_op jit(solution)/shard_map/ppermute | solution.py:28
  45.9 0.0 collective-permute-done.6.far_ref
  45.9 0.1 tiles.1.tiles_ref
  46.1 0.0 collective-permute-done.7.mine_ref
  46.1 0.0 collective-permute-done.8.other_ref
  46.1 0.0 collective-permute-done.10.far_ref
  46.1 0.6 %final.1 = f32[32,384]{1,0:T(8,128)} custom-call(s32[1]{0:T(128)} %bitcast.chip_ref, f32[32,384]{1,0:T(8,128)S(1)} %next_columns.1.tiles_ref, f32[32,128]{1,0:T(8,128)S(1)} %collective-permute-done.10.far_ref), custom_call_target="tpu_custom_call" | custom-call | tf_op jit(solution)/shard_map/final/pallas_call | solution.py:199
  (3 shorter events, 0.0 us)
Async XLA Ops:
  0.0 25.0 %collective-permute-start.3 = (f32[96,1024]{1,0:T(8,128)}, f32[96,1024]{1,0:T(8,128)S(1)}, u32[]{:S(2)}, u32[]{:S(2)}) collective-permute-start(f32[96,1024]{1,0:T(8,128)} %bitcast.5), channel_id=1, source_target_pairs={{4,8},{5,9},{8,4},{9,5},{12,16},{13,17},{16,12},{17,13},{20,24},{2... | collective-permute-start | bytes 1179656 | tf_op jit(solution)/shard_map/ppermute | solution.py:33
  1.3 23.7 %collective-permute-start.4 = (f32[96,1024]{1,0:T(8,128)}, f32[96,1024]{1,0:T(8,128)S(1)}, u32[]{:S(2)}, u32[]{:S(2)}) collective-permute-start(f32[96,1024]{1,0:T(8,128)} %bitcast.6), channel_id=1, source_target_pairs={{0,4},{1,5},{4,0},{5,1},{8,12},{9,13},{12,8},{13,9},{16,20},{17,21... | collective-permute-start | bytes 1179656 | tf_op jit(solution)/shard_map/ppermute | solution.py:33
  7.1 27.0 %collective-permute-start.5 = (f32[96,1024]{1,0:T(8,128)}, f32[96,1024]{1,0:T(8,128)S(1)}, u32[]{:S(2)}, u32[]{:S(2)}) collective-permute-start(f32[96,1024]{1,0:T(8,128)} %bitcast.7), channel_id=1, source_target_pairs={{0,2},{1,3},{4,6},{5,7},{8,10},{9,11},{12,14},{13,15},{16,18},{17,... | collective-permute-start | bytes 1179656 | tf_op jit(solution)/shard_map/ppermute | solution.py:28
  14.5 30.7 %collective-permute-start.9 = (f32[96,1024]{1,0:T(8,128)}, f32[96,1024]{1,0:T(8,128)S(1)}, u32[]{:S(2)}, u32[]{:S(2)}) collective-permute-start(f32[96,1024]{1,0:T(8,128)} %bitcast.8), channel_id=1, source_target_pairs={{124,126},{125,127},{252,254},{253,255},{380,382},{381,383},{508,5... | collective-permute-start | bytes 1179656 | tf_op jit(solution)/shard_map/ppermute | solution.py:28
  15.3 5.1 %collective-permute-start.2 = (f32[96,1024]{1,0:T(8,128)}, f32[96,1024]{1,0:T(8,128)}, u32[]{:S(2)}, u32[]{:S(2)}) collective-permute-start(f32[96,1024]{1,0:T(8,128)} %param.3), channel_id=1, source_target_pairs={{0,1},{1,0},{4,5},{5,4},{8,9},{9,8},{12,13},{13,12},{16,17},{17,16... | collective-permute-start | bytes 1179656 | tf_op jit(solution)/shard_map/cond/branch_1_fun/ppermute | solution.py:28
  20.4 11.6 %copy-start = (f32[32,3,1024]{2,0,1:T(8,128)S(1)}, f32[32,3,1024]{2,0,1:T(8,128)}, u32[]{:S(2)}) copy-start(f32[32,3,1024]{2,0,1:T(8,128)} %param.5) | copy-start | bytes 1179652
  25.0 5.1 %collective-permute-start = (f32[96,1024]{1,0:T(8,128)S(1)}, f32[96,1024]{1,0:T(8,128)}, u32[]{:S(2)}, u32[]{:S(2)}) collective-permute-start(f32[96,1024]{1,0:T(8,128)S(1)} %get-tuple-element.18), channel_id=1, source_target_pairs={{0,1},{1,0},{4,5},{5,4},{8,9},{9,8},{12,13},{13,12},{16,17},{17,16... | collective-permute-start | bytes 1179656 | tf_op jit(solution)/shard_map/cond/branch_1_fun/ppermute | solution.py:28
  28.2 3.7 %collective-permute-start.1 = (f32[96,1024]{1,0:T(8,128)S(1)}, f32[96,1024]{1,0:T(8,128)}, u32[]{:S(2)}, u32[]{:S(2)}) collective-permute-start(f32[96,1024]{1,0:T(8,128)S(1)} %get-tuple-element.19), channel_id=1, source_target_pairs={{0,1},{1,0},{4,5},{5,4},{8,9},{9,8},{12,13},{13,12},{16,17},{17,16... | collective-permute-start | bytes 1179656 | tf_op jit(solution)/shard_map/cond/branch_1_fun/ppermute | solution.py:28
  36.1 9.8 %collective-permute-start.6 = (f32[48,128]{1,0:T(8,128)S(1)}, f32[48,128]{1,0:T(8,128)S(1)}, u32[]{:S(2)}, u32[]{:S(2)}) collective-permute-start(f32[48,128]{1,0:T(8,128)S(1)} %rows_of_partner.2.partner_ref), channel_id=1, source_target_pairs={{0,2},{1,3},{4,6},{5,7},{8,10},{9,11},{12,14},{13,15},{16,18},{17,... | collective-permute-start | bytes 73736 | tf_op jit(solution)/shard_map/ppermute | solution.py:28
  42.6 3.5 %collective-permute-start.7 = (f32[32,128]{1,0:T(8,128)S(1)}, f32[32,128]{1,0:T(8,128)S(1)}, u32[]{:S(2)}, u32[]{:S(2)}) collective-permute-start(f32[32,128]{1,0:T(8,128)S(1)} %get-tuple-element.33.refs_0_), channel_id=1, source_target_pairs={{0,510},{1,511},{128,124},{129,125},{256,252},{257,253},{384,380},... | collective-permute-start | bytes 49160 | tf_op jit(solution)/shard_map/ppermute | solution.py:28
  43.9 2.2 %collective-permute-start.8 = (f32[32,128]{1,0:T(8,128)S(1)}, f32[32,128]{1,0:T(8,128)S(1)}, u32[]{:S(2)}, u32[]{:S(2)}) collective-permute-start(f32[32,128]{1,0:T(8,128)S(1)} %get-tuple-element.33.refs_0_), channel_id=1, source_target_pairs={{0,511},{1,510},{128,125},{129,124},{256,253},{257,252},{384,381},... | collective-permute-start | bytes 49160 | tf_op jit(solution)/shard_map/ppermute | solution.py:28
  45.3 0.9 %collective-permute-start.10 = (f32[32,128]{1,0:T(8,128)S(1)}, f32[32,128]{1,0:T(8,128)S(1)}, u32[]{:S(2)}, u32[]{:S(2)}) collective-permute-start(f32[32,128]{1,0:T(8,128)S(1)} %rows_of_partner.3), channel_id=1, source_target_pairs={{124,126},{125,127},{252,254},{253,255},{380,382},{381,383},{508,5... | collective-permute-start | bytes 49160 | tf_op jit(solution)/shard_map/ppermute | solution.py:28

commit v5 on v4

--- a/solution.py
+++ b/solution.py
@@ -271,11 +271,14 @@
     far = moved(raw, half, 0, not_before)
     far_before = moved(raw, half, 0, befores)
 
-    def swap_near(one, two):
-        return moved(one, 0, 1, not_before), moved(two, 0, 1)
-
-    raw_other, then = lax.cond(always, lambda raw: (moved(raw, 0, 1), chip), lambda raw: (raw, chip), raw)
-    one_other, two_other = lax.cond(then < CHIPS, swap_near, lambda one, two: (one, two), one, two)
+    def swap_near(one, two, scale):
+        return moved(one, 0, 1, not_before) * scale, moved(two, 0, 1) * scale
+
+    scale = always.astype(jnp.float32)
+    raw_other, then = lax.cond(
+        always, lambda raw, scale: (moved(raw, 0, 1) * scale, chip), lambda raw, _: (raw, chip), raw, scale
+    )
+    one_other, two_other = lax.cond(then < CHIPS, swap_near, lambda one, two, _: (one, two), one, two, scale)
     place = tuple(value.reshape(1).astype(jnp.int32) for value in (chip, core))
     columns = prepare(*place, one, one_other, raw, raw_other, two, two_other)
     early = own_rows(place[0], raw, *columns)

time: 47.1 us -> 46.3 us (0.983)
  Pallas kernels: 7.09 us -> 5.85 us
    pallas_call x1, Pallas kernels: 2.16 us -> 0.92 us  [prepare(): pl.pallas_call(prepare_kernel, out_shape=(wide, wide, jax.ShapeDtypeStruc...]
  transfers between devices with their start and end apart: 11 -> 11, of which waited for: 3 -> 3; matrix products, arithmetic and copies ran while one was open for 0% -> 0% of each run, Pallas kernels for 14% -> 11%
where the time goes in v5:
time: 46.3 us; the launch traced here: 45.5 us
  starting transfers between devices  31.5 us (68%)
  waiting for transfers between devices  7.92 us (17%)
  Pallas kernels  5.85 us (13%)
    ppermute x9, starting transfers between devices, moved(): return lax.ppermute(value, AXES, pairs)  24.4 us
    ppermute x2, starting transfers between devices, stepped(): return lax.ppermute(value, AXES, pairs)  7.06 us
    ppermute x2, waiting for transfers between devices, stepped(): return lax.ppermute(value, AXES, pairs)  4.72 us
    ppermute x9, waiting for transfers between devices, moved(): return lax.ppermute(value, AXES, pairs)  3.2 us
    pallas_call x2, Pallas kernels, own_rows(): pl.pallas_call(own_kernel if more else early_kernel, out_shape=(TILES, ME...  2.1 us
    pallas_call x2, Pallas kernels, partner_rows(): pl.pallas_call(functools.partial(partner_kernel, before=before), out_shap...  2.03 us
  transfers between devices with their start and end apart: 11, of which 3 were waited for; matrix products, arithmetic and copies ran while one was open for 0% of the time, Pallas kernels for 11%

profile of v5, /device:TPU:1, one launch (start us, length us, event | category | flops | bytes accessed | tf_op | source)
XLA Modules:
  0.0 45.5 jit_solution(14339339454791979911)
XLA Ops:
  0.0 1.3 %collective-permute-start.3 = (f32[96,1024]{1,0:T(8,128)}, f32[96,1024]{1,0:T(8,128)S(1)}, u32[]{:S(2)}, u32[]{:S(2)}) collective-permute-start(f32[96,1024]{1,0:T(8,128)} %bitcast.5), channel_id=1, source_target_pairs={{4,8},{5,9},{8,4},{9,5},{12,16},{13,17},{16,12},{17,13},{20,24},{2... | collective-permute-start | bytes 1179656 | tf_op jit(solution)/shard_map/ppermute | solution.py:33
  1.3 5.8 %collective-permute-start.4 = (f32[96,1024]{1,0:T(8,128)}, f32[96,1024]{1,0:T(8,128)S(1)}, u32[]{:S(2)}, u32[]{:S(2)}) collective-permute-start(f32[96,1024]{1,0:T(8,128)} %bitcast.6), channel_id=1, source_target_pairs={{0,4},{1,5},{4,0},{5,1},{8,12},{9,13},{12,8},{13,9},{16,20},{17,21... | collective-permute-start | bytes 1179656 | tf_op jit(solution)/shard_map/ppermute | solution.py:33
  7.1 7.5 %collective-permute-start.5 = (f32[96,1024]{1,0:T(8,128)}, f32[96,1024]{1,0:T(8,128)S(1)}, u32[]{:S(2)}, u32[]{:S(2)}) collective-permute-start(f32[96,1024]{1,0:T(8,128)} %bitcast.7), channel_id=1, source_target_pairs={{0,2},{1,3},{4,6},{5,7},{8,10},{9,11},{12,14},{13,15},{16,18},{17,... | collective-permute-start | bytes 1179656 | tf_op jit(solution)/shard_map/ppermute | solution.py:28
  14.5 0.7 %collective-permute-start.9 = (f32[96,1024]{1,0:T(8,128)}, f32[96,1024]{1,0:T(8,128)S(1)}, u32[]{:S(2)}, u32[]{:S(2)}) collective-permute-start(f32[96,1024]{1,0:T(8,128)} %bitcast.8), channel_id=1, source_target_pairs={{124,126},{125,127},{252,254},{253,255},{380,382},{381,383},{508,5... | collective-permute-start | bytes 1179656 | tf_op jit(solution)/shard_map/ppermute | solution.py:28
  15.3 5.0 %conditional.3 = (f32[96,1024]{1,0:T(8,128)S(1)}) conditional(s32[]{:T(128)} %convert_element_type.7, f32[96,1024]{1,0:T(8,128)} %bitcast.9, (f32[96,1024]{1,0:T(8,128)}, f32[]{:T(128)}) %tuple.25), branch_computations={%region_2.3_spmd, %region_3.4_spmd} | conditional | flops 98304 | bytes 2359348 | solution.py:278
  15.3 3.4 %collective-permute-start.2 = (f32[96,1024]{1,0:T(8,128)}, f32[96,1024]{1,0:T(8,128)S(1)}, u32[]{:S(2)}, u32[]{:S(2)}) collective-permute-start(f32[96,1024]{1,0:T(8,128)} %get-tuple-element.26), channel_id=1, source_target_pairs={{0,1},{1,0},{4,5},{5,4},{8,9},{9,8},{12,13},{13,12},{16,17},{17,16... | collective-permute-start | bytes 1179656 | tf_op jit(solution)/shard_map/cond/branch_1_fun/ppermute | solution.py:28
  18.7 1.5 %collective-permute-done.2 = f32[96,1024]{1,0:T(8,128)S(1)} collective-permute-done((f32[96,1024]{1,0:T(8,128)}, f32[96,1024]{1,0:T(8,128)S(1)}, u32[]{:S(2)}, u32[]{:S(2)}) %collective-permute-start.2) | collective-permute-done | bytes 393248 | tf_op jit(solution)/shard_map/cond/branch_1_fun/ppermute | solution.py:28
  20.3 4.7 %collective-permute-done.3.refs_0_ = f32[96,1024]{1,0:T(8,128)S(1)} collective-permute-done((f32[96,1024]{1,0:T(8,128)}, f32[96,1024]{1,0:T(8,128)S(1)}, u32[]{:S(2)}, u32[]{:S(2)}) %collective-permute-start.3) | collective-permute-done | bytes 393248 | tf_op jit(solution)/shard_map/ppermute | solution.py:33
  25.0 0.0 collective-permute-done.4.refs_4_
  25.0 0.0 copy-start
  25.0 7.0 %conditional.2 = (f32[96,1024]{1,0:T(8,128)S(1)}, f32[96,1024]{1,0:T(8,128)S(1)}) conditional(s32[]{:T(128)} %convert_element_type.7, (f32[96,1024]{1,0:T(8,128)S(1)}, f32[96,1024]{1,0:T(8,128)S(1)}) %tuple.18, (f32[96,1024]{1,0:T(8,128)S(1)}, f32[]{:T(128)}, f32[96,1024]{1,0:T(8,128)S(1)}) %tuple.19), branch_computations={%region_0.1_spmd, %region_1.2_spmd} | conditional | flops 196608 | bytes 4718696 | solution.py:281
  25.0 3.3 %collective-permute-start.1 = (f32[96,1024]{1,0:T(8,128)S(1)}, f32[96,1024]{1,0:T(8,128)S(1)}, u32[]{:S(2)}, u32[]{:S(2)}) collective-permute-start(f32[96,1024]{1,0:T(8,128)S(1)} %get-tuple-element.25), channel_id=1, source_target_pairs={{0,1},{1,0},{4,5},{5,4},{8,9},{9,8},{12,13},{13,12},{16,17},{17,16... | collective-permute-start | bytes 1179656 | tf_op jit(solution)/shard_map/cond/branch_1_fun/ppermute | solution.py:28
  28.3 1.9 %collective-permute-start = (f32[96,1024]{1,0:T(8,128)S(1)}, f32[96,1024]{1,0:T(8,128)S(1)}, u32[]{:S(2)}, u32[]{:S(2)}) collective-permute-start(f32[96,1024]{1,0:T(8,128)S(1)} %get-tuple-element.23), channel_id=1, source_target_pairs={{0,1},{1,0},{4,5},{5,4},{8,9},{9,8},{12,13},{13,12},{16,17},{17,16... | collective-permute-start | bytes 1179656 | tf_op jit(solution)/shard_map/cond/branch_1_fun/ppermute | solution.py:28
  30.2 0.0 collective-permute-done.1
  30.3 1.6 %collective-permute-done = f32[96,1024]{1,0:T(8,128)S(1)} collective-permute-done((f32[96,1024]{1,0:T(8,128)S(1)}, f32[96,1024]{1,0:T(8,128)S(1)}, u32[]{:S(2)}, u32[]{:S(2)}) %collective-permute-start) | collective-permute-done | bytes 393248 | tf_op jit(solution)/shard_map/cond/branch_1_fun/ppermute | solution.py:28
  32.0 0.0 copy-done
  32.0 0.9 %prepare.1 = (bf16[3,256,1024]{2,1,0:T(8,128)(2,1)S(1)}, bf16[3,256,1024]{2,1,0:T(8,128)(2,1)S(1)}, f32[8,256]{1,0:T(8,128)S(1)}) custom-call(s32[1]{0:T(128)} %bitcast.chip_ref, s32[1]{0:T(128)} %bitcast.1.core_ref, f32[96,1024]{1,0:T(8,128)S(1)} %collective-permute-done.3.refs_0_, f32[96,1024]{1,0:T(8,128)S(1)} %get-tuple-element.35.refs_1_, ...), custom_call_target="tpu_custom_call" | custom-call | tf_op jit(solution)/shard_map/prepare/pallas_call | solution.py:212
  32.9 0.0 collective-permute-done.5.rows_ref
  32.9 2.0 %rows_of_partner.2.partner_ref = f32[48,128]{1,0:T(8,128)S(1)} custom-call(s32[1]{0:T(128)} %bitcast.chip_ref, f32[96,1024]{1,0:T(8,128)S(1)} %collective-permute-done.5.rows_ref, bf16[3,256,1024]{2,1,0:T(8,128)(2,1)S(1)} %get-tuple-element.37.high_ref, bf16[3,256,1024]{2,1,0:T(8,128)(2,1)S(1)} %get-tuple-element.38.low_ref, ...), custom_call_target="tpu_custom_call" | custom-call | tf_op jit(solution)/shard_map/rows_of_partner/pallas_call | solution.py:243
  34.9 4.4 %collective-permute-start.6 = (f32[48,128]{1,0:T(8,128)S(1)}, f32[48,128]{1,0:T(8,128)S(1)}, u32[]{:S(2)}, u32[]{:S(2)}) collective-permute-start(f32[48,128]{1,0:T(8,128)S(1)} %rows_of_partner.2.partner_ref), channel_id=1, source_target_pairs={{0,2},{1,3},{4,6},{5,7},{8,10},{9,11},{12,14},{13,15},{16,18},{17,... | collective-permute-start | bytes 73736 | tf_op jit(solution)/shard_map/ppermute | solution.py:28
  39.3 2.1 %rows_of_own.1 = (f32[32,384]{1,0:T(8,128)S(1)}, f32[32,128]{1,0:T(8,128)S(1)}) custom-call(s32[1]{0:T(128)} %bitcast.chip_ref, f32[96,1024]{1,0:T(8,128)S(1)} %bitcast.13, bf16[3,256,1024]{2,1,0:T(8,128)(2,1)S(1)} %get-tuple-element.37.high_ref, bf16[3,256,1024]{2,1,0:T(8,128)(2,1)S(1)} %get-tuple-element.38.low_ref, ...), custom_call_target="tpu_custom_call" | custom-call | tf_op jit(solution)/shard_map/rows_of_own/pallas_call | solution.py:231
  41.4 1.3 %collective-permute-start.7 = (f32[32,128]{1,0:T(8,128)S(1)}, f32[32,128]{1,0:T(8,128)S(1)}, u32[]{:S(2)}, u32[]{:S(2)}) collective-permute-start(f32[32,128]{1,0:T(8,128)S(1)} %get-tuple-element.41.refs_0_), channel_id=1, source_target_pairs={{0,510},{1,511},{128,124},{129,125},{256,252},{257,253},{384,380},... | collective-permute-start | bytes 49160 | tf_op jit(solution)/shard_map/ppermute | solution.py:28
  42.7 1.3 %collective-permute-start.8 = (f32[32,128]{1,0:T(8,128)S(1)}, f32[32,128]{1,0:T(8,128)S(1)}, u32[]{:S(2)}, u32[]{:S(2)}) collective-permute-start(f32[32,128]{1,0:T(8,128)S(1)} %get-tuple-element.41.refs_0_), channel_id=1, source_target_pairs={{0,511},{1,510},{128,125},{129,124},{256,253},{257,252},{384,381},... | collective-permute-start | bytes 49160 | tf_op jit(solution)/shard_map/ppermute | solution.py:28
  44.0 0.0 collective-permute-done.9.rows_ref
  44.0 0.7 %collective-permute-start.10 = (f32[32,128]{1,0:T(8,128)S(1)}, f32[32,128]{1,0:T(8,128)S(1)}, u32[]{:S(2)}, u32[]{:S(2)}) collective-permute-start(f32[32,128]{1,0:T(8,128)S(1)} %rows_of_partner.3), channel_id=1, source_target_pairs={{124,126},{125,127},{252,254},{253,255},{380,382},{381,383},{508,5... | collective-permute-start | bytes 49160 | tf_op jit(solution)/shard_map/ppermute | solution.py:28
  44.7 0.0 collective-permute-done.6.far_ref
  44.7 0.1 tiles.1.tiles_ref
  44.9 0.0 collective-permute-done.7.mine_ref
  44.9 0.0 collective-permute-done.8.other_ref
  44.9 0.0 collective-permute-done.10.far_ref
  44.9 0.6 %final.1 = f32[32,384]{1,0:T(8,128)} custom-call(s32[1]{0:T(128)} %bitcast.chip_ref, f32[32,384]{1,0:T(8,128)S(1)} %next_columns.1.tiles_ref, f32[32,128]{1,0:T(8,128)S(1)} %collective-permute-done.10.far_ref), custom_call_target="tpu_custom_call" | custom-call | tf_op jit(solution)/shard_map/final/pallas_call | solution.py:199
  (6 shorter events, 0.1 us)
Async XLA Ops:
  0.0 25.0 %collective-permute-start.3 = (f32[96,1024]{1,0:T(8,128)}, f32[96,1024]{1,0:T(8,128)S(1)}, u32[]{:S(2)}, u32[]{:S(2)}) collective-permute-start(f32[96,1024]{1,0:T(8,128)} %bitcast.5), channel_id=1, source_target_pairs={{4,8},{5,9},{8,4},{9,5},{12,16},{13,17},{16,12},{17,13},{20,24},{2... | collective-permute-start | bytes 1179656 | tf_op jit(solution)/shard_map/ppermute | solution.py:33
  1.3 23.7 %collective-permute-start.4 = (f32[96,1024]{1,0:T(8,128)}, f32[96,1024]{1,0:T(8,128)S(1)}, u32[]{:S(2)}, u32[]{:S(2)}) collective-permute-start(f32[96,1024]{1,0:T(8,128)} %bitcast.6), channel_id=1, source_target_pairs={{0,4},{1,5},{4,0},{5,1},{8,12},{9,13},{12,8},{13,9},{16,20},{17,21... | collective-permute-start | bytes 1179656 | tf_op jit(solution)/shard_map/ppermute | solution.py:33
  7.1 25.8 %collective-permute-start.5 = (f32[96,1024]{1,0:T(8,128)}, f32[96,1024]{1,0:T(8,128)S(1)}, u32[]{:S(2)}, u32[]{:S(2)}) collective-permute-start(f32[96,1024]{1,0:T(8,128)} %bitcast.7), channel_id=1, source_target_pairs={{0,2},{1,3},{4,6},{5,7},{8,10},{9,11},{12,14},{13,15},{16,18},{17,... | collective-permute-start | bytes 1179656 | tf_op jit(solution)/shard_map/ppermute | solution.py:28
  14.5 29.5 %collective-permute-start.9 = (f32[96,1024]{1,0:T(8,128)}, f32[96,1024]{1,0:T(8,128)S(1)}, u32[]{:S(2)}, u32[]{:S(2)}) collective-permute-start(f32[96,1024]{1,0:T(8,128)} %bitcast.8), channel_id=1, source_target_pairs={{124,126},{125,127},{252,254},{253,255},{380,382},{381,383},{508,5... | collective-permute-start | bytes 1179656 | tf_op jit(solution)/shard_map/ppermute | solution.py:28
  15.3 5.0 %collective-permute-start.2 = (f32[96,1024]{1,0:T(8,128)}, f32[96,1024]{1,0:T(8,128)S(1)}, u32[]{:S(2)}, u32[]{:S(2)}) collective-permute-start(f32[96,1024]{1,0:T(8,128)} %get-tuple-element.26), channel_id=1, source_target_pairs={{0,1},{1,0},{4,5},{5,4},{8,9},{9,8},{12,13},{13,12},{16,17},{17,16... | collective-permute-start | bytes 1179656 | tf_op jit(solution)/shard_map/cond/branch_1_fun/ppermute | solution.py:28
  25.0 7.0 %copy-start = (f32[32,3,1024]{2,0,1:T(8,128)S(1)}, f32[32,3,1024]{2,0,1:T(8,128)}, u32[]{:S(2)}) copy-start(f32[32,3,1024]{2,0,1:T(8,128)} %param.5) | copy-start | bytes 1179652
  25.0 5.2 %collective-permute-start.1 = (f32[96,1024]{1,0:T(8,128)S(1)}, f32[96,1024]{1,0:T(8,128)S(1)}, u32[]{:S(2)}, u32[]{:S(2)}) collective-permute-start(f32[96,1024]{1,0:T(8,128)S(1)} %get-tuple-element.25), channel_id=1, source_target_pairs={{0,1},{1,0},{4,5},{5,4},{8,9},{9,8},{12,13},{13,12},{16,17},{17,16... | collective-permute-start | bytes 1179656 | tf_op jit(solution)/shard_map/cond/branch_1_fun/ppermute | solution.py:28
  28.3 3.6 %collective-permute-start = (f32[96,1024]{1,0:T(8,128)S(1)}, f32[96,1024]{1,0:T(8,128)S(1)}, u32[]{:S(2)}, u32[]{:S(2)}) collective-permute-start(f32[96,1024]{1,0:T(8,128)S(1)} %get-tuple-element.23), channel_id=1, source_target_pairs={{0,1},{1,0},{4,5},{5,4},{8,9},{9,8},{12,13},{13,12},{16,17},{17,16... | collective-permute-start | bytes 1179656 | tf_op jit(solution)/shard_map/cond/branch_1_fun/ppermute | solution.py:28
  34.9 9.8 %collective-permute-start.6 = (f32[48,128]{1,0:T(8,128)S(1)}, f32[48,128]{1,0:T(8,128)S(1)}, u32[]{:S(2)}, u32[]{:S(2)}) collective-permute-start(f32[48,128]{1,0:T(8,128)S(1)} %rows_of_partner.2.partner_ref), channel_id=1, source_target_pairs={{0,2},{1,3},{4,6},{5,7},{8,10},{9,11},{12,14},{13,15},{16,18},{17,... | collective-permute-start | bytes 73736 | tf_op jit(solution)/shard_map/ppermute | solution.py:28
  41.4 3.5 %collective-permute-start.7 = (f32[32,128]{1,0:T(8,128)S(1)}, f32[32,128]{1,0:T(8,128)S(1)}, u32[]{:S(2)}, u32[]{:S(2)}) collective-permute-start(f32[32,128]{1,0:T(8,128)S(1)} %get-tuple-element.41.refs_0_), channel_id=1, source_target_pairs={{0,510},{1,511},{128,124},{129,125},{256,252},{257,253},{384,380},... | collective-permute-start | bytes 49160 | tf_op jit(solution)/shard_map/ppermute | solution.py:28
  42.7 2.2 %collective-permute-start.8 = (f32[32,128]{1,0:T(8,128)S(1)}, f32[32,128]{1,0:T(8,128)S(1)}, u32[]{:S(2)}, u32[]{:S(2)}) collective-permute-start(f32[32,128]{1,0:T(8,128)S(1)} %get-tuple-element.41.refs_0_), channel_id=1, source_target_pairs={{0,511},{1,510},{128,125},{129,124},{256,253},{257,252},{384,381},... | collective-permute-start | bytes 49160 | tf_op jit(solution)/shard_map/ppermute | solution.py:28
  44.0 0.9 %collective-permute-start.10 = (f32[32,128]{1,0:T(8,128)S(1)}, f32[32,128]{1,0:T(8,128)S(1)}, u32[]{:S(2)}, u32[]{:S(2)}) collective-permute-start(f32[32,128]{1,0:T(8,128)S(1)} %rows_of_partner.3), channel_id=1, source_target_pairs={{124,126},{125,127},{252,254},{253,255},{380,382},{381,383},{508,5... | collective-permute-start | bytes 49160 | tf_op jit(solution)/shard_map/ppermute | solution.py:28

commit v6 on v5

--- a/solution.py
+++ b/solution.py
@@ -59,9 +59,6 @@
             high_ref[b, pl.ds(start, 32), :] = high
             low_ref[b, pl.ds(start, 32), :] = low
         column_ref[pl.ds(start, 32), :] = jnp.broadcast_to(norm, (32, 128))
-    for b in range(3):
-        high_ref[b, 192:256, :] = jnp.zeros((64, ATOMS), jnp.bfloat16)
-        low_ref[b, 192:256, :] = jnp.zeros((64, ATOMS), jnp.bfloat16)
     norm_ref[...] = jnp.transpose(column_ref[...])[0:8, :]
 
 
@@ -77,6 +74,10 @@
     return sum(x[a][b] * cov[a][b] for a in range(3) for b in range(3))
 
 
+def folded(value):
+    return jnp.concatenate([value[:16], value[16:]], axis=1)
+
+
 def fill_rows(rows_ref, high_ref, low_ref, norm_ref, out_ref, left_ref, cov_ref):
     norm = jnp.zeros((32, 1), jnp.float32)
     for a in range(3):
@@ -86,25 +87,33 @@
         left_ref[32 * a : 32 * a + 32, :] = high
         left_ref[96 + 32 * a : 128 + 32 * a, :] = low
     dims = (((1,), (1,)), ((), ()))
+    used = 128 if out_ref.shape == (32, 128) else 192
     for b in range(3):
-        one = lax.dot_general(left_ref[...], high_ref[b], dims, preferred_element_type=jnp.float32)
-        two = lax.dot_general(left_ref[...], low_ref[b], dims, preferred_element_type=jnp.float32)
-        cov_ref[b] = one[:96] + (one[96:] + two[:96] + two[96:])
-    row_root = 1.0 / jnp.sqrt(norm + 1e-6)
-    tiles = []
-    for t in range(2):
-        lanes = slice(128 * t, 128 * t + 128)
-        columns = norm_ref[0:1, lanes]
-        scale = row_root * (1.0 / jnp.sqrt(columns + 1e-6))
-        cov = [[cov_ref[b, 32 * a : 32 * a + 32, lanes] for b in range(3)] for a in range(3)]
-        aligned = polar_trace(cov, scale)
-        tiles.append((norm + columns - 2.0 * aligned) * (1.0 / ATOMS))
+        one = lax.dot_general(left_ref[...], high_ref[b, :used], dims, preferred_element_type=jnp.float32)
+        two = lax.dot_general(left_ref[...], low_ref[b, :used], dims, preferred_element_type=jnp.float32)
+        cov_ref[b, :, :used] = one[:96] + (one[96:] + two[:96] + two[96:])
+
+    def tile(lanes, norm, columns, shaped=lambda value: value):
+        scale = (1.0 / jnp.sqrt(norm + 1e-6)) * (1.0 / jnp.sqrt(columns + 1e-6))
+        cov = [[shaped(cov_ref[b, 32 * a : 32 * a + 32, lanes]) for b in range(3)] for a in range(3)]
+        return (norm + columns - 2.0 * polar_trace(cov, scale)) * (1.0 / ATOMS)
+
+    first = tile(slice(0, 128), norm, norm_ref[0:1, :128])
+    if used == 128:
+        out_ref[...] = first
+        return
+    columns = norm_ref[0:1, 128:192]
+    second = tile(
+        slice(128, 192),
+        folded(jnp.broadcast_to(norm, (32, 64))),
+        jnp.concatenate([columns, columns], axis=1),
+        folded,
+    )
     if out_ref.shape[1] == 128:
-        out_ref[0:32, :] = tiles[0]
-        if out_ref.shape[0] == 48:
-            out_ref[32:48, :] = jnp.concatenate([tiles[1][:16, :64], tiles[1][16:, :64]], axis=1)
+        out_ref[0:32, :] = first
+        out_ref[32:48, :] = second
     else:
-        out_ref[...] = doubled(tiles[0], tiles[1][:, :64])
+        out_ref[...] = doubled(first, jnp.concatenate([second[:, :64], second[:, 64:]], axis=0))
 
 
 def doubled(first, nxt):
@@ -208,7 +217,7 @@
 
 def prepare(chip, core, *frames):
     spec = pl.BlockSpec(memory_space=pltpu.VMEM)
-    wide = jax.ShapeDtypeStruct((3, 256, ATOMS), jnp.bfloat16)
+    wide = jax.ShapeDtypeStruct((3, 192, ATOMS), jnp.bfloat16)
     return pl.pallas_call(
         prepare_kernel,
         out_shape=(wide, wide, jax.ShapeDtypeStruct((8, 256), jnp.float32)),

time: 46.3 us -> 45.8 us (0.989)
  the two profiles are of different devices: /device:TPU:1 before, /device:TPU:196 now
where the time goes in v6:
time: 45.8 us; the launch traced here: 45.5 us
  starting transfers between devices  37.1 us (81%)
  Pallas kernels  4.75 us (10%)
  waiting for transfers between devices  3.2 us (7%)
    ppermute x9, starting transfers between devices, moved(): return lax.ppermute(value, AXES, pairs)  28.6 us
    ppermute x2, starting transfers between devices, stepped(): return lax.ppermute(value, AXES, pairs)  8.5 us
    ppermute x9, waiting for transfers between devices, moved(): return lax.ppermute(value, AXES, pairs)  3.2 us
    pallas_call x2, Pallas kernels, own_rows(): pl.pallas_call(own_kernel if more else early_kernel, out_shape=(TILES, ME...  1.65 us
    pallas_call x2, Pallas kernels, partner_rows(): pl.pallas_call(functools.partial(partner_kernel, before=before), out_shap...  1.45 us
  transfers between devices with their start and end apart: 11, of which 2 were waited for; matrix products, arithmetic and copies ran while one was open for 0% of the time, Pallas kernels for 9%

profile of v6, /device:TPU:196, one launch (start us, length us, event | category | flops | bytes accessed | tf_op | source)
XLA Modules:
  0.0 45.5 jit_solution(12799863425177311153)
XLA Ops:
  0.0 2.4 %collective-permute-start.3 = (f32[96,1024]{1,0:T(8,128)}, f32[96,1024]{1,0:T(8,128)S(1)}, u32[]{:S(2)}, u32[]{:S(2)}) collective-permute-start(f32[96,1024]{1,0:T(8,128)} %bitcast.5), channel_id=1, source_target_pairs={{4,8},{5,9},{8,4},{9,5},{12,16},{13,17},{16,12},{17,13},{20,24},{2... | collective-permute-start | bytes 1179656 | tf_op jit(solution)/shard_map/ppermute | solution.py:33
  2.4 6.1 %collective-permute-start.4 = (f32[96,1024]{1,0:T(8,128)}, f32[96,1024]{1,0:T(8,128)S(1)}, u32[]{:S(2)}, u32[]{:S(2)}) collective-permute-start(f32[96,1024]{1,0:T(8,128)} %bitcast.6), channel_id=1, source_target_pairs={{0,4},{1,5},{4,0},{5,1},{8,12},{9,13},{12,8},{13,9},{16,20},{17,21... | collective-permute-start | bytes 1179656 | tf_op jit(solution)/shard_map/ppermute | solution.py:33
  8.5 7.7 %collective-permute-start.5 = (f32[96,1024]{1,0:T(8,128)}, f32[96,1024]{1,0:T(8,128)S(1)}, u32[]{:S(2)}, u32[]{:S(2)}) collective-permute-start(f32[96,1024]{1,0:T(8,128)} %bitcast.7), channel_id=1, source_target_pairs={{0,2},{1,3},{4,6},{5,7},{8,10},{9,11},{12,14},{13,15},{16,18},{17,... | collective-permute-start | bytes 1179656 | tf_op jit(solution)/shard_map/ppermute | solution.py:28
  16.3 0.7 %collective-permute-start.9 = (f32[96,1024]{1,0:T(8,128)}, f32[96,1024]{1,0:T(8,128)S(1)}, u32[]{:S(2)}, u32[]{:S(2)}) collective-permute-start(f32[96,1024]{1,0:T(8,128)} %bitcast.8), channel_id=1, source_target_pairs={{124,126},{125,127},{252,254},{253,255},{380,382},{381,383},{508,5... | collective-permute-start | bytes 1179656 | tf_op jit(solution)/shard_map/ppermute | solution.py:28
  17.0 3.9 %conditional.3 = (f32[96,1024]{1,0:T(8,128)S(1)}) conditional(s32[]{:T(128)} %convert_element_type.7, f32[96,1024]{1,0:T(8,128)} %bitcast.9, (f32[96,1024]{1,0:T(8,128)}, f32[]{:T(128)}) %tuple.25), branch_computations={%region_2.3_spmd, %region_3.4_spmd} | conditional | flops 98304 | bytes 2359348 | solution.py:287
  17.0 1.9 %collective-permute-start.2 = (f32[96,1024]{1,0:T(8,128)}, f32[96,1024]{1,0:T(8,128)S(1)}, u32[]{:S(2)}, u32[]{:S(2)}) collective-permute-start(f32[96,1024]{1,0:T(8,128)} %get-tuple-element.26), channel_id=1, source_target_pairs={{0,1},{1,0},{4,5},{5,4},{8,9},{9,8},{12,13},{13,12},{16,17},{17,16... | collective-permute-start | bytes 1179656 | tf_op jit(solution)/shard_map/cond/branch_1_fun/ppermute | solution.py:28
  18.9 1.9 %collective-permute-done.2 = f32[96,1024]{1,0:T(8,128)S(1)} collective-permute-done((f32[96,1024]{1,0:T(8,128)}, f32[96,1024]{1,0:T(8,128)S(1)}, u32[]{:S(2)}, u32[]{:S(2)}) %collective-permute-start.2) | collective-permute-done | bytes 393248 | tf_op jit(solution)/shard_map/cond/branch_1_fun/ppermute | solution.py:28
  20.9 0.0 collective-permute-done.3.refs_0_
  20.9 0.0 collective-permute-done.4.refs_4_
  20.9 0.0 copy-start
  20.9 5.9 %conditional.2 = (f32[96,1024]{1,0:T(8,128)S(1)}, f32[96,1024]{1,0:T(8,128)S(1)}) conditional(s32[]{:T(128)} %convert_element_type.7, (f32[96,1024]{1,0:T(8,128)S(1)}, f32[96,1024]{1,0:T(8,128)S(1)}) %tuple.18, (f32[96,1024]{1,0:T(8,128)S(1)}, f32[]{:T(128)}, f32[96,1024]{1,0:T(8,128)S(1)}) %tuple.19), branch_computations={%region_0.1_spmd, %region_1.2_spmd} | conditional | flops 196608 | bytes 4718696 | solution.py:290
  20.9 2.2 %collective-permute-start.1 = (f32[96,1024]{1,0:T(8,128)S(1)}, f32[96,1024]{1,0:T(8,128)S(1)}, u32[]{:S(2)}, u32[]{:S(2)}) collective-permute-start(f32[96,1024]{1,0:T(8,128)S(1)} %get-tuple-element.25), channel_id=1, source_target_pairs={{0,1},{1,0},{4,5},{5,4},{8,9},{9,8},{12,13},{13,12},{16,17},{17,16... | collective-permute-start | bytes 1179656 | tf_op jit(solution)/shard_map/cond/branch_1_fun/ppermute | solution.py:28
  23.1 2.3 %collective-permute-start = (f32[96,1024]{1,0:T(8,128)S(1)}, f32[96,1024]{1,0:T(8,128)S(1)}, u32[]{:S(2)}, u32[]{:S(2)}) collective-permute-start(f32[96,1024]{1,0:T(8,128)S(1)} %get-tuple-element.23), channel_id=1, source_target_pairs={{0,1},{1,0},{4,5},{5,4},{8,9},{9,8},{12,13},{13,12},{16,17},{17,16... | collective-permute-start | bytes 1179656 | tf_op jit(solution)/shard_map/cond/branch_1_fun/ppermute | solution.py:28
  25.4 0.0 collective-permute-done.1
  25.4 1.3 %collective-permute-done = f32[96,1024]{1,0:T(8,128)S(1)} collective-permute-done((f32[96,1024]{1,0:T(8,128)S(1)}, f32[96,1024]{1,0:T(8,128)S(1)}, u32[]{:S(2)}, u32[]{:S(2)}) %collective-permute-start) | collective-permute-done | bytes 393248 | tf_op jit(solution)/shard_map/cond/branch_1_fun/ppermute | solution.py:28
  26.8 0.0 copy-done
  26.8 0.9 %prepare.1 = (bf16[3,192,1024]{2,1,0:T(8,128)(2,1)S(1)}, bf16[3,192,1024]{2,1,0:T(8,128)(2,1)S(1)}, f32[8,256]{1,0:T(8,128)S(1)}) custom-call(s32[1]{0:T(128)} %bitcast.chip_ref, s32[1]{0:T(128)} %bitcast.1.core_ref, f32[96,1024]{1,0:T(8,128)S(1)} %collective-permute-done.3.refs_0_, f32[96,1024]{1,0:T(8,128)S(1)} %get-tuple-element.35.refs_1_, ...), custom_call_target="tpu_custom_call" | custom-call | tf_op jit(solution)/shard_map/prepare/pallas_call | solution.py:221
  27.6 1.6 %early_rows_of_own.1.refs_0_.early_ref = f32[32,384]{1,0:T(8,128)S(1)} custom-call(s32[1]{0:T(128)} %bitcast.chip_ref, f32[96,1024]{1,0:T(8,128)S(1)} %bitcast.12, bf16[3,192,1024]{2,1,0:T(8,128)(2,1)S(1)} %get-tuple-element.37.high_ref, bf16[3,192,1024]{2,1,0:T(8,128)(2,1)S(1)} %get-tuple-element.38.low_ref, f32[8,256]{1,0:T(8,128)S(1)} %get-tuple-element.39.norm_ref), custom_call_target="tpu_custom_call" | custom-call | tf_op jit(solution)/shard_map/early_rows_of_own/pallas_call | solution.py:240
  29.2 0.0 collective-permute-done.5.rows_ref
  29.2 1.4 %rows_of_partner.2.partner_ref = f32[48,128]{1,0:T(8,128)S(1)} custom-call(s32[1]{0:T(128)} %bitcast.chip_ref, f32[96,1024]{1,0:T(8,128)S(1)} %collective-permute-done.5.rows_ref, bf16[3,192,1024]{2,1,0:T(8,128)(2,1)S(1)} %get-tuple-element.37.high_ref, bf16[3,192,1024]{2,1,0:T(8,128)(2,1)S(1)} %get-tuple-element.38.low_ref, ...), custom_call_target="tpu_custom_call" | custom-call | tf_op jit(solution)/shard_map/rows_of_partner/pallas_call | solution.py:252
  30.6 11.9 %collective-permute-start.6 = (f32[48,128]{1,0:T(8,128)S(1)}, f32[48,128]{1,0:T(8,128)S(1)}, u32[]{:S(2)}, u32[]{:S(2)}) collective-permute-start(f32[48,128]{1,0:T(8,128)S(1)} %rows_of_partner.2.partner_ref), channel_id=1, source_target_pairs={{0,2},{1,3},{4,6},{5,7},{8,10},{9,11},{12,14},{13,15},{16,18},{17,... | collective-permute-start | bytes 73736 | tf_op jit(solution)/shard_map/ppermute | solution.py:28
  42.5 0.1 rows_of_own.1
  42.6 0.7 %collective-permute-start.7 = (f32[32,128]{1,0:T(8,128)S(1)}, f32[32,128]{1,0:T(8,128)S(1)}, u32[]{:S(2)}, u32[]{:S(2)}) collective-permute-start(f32[32,128]{1,0:T(8,128)S(1)} %get-tuple-element.41.refs_0_), channel_id=1, source_target_pairs={{0,510},{1,511},{128,124},{129,125},{256,252},{257,253},{384,380},... | collective-permute-start | bytes 49160 | tf_op jit(solution)/shard_map/ppermute | solution.py:28
  43.2 0.7 %collective-permute-start.8 = (f32[32,128]{1,0:T(8,128)S(1)}, f32[32,128]{1,0:T(8,128)S(1)}, u32[]{:S(2)}, u32[]{:S(2)}) collective-permute-start(f32[32,128]{1,0:T(8,128)S(1)} %get-tuple-element.41.refs_0_), channel_id=1, source_target_pairs={{0,511},{1,510},{128,125},{129,124},{256,253},{257,252},{384,381},... | collective-permute-start | bytes 49160 | tf_op jit(solution)/shard_map/ppermute | solution.py:28
  43.9 0.0 collective-permute-done.9.rows_ref
  44.0 0.7 %collective-permute-start.10 = (f32[32,128]{1,0:T(8,128)S(1)}, f32[32,128]{1,0:T(8,128)S(1)}, u32[]{:S(2)}, u32[]{:S(2)}) collective-permute-start(f32[32,128]{1,0:T(8,128)S(1)} %rows_of_partner.3), channel_id=1, source_target_pairs={{124,126},{125,127},{252,254},{253,255},{380,382},{381,383},{508,5... | collective-permute-start | bytes 49160 | tf_op jit(solution)/shard_map/ppermute | solution.py:28
  44.6 0.0 collective-permute-done.6.far_ref
  44.6 0.1 tiles.1.tiles_ref
  44.8 0.0 collective-permute-done.7.mine_ref
  44.8 0.0 collective-permute-done.8.other_ref
  44.8 0.0 collective-permute-done.10.far_ref
  44.8 0.6 %final.1 = f32[32,384]{1,0:T(8,128)} custom-call(s32[1]{0:T(128)} %bitcast.chip_ref, f32[32,384]{1,0:T(8,128)S(1)} %next_columns.1.tiles_ref, f32[32,128]{1,0:T(8,128)S(1)} %collective-permute-done.10.far_ref), custom_call_target="tpu_custom_call" | custom-call | tf_op jit(solution)/shard_map/final/pallas_call | solution.py:208
  (5 shorter events, 0.1 us)
Async XLA Ops:
  0.0 20.9 %collective-permute-start.3 = (f32[96,1024]{1,0:T(8,128)}, f32[96,1024]{1,0:T(8,128)S(1)}, u32[]{:S(2)}, u32[]{:S(2)}) collective-permute-start(f32[96,1024]{1,0:T(8,128)} %bitcast.5), channel_id=1, source_target_pairs={{4,8},{5,9},{8,4},{9,5},{12,16},{13,17},{16,12},{17,13},{20,24},{2... | collective-permute-start | bytes 1179656 | tf_op jit(solution)/shard_map/ppermute | solution.py:33
  2.4 18.4 %collective-permute-start.4 = (f32[96,1024]{1,0:T(8,128)}, f32[96,1024]{1,0:T(8,128)S(1)}, u32[]{:S(2)}, u32[]{:S(2)}) collective-permute-start(f32[96,1024]{1,0:T(8,128)} %bitcast.6), channel_id=1, source_target_pairs={{0,4},{1,5},{4,0},{5,1},{8,12},{9,13},{12,8},{13,9},{16,20},{17,21... | collective-permute-start | bytes 1179656 | tf_op jit(solution)/shard_map/ppermute | solution.py:33
  8.5 20.7 %collective-permute-start.5 = (f32[96,1024]{1,0:T(8,128)}, f32[96,1024]{1,0:T(8,128)S(1)}, u32[]{:S(2)}, u32[]{:S(2)}) collective-permute-start(f32[96,1024]{1,0:T(8,128)} %bitcast.7), channel_id=1, source_target_pairs={{0,2},{1,3},{4,6},{5,7},{8,10},{9,11},{12,14},{13,15},{16,18},{17,... | collective-permute-start | bytes 1179656 | tf_op jit(solution)/shard_map/ppermute | solution.py:28
  16.3 27.7 %collective-permute-start.9 = (f32[96,1024]{1,0:T(8,128)}, f32[96,1024]{1,0:T(8,128)S(1)}, u32[]{:S(2)}, u32[]{:S(2)}) collective-permute-start(f32[96,1024]{1,0:T(8,128)} %bitcast.8), channel_id=1, source_target_pairs={{124,126},{125,127},{252,254},{253,255},{380,382},{381,383},{508,5... | collective-permute-start | bytes 1179656 | tf_op jit(solution)/shard_map/ppermute | solution.py:28
  17.0 3.8 %collective-permute-start.2 = (f32[96,1024]{1,0:T(8,128)}, f32[96,1024]{1,0:T(8,128)S(1)}, u32[]{:S(2)}, u32[]{:S(2)}) collective-permute-start(f32[96,1024]{1,0:T(8,128)} %get-tuple-element.26), channel_id=1, source_target_pairs={{0,1},{1,0},{4,5},{5,4},{8,9},{9,8},{12,13},{13,12},{16,17},{17,16... | collective-permute-start | bytes 1179656 | tf_op jit(solution)/shard_map/cond/branch_1_fun/ppermute | solution.py:28
  20.9 5.9 %copy-start = (f32[32,3,1024]{2,0,1:T(8,128)S(1)}, f32[32,3,1024]{2,0,1:T(8,128)}, u32[]{:S(2)}) copy-start(f32[32,3,1024]{2,0,1:T(8,128)} %param.5) | copy-start | bytes 1179652
  20.9 4.5 %collective-permute-start.1 = (f32[96,1024]{1,0:T(8,128)S(1)}, f32[96,1024]{1,0:T(8,128)S(1)}, u32[]{:S(2)}, u32[]{:S(2)}) collective-permute-start(f32[96,1024]{1,0:T(8,128)S(1)} %get-tuple-element.25), channel_id=1, source_target_pairs={{0,1},{1,0},{4,5},{5,4},{8,9},{9,8},{12,13},{13,12},{16,17},{17,16... | collective-permute-start | bytes 1179656 | tf_op jit(solution)/shard_map/cond/branch_1_fun/ppermute | solution.py:28
  23.1 3.6 %collective-permute-start = (f32[96,1024]{1,0:T(8,128)S(1)}, f32[96,1024]{1,0:T(8,128)S(1)}, u32[]{:S(2)}, u32[]{:S(2)}) collective-permute-start(f32[96,1024]{1,0:T(8,128)S(1)} %get-tuple-element.23), channel_id=1, source_target_pairs={{0,1},{1,0},{4,5},{5,4},{8,9},{9,8},{12,13},{13,12},{16,17},{17,16... | collective-permute-start | bytes 1179656 | tf_op jit(solution)/shard_map/cond/branch_1_fun/ppermute | solution.py:28
  30.6 14.0 %collective-permute-start.6 = (f32[48,128]{1,0:T(8,128)S(1)}, f32[48,128]{1,0:T(8,128)S(1)}, u32[]{:S(2)}, u32[]{:S(2)}) collective-permute-start(f32[48,128]{1,0:T(8,128)S(1)} %rows_of_partner.2.partner_ref), channel_id=1, source_target_pairs={{0,2},{1,3},{4,6},{5,7},{8,10},{9,11},{12,14},{13,15},{16,18},{17,... | collective-permute-start | bytes 73736 | tf_op jit(solution)/shard_map/ppermute | solution.py:28
  42.6 2.2 %collective-permute-start.7 = (f32[32,128]{1,0:T(8,128)S(1)}, f32[32,128]{1,0:T(8,128)S(1)}, u32[]{:S(2)}, u32[]{:S(2)}) collective-permute-start(f32[32,128]{1,0:T(8,128)S(1)} %get-tuple-element.41.refs_0_), channel_id=1, source_target_pairs={{0,510},{1,511},{128,124},{129,125},{256,252},{257,253},{384,380},... | collective-permute-start | bytes 49160 | tf_op jit(solution)/shard_map/ppermute | solution.py:28
  43.2 1.5 %collective-permute-start.8 = (f32[32,128]{1,0:T(8,128)S(1)}, f32[32,128]{1,0:T(8,128)S(1)}, u32[]{:S(2)}, u32[]{:S(2)}) collective-permute-start(f32[32,128]{1,0:T(8,128)S(1)} %get-tuple-element.41.refs_0_), channel_id=1, source_target_pairs={{0,511},{1,510},{128,125},{129,124},{256,253},{257,252},{384,381},... | collective-permute-start | bytes 49160 | tf_op jit(solution)/shard_map/ppermute | solution.py:28
  44.0 0.9 %collective-permute-start.10 = (f32[32,128]{1,0:T(8,128)S(1)}, f32[32,128]{1,0:T(8,128)S(1)}, u32[]{:S(2)}, u32[]{:S(2)}) collective-permute-start(f32[32,128]{1,0:T(8,128)S(1)} %rows_of_partner.3), channel_id=1, source_target_pairs={{124,126},{125,127},{252,254},{253,255},{380,382},{381,383},{508,5... | collective-permute-start | bytes 49160 | tf_op jit(solution)/shard_map/ppermute | solution.py:28

commit v7 on v6

--- a/solution.py
+++ b/solution.py
@@ -62,16 +62,25 @@
     norm_ref[...] = jnp.transpose(column_ref[...])[0:8, :]
 
 
+ROOT_HALF = 0.5**0.5
+
+
 def polar_trace(cov, scale):
+    scale = scale * ROOT_HALF
     x = [[cov[a][b] * scale for b in range(3)] for a in range(3)]
     for _ in range(ITERS):
-        m = {}
+        g = {}
         for p in range(3):
             for q in range(p, 3):
-                g = x[0][p] * x[0][q] + x[1][p] * x[1][q] + x[2][p] * x[2][q]
-                m[p, q] = m[q, p] = 1.5 - 0.5 * g if p == q else -0.5 * g
-        x = [[x[a][0] * m[0, b] + x[a][1] * m[1, b] + x[a][2] * m[2, b] for b in range(3)] for a in range(3)]
-    return sum(x[a][b] * cov[a][b] for a in range(3) for b in range(3))
+                g[p, q] = g[q, p] = x[0][p] * x[0][q] + x[1][p] * x[1][q] + x[2][p] * x[2][q]
+        x = [
+            [
+                x[a][b] * (1.5 - g[b, b]) - (x[a][(b + 1) % 3] * g[(b + 1) % 3, b] + x[a][(b + 2) % 3] * g[(b + 2) % 3, b])
+                for b in range(3)
+            ]
+            for a in range(3)
+        ]
+    return sum(x[a][b] * cov[a][b] for a in range(3) for b in range(3)) * (1.0 / ROOT_HALF)
 
 
 def folded(value):
@@ -164,9 +173,9 @@
         out_ref[...] = jnp.zeros_like(out_ref)
 
 
-def next_kernel(chip_ref, core_ref, tiles_ref, mine_ref, other_ref, out_ref):
+def next_kernel(chip_ref, core_ref, own_ref, far_ref, mine_ref, other_ref, out_ref):
     chip, core = chip_ref[0], core_ref[0]
-    out_ref[...] = tiles_ref[...]
+    tiles_kernel(chip_ref, own_ref, far_ref, out_ref)
 
     @pl.when(chip % PLANE == PLANE - 1)
     def _():
@@ -298,8 +307,7 @@
     other = moved(message, -1, 1, afters)
     for_partner_before = partner_rows(place[0], True, far_before, *columns, message)
     returned_before = moved(for_partner_before, half, 0, befores)
-    tiles = small_call(tiles_kernel, place[:1], (own, returned), "tiles")
-    tiles = small_call(next_kernel, place, (tiles, mine, other), "next_columns")
+    tiles = small_call(next_kernel, place, (own, returned, mine, other), "next_columns")
     return small_call(final_kernel, place[:1], (tiles, returned_before), "final")
 
 

time: 45.8 us -> 45.7 us (level)
  no operation moved by 1% of the time
where the time goes in v7:
time: 45.7 us; the launch traced here: 45.4 us
  starting transfers between devices  37.2 us (81%)
  Pallas kernels  4.66 us (10%)
  waiting for transfers between devices  3.2 us (7%)
    ppermute x9, starting transfers between devices, moved(): return lax.ppermute(value, AXES, pairs)  28.7 us
    ppermute x2, starting transfers between devices, stepped(): return lax.ppermute(value, AXES, pairs)  8.5 us
    ppermute x9, waiting for transfers between devices, moved(): return lax.ppermute(value, AXES, pairs)  3.2 us
    pallas_call x2, Pallas kernels, own_rows(): pl.pallas_call(own_kernel if more else early_kernel, out_shape=(TILES, ME...  1.62 us
    pallas_call x2, Pallas kernels, partner_rows(): pl.pallas_call(functools.partial(partner_kernel, before=before), out_shap...  1.41 us
  transfers between devices with their start and end apart: 11, of which 2 were waited for; matrix products, arithmetic and copies ran while one was open for 0% of the time, Pallas kernels for 9%

profile of v7, /device:TPU:196, one launch (start us, length us, event | category | flops | bytes accessed | tf_op | source)
XLA Modules:
  0.0 45.4 jit_solution(5028825306402685456)
XLA Ops:
  0.0 2.4 %collective-permute-start.3 = (f32[96,1024]{1,0:T(8,128)}, f32[96,1024]{1,0:T(8,128)S(1)}, u32[]{:S(2)}, u32[]{:S(2)}) collective-permute-start(f32[96,1024]{1,0:T(8,128)} %bitcast.5), channel_id=1, source_target_pairs={{4,8},{5,9},{8,4},{9,5},{12,16},{13,17},{16,12},{17,13},{20,24},{2... | collective-permute-start | bytes 1179656 | tf_op jit(solution)/shard_map/ppermute | solution.py:33
  2.4 6.1 %collective-permute-start.4 = (f32[96,1024]{1,0:T(8,128)}, f32[96,1024]{1,0:T(8,128)S(1)}, u32[]{:S(2)}, u32[]{:S(2)}) collective-permute-start(f32[96,1024]{1,0:T(8,128)} %bitcast.6), channel_id=1, source_target_pairs={{0,4},{1,5},{4,0},{5,1},{8,12},{9,13},{12,8},{13,9},{16,20},{17,21... | collective-permute-start | bytes 1179656 | tf_op jit(solution)/shard_map/ppermute | solution.py:33
  8.5 7.7 %collective-permute-start.5 = (f32[96,1024]{1,0:T(8,128)}, f32[96,1024]{1,0:T(8,128)S(1)}, u32[]{:S(2)}, u32[]{:S(2)}) collective-permute-start(f32[96,1024]{1,0:T(8,128)} %bitcast.7), channel_id=1, source_target_pairs={{0,2},{1,3},{4,6},{5,7},{8,10},{9,11},{12,14},{13,15},{16,18},{17,... | collective-permute-start | bytes 1179656 | tf_op jit(solution)/shard_map/ppermute | solution.py:28
  16.3 0.7 %collective-permute-start.9 = (f32[96,1024]{1,0:T(8,128)}, f32[96,1024]{1,0:T(8,128)S(1)}, u32[]{:S(2)}, u32[]{:S(2)}) collective-permute-start(f32[96,1024]{1,0:T(8,128)} %bitcast.8), channel_id=1, source_target_pairs={{124,126},{125,127},{252,254},{253,255},{380,382},{381,383},{508,5... | collective-permute-start | bytes 1179656 | tf_op jit(solution)/shard_map/ppermute | solution.py:28
  17.0 3.9 %conditional.3 = (f32[96,1024]{1,0:T(8,128)S(1)}) conditional(s32[]{:T(128)} %convert_element_type.7, f32[96,1024]{1,0:T(8,128)} %bitcast.9, (f32[96,1024]{1,0:T(8,128)}, f32[]{:T(128)}) %tuple.25), branch_computations={%region_2.3_spmd, %region_3.4_spmd} | conditional | flops 98304 | bytes 2359348 | solution.py:296
  17.0 1.9 %collective-permute-start.2 = (f32[96,1024]{1,0:T(8,128)}, f32[96,1024]{1,0:T(8,128)S(1)}, u32[]{:S(2)}, u32[]{:S(2)}) collective-permute-start(f32[96,1024]{1,0:T(8,128)} %get-tuple-element.26), channel_id=1, source_target_pairs={{0,1},{1,0},{4,5},{5,4},{8,9},{9,8},{12,13},{13,12},{16,17},{17,16... | collective-permute-start | bytes 1179656 | tf_op jit(solution)/shard_map/cond/branch_1_fun/ppermute | solution.py:28
  18.9 1.9 %collective-permute-done.2 = f32[96,1024]{1,0:T(8,128)S(1)} collective-permute-done((f32[96,1024]{1,0:T(8,128)}, f32[96,1024]{1,0:T(8,128)S(1)}, u32[]{:S(2)}, u32[]{:S(2)}) %collective-permute-start.2) | collective-permute-done | bytes 393248 | tf_op jit(solution)/shard_map/cond/branch_1_fun/ppermute | solution.py:28
  20.9 0.0 collective-permute-done.3.refs_0_
  20.9 0.0 collective-permute-done.4.refs_4_
  20.9 0.0 copy-start
  20.9 5.9 %conditional.2 = (f32[96,1024]{1,0:T(8,128)S(1)}, f32[96,1024]{1,0:T(8,128)S(1)}) conditional(s32[]{:T(128)} %convert_element_type.7, (f32[96,1024]{1,0:T(8,128)S(1)}, f32[96,1024]{1,0:T(8,128)S(1)}) %tuple.18, (f32[96,1024]{1,0:T(8,128)S(1)}, f32[]{:T(128)}, f32[96,1024]{1,0:T(8,128)S(1)}) %tuple.19), branch_computations={%region_0.1_spmd, %region_1.2_spmd} | conditional | flops 196608 | bytes 4718696 | solution.py:299
  20.9 2.2 %collective-permute-start.1 = (f32[96,1024]{1,0:T(8,128)S(1)}, f32[96,1024]{1,0:T(8,128)S(1)}, u32[]{:S(2)}, u32[]{:S(2)}) collective-permute-start(f32[96,1024]{1,0:T(8,128)S(1)} %get-tuple-element.25), channel_id=1, source_target_pairs={{0,1},{1,0},{4,5},{5,4},{8,9},{9,8},{12,13},{13,12},{16,17},{17,16... | collective-permute-start | bytes 1179656 | tf_op jit(solution)/shard_map/cond/branch_1_fun/ppermute | solution.py:28
  23.1 2.3 %collective-permute-start = (f32[96,1024]{1,0:T(8,128)S(1)}, f32[96,1024]{1,0:T(8,128)S(1)}, u32[]{:S(2)}, u32[]{:S(2)}) collective-permute-start(f32[96,1024]{1,0:T(8,128)S(1)} %get-tuple-element.23), channel_id=1, source_target_pairs={{0,1},{1,0},{4,5},{5,4},{8,9},{9,8},{12,13},{13,12},{16,17},{17,16... | collective-permute-start | bytes 1179656 | tf_op jit(solution)/shard_map/cond/branch_1_fun/ppermute | solution.py:28
  25.4 0.0 collective-permute-done.1
  25.4 1.3 %collective-permute-done = f32[96,1024]{1,0:T(8,128)S(1)} collective-permute-done((f32[96,1024]{1,0:T(8,128)S(1)}, f32[96,1024]{1,0:T(8,128)S(1)}, u32[]{:S(2)}, u32[]{:S(2)}) %collective-permute-start) | collective-permute-done | bytes 393248 | tf_op jit(solution)/shard_map/cond/branch_1_fun/ppermute | solution.py:28
  26.8 0.0 copy-done
  26.8 0.9 %prepare.1 = (bf16[3,192,1024]{2,1,0:T(8,128)(2,1)S(1)}, bf16[3,192,1024]{2,1,0:T(8,128)(2,1)S(1)}, f32[8,256]{1,0:T(8,128)S(1)}) custom-call(s32[1]{0:T(128)} %bitcast.chip_ref, s32[1]{0:T(128)} %bitcast.1.core_ref, f32[96,1024]{1,0:T(8,128)S(1)} %collective-permute-done.3.refs_0_, f32[96,1024]{1,0:T(8,128)S(1)} %get-tuple-element.35.refs_1_, ...), custom_call_target="tpu_custom_call" | custom-call | tf_op jit(solution)/shard_map/prepare/pallas_call | solution.py:230
  27.6 1.5 %early_rows_of_own.1.refs_0_.early_ref = f32[32,384]{1,0:T(8,128)S(1)} custom-call(s32[1]{0:T(128)} %bitcast.chip_ref, f32[96,1024]{1,0:T(8,128)S(1)} %bitcast.12, bf16[3,192,1024]{2,1,0:T(8,128)(2,1)S(1)} %get-tuple-element.37.high_ref, bf16[3,192,1024]{2,1,0:T(8,128)(2,1)S(1)} %get-tuple-element.38.low_ref, f32[8,256]{1,0:T(8,128)S(1)} %get-tuple-element.39.norm_ref), custom_call_target="tpu_custom_call" | custom-call | tf_op jit(solution)/shard_map/early_rows_of_own/pallas_call | solution.py:249
  29.1 0.0 collective-permute-done.5.rows_ref
  29.2 1.4 %rows_of_partner.2.partner_ref = f32[48,128]{1,0:T(8,128)S(1)} custom-call(s32[1]{0:T(128)} %bitcast.chip_ref, f32[96,1024]{1,0:T(8,128)S(1)} %collective-permute-done.5.rows_ref, bf16[3,192,1024]{2,1,0:T(8,128)(2,1)S(1)} %get-tuple-element.37.high_ref, bf16[3,192,1024]{2,1,0:T(8,128)(2,1)S(1)} %get-tuple-element.38.low_ref, ...), custom_call_target="tpu_custom_call" | custom-call | tf_op jit(solution)/shard_map/rows_of_partner/pallas_call | solution.py:261
  30.6 11.9 %collective-permute-start.6 = (f32[48,128]{1,0:T(8,128)S(1)}, f32[48,128]{1,0:T(8,128)S(1)}, u32[]{:S(2)}, u32[]{:S(2)}) collective-permute-start(f32[48,128]{1,0:T(8,128)S(1)} %rows_of_partner.2.partner_ref), channel_id=1, source_target_pairs={{0,2},{1,3},{4,6},{5,7},{8,10},{9,11},{12,14},{13,15},{16,18},{17,... | collective-permute-start | bytes 73736 | tf_op jit(solution)/shard_map/ppermute | solution.py:28
  42.5 0.1 rows_of_own.1
  42.6 0.7 %collective-permute-start.7 = (f32[32,128]{1,0:T(8,128)S(1)}, f32[32,128]{1,0:T(8,128)S(1)}, u32[]{:S(2)}, u32[]{:S(2)}) collective-permute-start(f32[32,128]{1,0:T(8,128)S(1)} %get-tuple-element.41.refs_0_), channel_id=1, source_target_pairs={{0,510},{1,511},{128,124},{129,125},{256,252},{257,253},{384,380},... | collective-permute-start | bytes 49160 | tf_op jit(solution)/shard_map/ppermute | solution.py:28
  43.2 0.7 %collective-permute-start.8 = (f32[32,128]{1,0:T(8,128)S(1)}, f32[32,128]{1,0:T(8,128)S(1)}, u32[]{:S(2)}, u32[]{:S(2)}) collective-permute-start(f32[32,128]{1,0:T(8,128)S(1)} %get-tuple-element.41.refs_0_), channel_id=1, source_target_pairs={{0,511},{1,510},{128,125},{129,124},{256,253},{257,252},{384,381},... | collective-permute-start | bytes 49160 | tf_op jit(solution)/shard_map/ppermute | solution.py:28
  43.9 0.0 collective-permute-done.9.rows_ref
  43.9 0.7 %collective-permute-start.10 = (f32[32,128]{1,0:T(8,128)S(1)}, f32[32,128]{1,0:T(8,128)S(1)}, u32[]{:S(2)}, u32[]{:S(2)}) collective-permute-start(f32[32,128]{1,0:T(8,128)S(1)} %rows_of_partner.3), channel_id=1, source_target_pairs={{124,126},{125,127},{252,254},{253,255},{380,382},{381,383},{508,5... | collective-permute-start | bytes 49160 | tf_op jit(solution)/shard_map/ppermute | solution.py:28
  44.6 0.0 collective-permute-done.7.mine_ref
  44.6 0.0 collective-permute-done.8.other_ref
  44.6 0.0 collective-permute-done.6.far_ref
  44.6 0.1 next_columns.1.tiles_ref
  44.8 0.0 collective-permute-done.10.far_ref
  44.8 0.6 %final.1 = f32[32,384]{1,0:T(8,128)} custom-call(s32[1]{0:T(128)} %bitcast.chip_ref, f32[32,384]{1,0:T(8,128)S(1)} %next_columns.1.tiles_ref, f32[32,128]{1,0:T(8,128)S(1)} %collective-permute-done.10.far_ref), custom_call_target="tpu_custom_call" | custom-call | tf_op jit(solution)/shard_map/final/pallas_call | solution.py:217
  (4 shorter events, 0.1 us)
Async XLA Ops:
  0.0 20.9 %collective-permute-start.3 = (f32[96,1024]{1,0:T(8,128)}, f32[96,1024]{1,0:T(8,128)S(1)}, u32[]{:S(2)}, u32[]{:S(2)}) collective-permute-start(f32[96,1024]{1,0:T(8,128)} %bitcast.5), channel_id=1, source_target_pairs={{4,8},{5,9},{8,4},{9,5},{12,16},{13,17},{16,12},{17,13},{20,24},{2... | collective-permute-start | bytes 1179656 | tf_op jit(solution)/shard_map/ppermute | solution.py:33
  2.4 18.4 %collective-permute-start.4 = (f32[96,1024]{1,0:T(8,128)}, f32[96,1024]{1,0:T(8,128)S(1)}, u32[]{:S(2)}, u32[]{:S(2)}) collective-permute-start(f32[96,1024]{1,0:T(8,128)} %bitcast.6), channel_id=1, source_target_pairs={{0,4},{1,5},{4,0},{5,1},{8,12},{9,13},{12,8},{13,9},{16,20},{17,21... | collective-permute-start | bytes 1179656 | tf_op jit(solution)/shard_map/ppermute | solution.py:33
  8.5 20.6 %collective-permute-start.5 = (f32[96,1024]{1,0:T(8,128)}, f32[96,1024]{1,0:T(8,128)S(1)}, u32[]{:S(2)}, u32[]{:S(2)}) collective-permute-start(f32[96,1024]{1,0:T(8,128)} %bitcast.7), channel_id=1, source_target_pairs={{0,2},{1,3},{4,6},{5,7},{8,10},{9,11},{12,14},{13,15},{16,18},{17,... | collective-permute-start | bytes 1179656 | tf_op jit(solution)/shard_map/ppermute | solution.py:28
  16.3 27.6 %collective-permute-start.9 = (f32[96,1024]{1,0:T(8,128)}, f32[96,1024]{1,0:T(8,128)S(1)}, u32[]{:S(2)}, u32[]{:S(2)}) collective-permute-start(f32[96,1024]{1,0:T(8,128)} %bitcast.8), channel_id=1, source_target_pairs={{124,126},{125,127},{252,254},{253,255},{380,382},{381,383},{508,5... | collective-permute-start | bytes 1179656 | tf_op jit(solution)/shard_map/ppermute | solution.py:28
  17.0 3.8 %collective-permute-start.2 = (f32[96,1024]{1,0:T(8,128)}, f32[96,1024]{1,0:T(8,128)S(1)}, u32[]{:S(2)}, u32[]{:S(2)}) collective-permute-start(f32[96,1024]{1,0:T(8,128)} %get-tuple-element.26), channel_id=1, source_target_pairs={{0,1},{1,0},{4,5},{5,4},{8,9},{9,8},{12,13},{13,12},{16,17},{17,16... | collective-permute-start | bytes 1179656 | tf_op jit(solution)/shard_map/cond/branch_1_fun/ppermute | solution.py:28
  20.9 5.9 %copy-start = (f32[32,3,1024]{2,0,1:T(8,128)S(1)}, f32[32,3,1024]{2,0,1:T(8,128)}, u32[]{:S(2)}) copy-start(f32[32,3,1024]{2,0,1:T(8,128)} %param.5) | copy-start | bytes 1179652
  20.9 4.5 %collective-permute-start.1 = (f32[96,1024]{1,0:T(8,128)S(1)}, f32[96,1024]{1,0:T(8,128)S(1)}, u32[]{:S(2)}, u32[]{:S(2)}) collective-permute-start(f32[96,1024]{1,0:T(8,128)S(1)} %get-tuple-element.25), channel_id=1, source_target_pairs={{0,1},{1,0},{4,5},{5,4},{8,9},{9,8},{12,13},{13,12},{16,17},{17,16... | collective-permute-start | bytes 1179656 | tf_op jit(solution)/shard_map/cond/branch_1_fun/ppermute | solution.py:28
  23.1 3.6 %collective-permute-start = (f32[96,1024]{1,0:T(8,128)S(1)}, f32[96,1024]{1,0:T(8,128)S(1)}, u32[]{:S(2)}, u32[]{:S(2)}) collective-permute-start(f32[96,1024]{1,0:T(8,128)S(1)} %get-tuple-element.23), channel_id=1, source_target_pairs={{0,1},{1,0},{4,5},{5,4},{8,9},{9,8},{12,13},{13,12},{16,17},{17,16... | collective-permute-start | bytes 1179656 | tf_op jit(solution)/shard_map/cond/branch_1_fun/ppermute | solution.py:28
  30.6 14.1 %collective-permute-start.6 = (f32[48,128]{1,0:T(8,128)S(1)}, f32[48,128]{1,0:T(8,128)S(1)}, u32[]{:S(2)}, u32[]{:S(2)}) collective-permute-start(f32[48,128]{1,0:T(8,128)S(1)} %rows_of_partner.2.partner_ref), channel_id=1, source_target_pairs={{0,2},{1,3},{4,6},{5,7},{8,10},{9,11},{12,14},{13,15},{16,18},{17,... | collective-permute-start | bytes 73736 | tf_op jit(solution)/shard_map/ppermute | solution.py:28
  42.6 2.0 %collective-permute-start.7 = (f32[32,128]{1,0:T(8,128)S(1)}, f32[32,128]{1,0:T(8,128)S(1)}, u32[]{:S(2)}, u32[]{:S(2)}) collective-permute-start(f32[32,128]{1,0:T(8,128)S(1)} %get-tuple-element.41.refs_0_), channel_id=1, source_target_pairs={{0,510},{1,511},{128,124},{129,125},{256,252},{257,253},{384,380},... | collective-permute-start | bytes 49160 | tf_op jit(solution)/shard_map/ppermute | solution.py:28
  43.2 1.4 %collective-permute-start.8 = (f32[32,128]{1,0:T(8,128)S(1)}, f32[32,128]{1,0:T(8,128)S(1)}, u32[]{:S(2)}, u32[]{:S(2)}) collective-permute-start(f32[32,128]{1,0:T(8,128)S(1)} %get-tuple-element.41.refs_0_), channel_id=1, source_target_pairs={{0,511},{1,510},{128,125},{129,124},{256,253},{257,252},{384,381},... | collective-permute-start | bytes 49160 | tf_op jit(solution)/shard_map/ppermute | solution.py:28
  43.9 0.8 %collective-permute-start.10 = (f32[32,128]{1,0:T(8,128)S(1)}, f32[32,128]{1,0:T(8,128)S(1)}, u32[]{:S(2)}, u32[]{:S(2)}) collective-permute-start(f32[32,128]{1,0:T(8,128)S(1)} %rows_of_partner.3), channel_id=1, source_target_pairs={{124,126},{125,127},{252,254},{253,255},{380,382},{381,383},{508,5... | collective-permute-start | bytes 49160 | tf_op jit(solution)/shard_map/ppermute | solution.py:28

commit v8 on v7

--- a/solution.py
+++ b/solution.py
@@ -59,7 +59,9 @@
             high_ref[b, pl.ds(start, 32), :] = high
             low_ref[b, pl.ds(start, 32), :] = low
         column_ref[pl.ds(start, 32), :] = jnp.broadcast_to(norm, (32, 128))
-    norm_ref[...] = jnp.transpose(column_ref[...])[0:8, :]
+    norms = jnp.transpose(column_ref[...])[0:8, :]
+    row = lax.broadcasted_iota(jnp.int32, norms.shape, 0)
+    norm_ref[...] = jnp.where(row < 4, norms, 1.0 / jnp.sqrt(norms + 1e-6))
 
 
 ROOT_HALF = 0.5**0.5
@@ -102,20 +104,21 @@
         two = lax.dot_general(left_ref[...], low_ref[b, :used], dims, preferred_element_type=jnp.float32)
         cov_ref[b, :, :used] = one[:96] + (one[96:] + two[:96] + two[96:])
 
-    def tile(lanes, norm, columns, shaped=lambda value: value):
-        scale = (1.0 / jnp.sqrt(norm + 1e-6)) * (1.0 / jnp.sqrt(columns + 1e-6))
+    def tile(lanes, norm, columns, roots, shaped=lambda value: value):
+        scale = (1.0 / jnp.sqrt(norm + 1e-6)) * roots
         cov = [[shaped(cov_ref[b, 32 * a : 32 * a + 32, lanes]) for b in range(3)] for a in range(3)]
         return (norm + columns - 2.0 * polar_trace(cov, scale)) * (1.0 / ATOMS)
 
-    first = tile(slice(0, 128), norm, norm_ref[0:1, :128])
+    first = tile(slice(0, 128), norm, norm_ref[0:1, :128], norm_ref[4:5, :128])
     if used == 128:
         out_ref[...] = first
         return
-    columns = norm_ref[0:1, 128:192]
+    columns, roots = norm_ref[0:1, 128:192], norm_ref[4:5, 128:192]
     second = tile(
         slice(128, 192),
         folded(jnp.broadcast_to(norm, (32, 64))),
         jnp.concatenate([columns, columns], axis=1),
+        jnp.concatenate([roots, roots], axis=1),
         folded,
     )
     if out_ref.shape[1] == 128:

time: 45.7 us -> 45.7 us (level)
  no operation moved by 1% of the time
where the time goes in v8:
time: 45.7 us; the launch traced here: 45.4 us
  starting transfers between devices  37.2 us (81%)
  Pallas kernels  4.68 us (10%)
  waiting for transfers between devices  3.2 us (7%)
    ppermute x9, starting transfers between devices, moved(): return lax.ppermute(value, AXES, pairs)  28.7 us
    ppermute x2, starting transfers between devices, stepped(): return lax.ppermute(value, AXES, pairs)  8.5 us
    ppermute x9, waiting for transfers between devices, moved(): return lax.ppermute(value, AXES, pairs)  3.2 us
    pallas_call x2, Pallas kernels, own_rows(): pl.pallas_call(own_kernel if more else early_kernel, out_shape=(TILES, ME...  1.63 us
    pallas_call x2, Pallas kernels, partner_rows(): pl.pallas_call(functools.partial(partner_kernel, before=before), out_shap...  1.43 us
  transfers between devices with their start and end apart: 11, of which 2 were waited for; matrix products, arithmetic and copies ran while one was open for 0% of the time, Pallas kernels for 9%

profile of v8, /device:TPU:196, one launch (start us, length us, event | category | flops | bytes accessed | tf_op | source)
XLA Modules:
  0.0 45.4 jit_solution(7959559776537048976)
XLA Ops:
  0.0 2.4 %collective-permute-start.3 = (f32[96,1024]{1,0:T(8,128)}, f32[96,1024]{1,0:T(8,128)S(1)}, u32[]{:S(2)}, u32[]{:S(2)}) collective-permute-start(f32[96,1024]{1,0:T(8,128)} %bitcast.5), channel_id=1, source_target_pairs={{4,8},{5,9},{8,4},{9,5},{12,16},{13,17},{16,12},{17,13},{20,24},{2... | collective-permute-start | bytes 1179656 | tf_op jit(solution)/shard_map/ppermute | solution.py:33
  2.4 6.1 %collective-permute-start.4 = (f32[96,1024]{1,0:T(8,128)}, f32[96,1024]{1,0:T(8,128)S(1)}, u32[]{:S(2)}, u32[]{:S(2)}) collective-permute-start(f32[96,1024]{1,0:T(8,128)} %bitcast.6), channel_id=1, source_target_pairs={{0,4},{1,5},{4,0},{5,1},{8,12},{9,13},{12,8},{13,9},{16,20},{17,21... | collective-permute-start | bytes 1179656 | tf_op jit(solution)/shard_map/ppermute | solution.py:33
  8.5 7.7 %collective-permute-start.5 = (f32[96,1024]{1,0:T(8,128)}, f32[96,1024]{1,0:T(8,128)S(1)}, u32[]{:S(2)}, u32[]{:S(2)}) collective-permute-start(f32[96,1024]{1,0:T(8,128)} %bitcast.7), channel_id=1, source_target_pairs={{0,2},{1,3},{4,6},{5,7},{8,10},{9,11},{12,14},{13,15},{16,18},{17,... | collective-permute-start | bytes 1179656 | tf_op jit(solution)/shard_map/ppermute | solution.py:28
  16.3 0.7 %collective-permute-start.9 = (f32[96,1024]{1,0:T(8,128)}, f32[96,1024]{1,0:T(8,128)S(1)}, u32[]{:S(2)}, u32[]{:S(2)}) collective-permute-start(f32[96,1024]{1,0:T(8,128)} %bitcast.8), channel_id=1, source_target_pairs={{124,126},{125,127},{252,254},{253,255},{380,382},{381,383},{508,5... | collective-permute-start | bytes 1179656 | tf_op jit(solution)/shard_map/ppermute | solution.py:28
  17.0 3.9 %conditional.3 = (f32[96,1024]{1,0:T(8,128)S(1)}) conditional(s32[]{:T(128)} %convert_element_type.7, f32[96,1024]{1,0:T(8,128)} %bitcast.9, (f32[96,1024]{1,0:T(8,128)}, f32[]{:T(128)}) %tuple.25), branch_computations={%region_2.3_spmd, %region_3.4_spmd} | conditional | flops 98304 | bytes 2359348 | solution.py:299
  17.0 1.9 %collective-permute-start.2 = (f32[96,1024]{1,0:T(8,128)}, f32[96,1024]{1,0:T(8,128)S(1)}, u32[]{:S(2)}, u32[]{:S(2)}) collective-permute-start(f32[96,1024]{1,0:T(8,128)} %get-tuple-element.26), channel_id=1, source_target_pairs={{0,1},{1,0},{4,5},{5,4},{8,9},{9,8},{12,13},{13,12},{16,17},{17,16... | collective-permute-start | bytes 1179656 | tf_op jit(solution)/shard_map/cond/branch_1_fun/ppermute | solution.py:28
  18.9 1.9 %collective-permute-done.2 = f32[96,1024]{1,0:T(8,128)S(1)} collective-permute-done((f32[96,1024]{1,0:T(8,128)}, f32[96,1024]{1,0:T(8,128)S(1)}, u32[]{:S(2)}, u32[]{:S(2)}) %collective-permute-start.2) | collective-permute-done | bytes 393248 | tf_op jit(solution)/shard_map/cond/branch_1_fun/ppermute | solution.py:28
  20.9 0.0 collective-permute-done.3.refs_0_
  20.9 0.0 collective-permute-done.4.refs_4_
  20.9 0.0 copy-start
  20.9 5.9 %conditional.2 = (f32[96,1024]{1,0:T(8,128)S(1)}, f32[96,1024]{1,0:T(8,128)S(1)}) conditional(s32[]{:T(128)} %convert_element_type.7, (f32[96,1024]{1,0:T(8,128)S(1)}, f32[96,1024]{1,0:T(8,128)S(1)}) %tuple.18, (f32[96,1024]{1,0:T(8,128)S(1)}, f32[]{:T(128)}, f32[96,1024]{1,0:T(8,128)S(1)}) %tuple.19), branch_computations={%region_0.1_spmd, %region_1.2_spmd} | conditional | flops 196608 | bytes 4718696 | solution.py:302
  20.9 2.2 %collective-permute-start.1 = (f32[96,1024]{1,0:T(8,128)S(1)}, f32[96,1024]{1,0:T(8,128)S(1)}, u32[]{:S(2)}, u32[]{:S(2)}) collective-permute-start(f32[96,1024]{1,0:T(8,128)S(1)} %get-tuple-element.25), channel_id=1, source_target_pairs={{0,1},{1,0},{4,5},{5,4},{8,9},{9,8},{12,13},{13,12},{16,17},{17,16... | collective-permute-start | bytes 1179656 | tf_op jit(solution)/shard_map/cond/branch_1_fun/ppermute | solution.py:28
  23.1 2.3 %collective-permute-start = (f32[96,1024]{1,0:T(8,128)S(1)}, f32[96,1024]{1,0:T(8,128)S(1)}, u32[]{:S(2)}, u32[]{:S(2)}) collective-permute-start(f32[96,1024]{1,0:T(8,128)S(1)} %get-tuple-element.23), channel_id=1, source_target_pairs={{0,1},{1,0},{4,5},{5,4},{8,9},{9,8},{12,13},{13,12},{16,17},{17,16... | collective-permute-start | bytes 1179656 | tf_op jit(solution)/shard_map/cond/branch_1_fun/ppermute | solution.py:28
  25.4 0.0 collective-permute-done.1
  25.4 1.3 %collective-permute-done = f32[96,1024]{1,0:T(8,128)S(1)} collective-permute-done((f32[96,1024]{1,0:T(8,128)S(1)}, f32[96,1024]{1,0:T(8,128)S(1)}, u32[]{:S(2)}, u32[]{:S(2)}) %collective-permute-start) | collective-permute-done | bytes 393248 | tf_op jit(solution)/shard_map/cond/branch_1_fun/ppermute | solution.py:28
  26.8 0.0 copy-done
  26.8 0.9 %prepare.1 = (bf16[3,192,1024]{2,1,0:T(8,128)(2,1)S(1)}, bf16[3,192,1024]{2,1,0:T(8,128)(2,1)S(1)}, f32[8,256]{1,0:T(8,128)S(1)}) custom-call(s32[1]{0:T(128)} %bitcast.chip_ref, s32[1]{0:T(128)} %bitcast.1.core_ref, f32[96,1024]{1,0:T(8,128)S(1)} %collective-permute-done.3.refs_0_, f32[96,1024]{1,0:T(8,128)S(1)} %get-tuple-element.35.refs_1_, ...), custom_call_target="tpu_custom_call" | custom-call | tf_op jit(solution)/shard_map/prepare/pallas_call | solution.py:233
  27.6 1.5 %early_rows_of_own.1.refs_0_.early_ref = f32[32,384]{1,0:T(8,128)S(1)} custom-call(s32[1]{0:T(128)} %bitcast.chip_ref, f32[96,1024]{1,0:T(8,128)S(1)} %bitcast.12, bf16[3,192,1024]{2,1,0:T(8,128)(2,1)S(1)} %get-tuple-element.37.high_ref, bf16[3,192,1024]{2,1,0:T(8,128)(2,1)S(1)} %get-tuple-element.38.low_ref, f32[8,256]{1,0:T(8,128)S(1)} %get-tuple-element.39.norm_ref), custom_call_target="tpu_custom_call" | custom-call | tf_op jit(solution)/shard_map/early_rows_of_own/pallas_call | solution.py:252
  29.2 0.0 collective-permute-done.5.rows_ref
  29.2 1.4 %rows_of_partner.2.partner_ref = f32[48,128]{1,0:T(8,128)S(1)} custom-call(s32[1]{0:T(128)} %bitcast.chip_ref, f32[96,1024]{1,0:T(8,128)S(1)} %collective-permute-done.5.rows_ref, bf16[3,192,1024]{2,1,0:T(8,128)(2,1)S(1)} %get-tuple-element.37.high_ref, bf16[3,192,1024]{2,1,0:T(8,128)(2,1)S(1)} %get-tuple-element.38.low_ref, ...), custom_call_target="tpu_custom_call" | custom-call | tf_op jit(solution)/shard_map/rows_of_partner/pallas_call | solution.py:264
  30.6 11.9 %collective-permute-start.6 = (f32[48,128]{1,0:T(8,128)S(1)}, f32[48,128]{1,0:T(8,128)S(1)}, u32[]{:S(2)}, u32[]{:S(2)}) collective-permute-start(f32[48,128]{1,0:T(8,128)S(1)} %rows_of_partner.2.partner_ref), channel_id=1, source_target_pairs={{0,2},{1,3},{4,6},{5,7},{8,10},{9,11},{12,14},{13,15},{16,18},{17,... | collective-permute-start | bytes 73736 | tf_op jit(solution)/shard_map/ppermute | solution.py:28
  42.5 0.1 rows_of_own.1
  42.6 0.7 %collective-permute-start.7 = (f32[32,128]{1,0:T(8,128)S(1)}, f32[32,128]{1,0:T(8,128)S(1)}, u32[]{:S(2)}, u32[]{:S(2)}) collective-permute-start(f32[32,128]{1,0:T(8,128)S(1)} %get-tuple-element.41.refs_0_), channel_id=1, source_target_pairs={{0,510},{1,511},{128,124},{129,125},{256,252},{257,253},{384,380},... | collective-permute-start | bytes 49160 | tf_op jit(solution)/shard_map/ppermute | solution.py:28
  43.2 0.7 %collective-permute-start.8 = (f32[32,128]{1,0:T(8,128)S(1)}, f32[32,128]{1,0:T(8,128)S(1)}, u32[]{:S(2)}, u32[]{:S(2)}) collective-permute-start(f32[32,128]{1,0:T(8,128)S(1)} %get-tuple-element.41.refs_0_), channel_id=1, source_target_pairs={{0,511},{1,510},{128,125},{129,124},{256,253},{257,252},{384,381},... | collective-permute-start | bytes 49160 | tf_op jit(solution)/shard_map/ppermute | solution.py:28
  43.9 0.0 collective-permute-done.9.rows_ref
  43.9 0.7 %collective-permute-start.10 = (f32[32,128]{1,0:T(8,128)S(1)}, f32[32,128]{1,0:T(8,128)S(1)}, u32[]{:S(2)}, u32[]{:S(2)}) collective-permute-start(f32[32,128]{1,0:T(8,128)S(1)} %rows_of_partner.3), channel_id=1, source_target_pairs={{124,126},{125,127},{252,254},{253,255},{380,382},{381,383},{508,5... | collective-permute-start | bytes 49160 | tf_op jit(solution)/shard_map/ppermute | solution.py:28
  44.6 0.0 collective-permute-done.7.mine_ref
  44.6 0.0 collective-permute-done.8.other_ref
  44.6 0.0 collective-permute-done.6.far_ref
  44.6 0.1 next_columns.1.tiles_ref
  44.8 0.0 collective-permute-done.10.far_ref
  44.8 0.6 %final.1 = f32[32,384]{1,0:T(8,128)} custom-call(s32[1]{0:T(128)} %bitcast.chip_ref, f32[32,384]{1,0:T(8,128)S(1)} %next_columns.1.tiles_ref, f32[32,128]{1,0:T(8,128)S(1)} %collective-permute-done.10.far_ref), custom_call_target="tpu_custom_call" | custom-call | tf_op jit(solution)/shard_map/final/pallas_call | solution.py:220
  (4 shorter events, 0.1 us)
Async XLA Ops:
  0.0 20.9 %collective-permute-start.3 = (f32[96,1024]{1,0:T(8,128)}, f32[96,1024]{1,0:T(8,128)S(1)}, u32[]{:S(2)}, u32[]{:S(2)}) collective-permute-start(f32[96,1024]{1,0:T(8,128)} %bitcast.5), channel_id=1, source_target_pairs={{4,8},{5,9},{8,4},{9,5},{12,16},{13,17},{16,12},{17,13},{20,24},{2... | collective-permute-start | bytes 1179656 | tf_op jit(solution)/shard_map/ppermute | solution.py:33
  2.4 18.4 %collective-permute-start.4 = (f32[96,1024]{1,0:T(8,128)}, f32[96,1024]{1,0:T(8,128)S(1)}, u32[]{:S(2)}, u32[]{:S(2)}) collective-permute-start(f32[96,1024]{1,0:T(8,128)} %bitcast.6), channel_id=1, source_target_pairs={{0,4},{1,5},{4,0},{5,1},{8,12},{9,13},{12,8},{13,9},{16,20},{17,21... | collective-permute-start | bytes 1179656 | tf_op jit(solution)/shard_map/ppermute | solution.py:33
  8.5 20.6 %collective-permute-start.5 = (f32[96,1024]{1,0:T(8,128)}, f32[96,1024]{1,0:T(8,128)S(1)}, u32[]{:S(2)}, u32[]{:S(2)}) collective-permute-start(f32[96,1024]{1,0:T(8,128)} %bitcast.7), channel_id=1, source_target_pairs={{0,2},{1,3},{4,6},{5,7},{8,10},{9,11},{12,14},{13,15},{16,18},{17,... | collective-permute-start | bytes 1179656 | tf_op jit(solution)/shard_map/ppermute | solution.py:28
  16.3 27.6 %collective-permute-start.9 = (f32[96,1024]{1,0:T(8,128)}, f32[96,1024]{1,0:T(8,128)S(1)}, u32[]{:S(2)}, u32[]{:S(2)}) collective-permute-start(f32[96,1024]{1,0:T(8,128)} %bitcast.8), channel_id=1, source_target_pairs={{124,126},{125,127},{252,254},{253,255},{380,382},{381,383},{508,5... | collective-permute-start | bytes 1179656 | tf_op jit(solution)/shard_map/ppermute | solution.py:28
  17.0 3.8 %collective-permute-start.2 = (f32[96,1024]{1,0:T(8,128)}, f32[96,1024]{1,0:T(8,128)S(1)}, u32[]{:S(2)}, u32[]{:S(2)}) collective-permute-start(f32[96,1024]{1,0:T(8,128)} %get-tuple-element.26), channel_id=1, source_target_pairs={{0,1},{1,0},{4,5},{5,4},{8,9},{9,8},{12,13},{13,12},{16,17},{17,16... | collective-permute-start | bytes 1179656 | tf_op jit(solution)/shard_map/cond/branch_1_fun/ppermute | solution.py:28
  20.9 5.9 %copy-start = (f32[32,3,1024]{2,0,1:T(8,128)S(1)}, f32[32,3,1024]{2,0,1:T(8,128)}, u32[]{:S(2)}) copy-start(f32[32,3,1024]{2,0,1:T(8,128)} %param.5) | copy-start | bytes 1179652
  20.9 4.5 %collective-permute-start.1 = (f32[96,1024]{1,0:T(8,128)S(1)}, f32[96,1024]{1,0:T(8,128)S(1)}, u32[]{:S(2)}, u32[]{:S(2)}) collective-permute-start(f32[96,1024]{1,0:T(8,128)S(1)} %get-tuple-element.25), channel_id=1, source_target_pairs={{0,1},{1,0},{4,5},{5,4},{8,9},{9,8},{12,13},{13,12},{16,17},{17,16... | collective-permute-start | bytes 1179656 | tf_op jit(solution)/shard_map/cond/branch_1_fun/ppermute | solution.py:28
  23.1 3.6 %collective-permute-start = (f32[96,1024]{1,0:T(8,128)S(1)}, f32[96,1024]{1,0:T(8,128)S(1)}, u32[]{:S(2)}, u32[]{:S(2)}) collective-permute-start(f32[96,1024]{1,0:T(8,128)S(1)} %get-tuple-element.23), channel_id=1, source_target_pairs={{0,1},{1,0},{4,5},{5,4},{8,9},{9,8},{12,13},{13,12},{16,17},{17,16... | collective-permute-start | bytes 1179656 | tf_op jit(solution)/shard_map/cond/branch_1_fun/ppermute | solution.py:28
  30.6 14.1 %collective-permute-start.6 = (f32[48,128]{1,0:T(8,128)S(1)}, f32[48,128]{1,0:T(8,128)S(1)}, u32[]{:S(2)}, u32[]{:S(2)}) collective-permute-start(f32[48,128]{1,0:T(8,128)S(1)} %rows_of_partner.2.partner_ref), channel_id=1, source_target_pairs={{0,2},{1,3},{4,6},{5,7},{8,10},{9,11},{12,14},{13,15},{16,18},{17,... | collective-permute-start | bytes 73736 | tf_op jit(solution)/shard_map/ppermute | solution.py:28
  42.6 2.0 %collective-permute-start.7 = (f32[32,128]{1,0:T(8,128)S(1)}, f32[32,128]{1,0:T(8,128)S(1)}, u32[]{:S(2)}, u32[]{:S(2)}) collective-permute-start(f32[32,128]{1,0:T(8,128)S(1)} %get-tuple-element.41.refs_0_), channel_id=1, source_target_pairs={{0,510},{1,511},{128,124},{129,125},{256,252},{257,253},{384,380},... | collective-permute-start | bytes 49160 | tf_op jit(solution)/shard_map/ppermute | solution.py:28
  43.2 1.4 %collective-permute-start.8 = (f32[32,128]{1,0:T(8,128)S(1)}, f32[32,128]{1,0:T(8,128)S(1)}, u32[]{:S(2)}, u32[]{:S(2)}) collective-permute-start(f32[32,128]{1,0:T(8,128)S(1)} %get-tuple-element.41.refs_0_), channel_id=1, source_target_pairs={{0,511},{1,510},{128,125},{129,124},{256,253},{257,252},{384,381},... | collective-permute-start | bytes 49160 | tf_op jit(solution)/shard_map/ppermute | solution.py:28
  43.9 0.8 %collective-permute-start.10 = (f32[32,128]{1,0:T(8,128)S(1)}, f32[32,128]{1,0:T(8,128)S(1)}, u32[]{:S(2)}, u32[]{:S(2)}) collective-permute-start(f32[32,128]{1,0:T(8,128)S(1)} %rows_of_partner.3), channel_id=1, source_target_pairs={{124,126},{125,127},{252,254},{253,255},{380,382},{381,383},{508,5... | collective-permute-start | bytes 49160 | tf_op jit(solution)/shard_map/ppermute | solution.py:28
